TPU v7x, 32 devices: a whole 2x2x4 slice. The times are simulated.
32 devices in a mesh: pipe: 2 (over x), dp: 4 (over z), seq: 4 (over y, core).
Axes of the slice: x: 2, y: 2, z: 4, core: 2. Of those that a mesh axis runs over, the one named last changes fastest.
Arguments:
- token_ids: int32 [8, 1024], P('dp'), may hold values from 0 to 50303
- segments: int32 [8, 1024], P('dp'), may hold values from 0 to 2, as said below
- valid: int32 [8, 1024], P('dp'), may hold values from 0 to 1
- attn_qkv: float32 [2, 1024, 3, 1024], P('pipe', 'dp', None, 'seq'), may hold values from -0.1875 to 0.1875
- attn_qkv_first: float32 [2, 1024, 3, 1024], P('pipe', 'dp', None, 'seq'), may hold values from -7.1525574e-07 to 7.1525574e-07
- attn_qkv_second: float32 [2, 1024, 3, 1024], P('pipe', 'dp', None, 'seq'), may hold values from 6.766497e-14 to 2.7014532e-13
- attn_out: float32 [2, 1024, 1024], P('pipe', 'seq', 'dp'), may hold values from -0.75 to 0.75
- attn_out_first: float32 [2, 1024, 1024], P('pipe', 'seq', 'dp'), may hold values from -7.1525574e-07 to 7.1525574e-07
- attn_out_second: float32 [2, 1024, 1024], P('pipe', 'seq', 'dp'), may hold values from 6.766497e-14 to 2.7014532e-13
- mlp_in: float32 [2, 1024, 4096], P('pipe', 'dp', 'seq'), may hold values from -0.1875 to 0.1875
- mlp_in_first: float32 [2, 1024, 4096], P('pipe', 'dp', 'seq'), may hold values from -7.1525574e-07 to 7.1525574e-07
- mlp_in_second: float32 [2, 1024, 4096], P('pipe', 'dp', 'seq'), may hold values from 6.766497e-14 to 2.7014532e-13
- mlp_out: float32 [2, 4096, 1024], P('pipe', 'seq', 'dp'), may hold values from -0.09375 to 0.09375
- mlp_out_first: float32 [2, 4096, 1024], P('pipe', 'seq', 'dp'), may hold values from -7.1525574e-07 to 7.1525574e-07
- mlp_out_second: float32 [2, 4096, 1024], P('pipe', 'seq', 'dp'), may hold values from 6.766497e-14 to 2.7014532e-13
- embed_table: float32 [50304, 1024], P('seq', 'dp')
- embed_table_first: float32 [50304, 1024], P('seq', 'dp'), may hold values from -7.1525574e-07 to 7.1525574e-07
- embed_table_second: float32 [50304, 1024], P('seq', 'dp'), may hold values from 6.766497e-14 to 2.7014532e-13
- position_table: float32 [1024, 1024], P('seq', 'dp'), may hold values from -1.25 to 1.25
- position_table_first: float32 [1024, 1024], P('seq', 'dp'), may hold values from -7.1525574e-07 to 7.1525574e-07
- position_table_second: float32 [1024, 1024], P('seq', 'dp'), may hold values from 6.766497e-14 to 2.7014532e-13
- norm_params: float32 [2, 4, 1024], P(None, None, ('pipe', 'dp', 'seq'))
- norm_params_first: float32 [2, 4, 1024], P(None, None, ('pipe', 'dp', 'seq')), may hold values from -2.3841858e-06 to 2.3841858e-06
- norm_params_second: float32 [2, 4, 1024], P(None, None, ('pipe', 'dp', 'seq')), may hold values from 6.04611e-13 to 2.444172e-12
- final_norm: float32 [2, 1024], P(None, ('pipe', 'dp', 'seq'))
- final_norm_first: float32 [2, 1024], P(None, ('pipe', 'dp', 'seq')), may hold values from -2.3841858e-06 to 2.3841858e-06
- final_norm_second: float32 [2, 1024], P(None, ('pipe', 'dp', 'seq')), may hold values from 6.04611e-13 to 2.444172e-12
Outputs:
- loss_parts: float32 [2], replicated
- penalty_sum: float32 [], replicated
- grad_norm: float32 [], replicated
- attn_qkv_new: float32 [2, 1024, 3, 1024], P('pipe', 'dp', None, 'seq')
- attn_qkv_first_new: float32 [2, 1024, 3, 1024], P('pipe', 'dp', None, 'seq')
- attn_qkv_second_new: float32 [2, 1024, 3, 1024], P('pipe', 'dp', None, 'seq')
- attn_out_new: float32 [2, 1024, 1024], P('pipe', 'seq', 'dp')
- attn_out_first_new: float32 [2, 1024, 1024], P('pipe', 'seq', 'dp')
- attn_out_second_new: float32 [2, 1024, 1024], P('pipe', 'seq', 'dp')
- mlp_in_new: float32 [2, 1024, 4096], P('pipe', 'dp', 'seq')
- mlp_in_first_new: float32 [2, 1024, 4096], P('pipe', 'dp', 'seq')
- mlp_in_second_new: float32 [2, 1024, 4096], P('pipe', 'dp', 'seq')
- mlp_out_new: float32 [2, 4096, 1024], P('pipe', 'seq', 'dp')
- mlp_out_first_new: float32 [2, 4096, 1024], P('pipe', 'seq', 'dp')
- mlp_out_second_new: float32 [2, 4096, 1024], P('pipe', 'seq', 'dp')
- embed_table_new: float32 [50304, 1024], P('seq', 'dp')
- embed_table_first_new: float32 [50304, 1024], P('seq', 'dp')
- embed_table_second_new: float32 [50304, 1024], P('seq', 'dp')
- position_table_new: float32 [1024, 1024], P('seq', 'dp')
- position_table_first_new: float32 [1024, 1024], P('seq', 'dp')
- position_table_second_new: float32 [1024, 1024], P('seq', 'dp')
- norm_params_new: float32 [2, 4, 1024], P(None, None, ('pipe', 'dp', 'seq'))
- norm_params_first_new: float32 [2, 4, 1024], P(None, None, ('pipe', 'dp', 'seq'))
- norm_params_second_new: float32 [2, 4, 1024], P(None, None, ('pipe', 'dp', 'seq'))
- final_norm_new: float32 [2, 1024], P(None, ('pipe', 'dp', 'seq'))
- final_norm_first_new: float32 [2, 1024], P(None, ('pipe', 'dp', 'seq'))
- final_norm_second_new: float32 [2, 1024], P(None, ('pipe', 'dp', 'seq'))
Inputs may be any that keep to these rules, and one draw needn't show every extreme that they name: `segments`: within a row document numbers never fall; every row holds documents 0, 1 and 2; document 1 begins at a position from 1 to 64 and document 2 at a position from 960 to 1023.
All inputs are finite; a program needn't handle non-finite values.
Results may differ from a plain program's by a relative error of at most 0.019.
Values may be sent and summed in bfloat16 or wider, within the bound.
No kernel may reach another device: no remote copies, remote signals or barrier semaphores. Data moves between devices by JAX's collectives and lax.ppermute only.
A program may use at most 1.25 GiB of HBM per device.

v0:
```python
import jax
import jax.numpy as jnp
from jax import lax
from jax.sharding import PartitionSpec as P

HEAD = 64
STEP = 10


EPS_NORM = 1e-05
ZLOSS = 0.001
CLIP = 0.01
BETA_ONE = 0.9
BETA_TWO = 0.95
EPS_ADAM = 1e-08
RATES = (0.03, 0.1, 0.03, 0.015, 0.05, 0.15, 0.7, 0.7)
DECAYS = (0.1, 0.1, 0.1, 0.1, 0.1, 0.0, 0.0, 0.0)


def joined(value, axis, join):
    pieces = jax.tree.map(lambda part: lax.all_gather(part, axis), value)
    head = jax.tree.map(lambda part: part[0], pieces)
    tail = jax.tree.map(lambda part: part[1:], pieces)
    subtotal, _ = lax.scan(lambda subtotal, share: (join(subtotal, share), None), head, tail)
    return subtotal


def from_behind(block, axis, distance):
    devices = range(lax.axis_size(axis))
    route = [(i - distance, i) for i in devices if i - distance in devices]
    return lax.ppermute(block, axis, route)


def norm_rows(values, gain, bias):
    center = values - jnp.mean(values, -1, keepdims=True)
    spread_sq = jnp.mean(center * center, -1, keepdims=True)
    return center * lax.rsqrt(spread_sq + EPS_NORM) * gain + bias


def gelu_tanh(values):
    return jax.nn.gelu(values, approximate=True)


def spread(values):
    return lax.all_gather(values, "seq", axis=0, tiled=True)


def collect(values):
    return lax.psum_scatter(
        values.astype(jnp.bfloat16), "seq", scatter_dimension=0, tiled=True
    ).astype(jnp.float32)


def branch_output(inner, w_local):
    return collect(jnp.dot(inner, w_local, preferred_element_type=jnp.float32))


def attend_forward(packed, allowed):
    length = packed.shape[0]
    column_count = packed.shape[2]
    head_count = column_count // HEAD
    queries = packed[:, 0].reshape(length, head_count, HEAD)
    key_rows = packed[:, 1].reshape(length, head_count, HEAD)
    value_rows = packed[:, 2].reshape(length, head_count, HEAD)
    scores = jnp.einsum(
        "qhe,khe->hqk", queries, key_rows, preferred_element_type=jnp.float32
    ) * HEAD ** (-0.5)
    scores = jnp.where(allowed[None], scores, -1e30)
    row_top = jnp.max(scores, -1, keepdims=True)
    exponent = jnp.exp(scores - row_top)
    probabilities = exponent / jnp.sum(exponent, -1, keepdims=True)
    mixed_rows = jnp.einsum(
        "hqk,khe->qhe",
        probabilities.astype(jnp.bfloat16),
        value_rows,
        preferred_element_type=jnp.float32,
    )
    return (probabilities, mixed_rows.reshape(length, column_count).astype(jnp.bfloat16))


def attend_backward(packed, probabilities, grad_mixed):
    length = packed.shape[0]
    column_count = packed.shape[2]
    head_count = column_count // HEAD
    queries = packed[:, 0].reshape(length, head_count, HEAD)
    key_rows = packed[:, 1].reshape(length, head_count, HEAD)
    value_rows = packed[:, 2].reshape(length, head_count, HEAD)
    grad_rows = grad_mixed.reshape(length, head_count, HEAD)
    grad_values = jnp.einsum(
        "hqk,qhe->khe",
        probabilities.astype(jnp.bfloat16),
        grad_rows,
        preferred_element_type=jnp.float32,
    )
    grad_soft = jnp.einsum(
        "qhe,khe->hqk", grad_rows, value_rows, preferred_element_type=jnp.float32
    )
    grad_scores = probabilities * (
        grad_soft - jnp.sum(probabilities * grad_soft, -1, keepdims=True)
    )
    grad_scores = grad_scores.astype(jnp.bfloat16)
    factor = HEAD ** (-0.5)
    grad_queries = (
        jnp.einsum("hqk,khe->qhe", grad_scores, key_rows, preferred_element_type=jnp.float32)
        * factor
    )
    grad_keys = (
        jnp.einsum("hqk,qhe->khe", grad_scores, queries, preferred_element_type=jnp.float32)
        * factor
    )
    stacked = jnp.stack(
        [
            grad_queries.reshape(length, column_count),
            grad_keys.reshape(length, column_count),
            grad_values.reshape(length, column_count),
        ],
        1,
    )
    return stacked.astype(jnp.bfloat16)


def forward_layer(residual, matrices, gain_rows, allowed):
    w_qkv, w_out, w_fc, w_proj = matrices
    normed = norm_rows(residual, gain_rows[0], gain_rows[1])
    first_full = spread(normed.astype(jnp.bfloat16))
    packed = jnp.einsum(
        "td,dcf->tcf", first_full, w_qkv, preferred_element_type=jnp.float32
    ).astype(jnp.bfloat16)
    probabilities, mixed_rows = attend_forward(packed, allowed)
    middle = residual + branch_output(mixed_rows, w_out)
    second = norm_rows(middle, gain_rows[2], gain_rows[3])
    second_full = spread(second.astype(jnp.bfloat16))
    hidden = jnp.dot(second_full, w_fc, preferred_element_type=jnp.float32)
    active = gelu_tanh(hidden).astype(jnp.bfloat16)
    output = middle + branch_output(active, w_proj)
    return (
        output,
        (
            residual,
            first_full,
            packed,
            probabilities,
            mixed_rows,
            middle,
            second_full,
            hidden,
            active,
        ),
    )


def backward_layer(saved, grad_out, matrices, gain_rows):
    w_qkv, w_out, w_fc, w_proj = matrices
    residual, first_full, packed, probabilities, mixed_rows, middle, second_full, hidden, active = (
        saved
    )
    grad_z = spread(grad_out.astype(jnp.bfloat16))
    grad_proj = jnp.einsum("tf,td->fd", active, grad_z, preferred_element_type=jnp.float32)
    grad_active = jnp.einsum("td,fd->tf", grad_z, w_proj, preferred_element_type=jnp.float32)
    gelu_value, gelu_pull = jax.vjp(gelu_tanh, hidden)
    grad_hidden = gelu_pull(grad_active)[0].astype(jnp.bfloat16)
    grad_fc = jnp.einsum("td,tf->df", second_full, grad_hidden, preferred_element_type=jnp.float32)
    grad_second = collect(
        jnp.einsum("tf,df->td", grad_hidden, w_fc, preferred_element_type=jnp.float32)
    )
    norm_value, norm_pull = jax.vjp(norm_rows, middle, gain_rows[2], gain_rows[3])
    grad_middle, grad_gain_two, grad_bias_two = norm_pull(grad_second)
    grad_middle = grad_middle + grad_out
    grad_y = spread(grad_middle.astype(jnp.bfloat16))
    grad_out_w = jnp.einsum("tc,td->cd", mixed_rows, grad_y, preferred_element_type=jnp.float32)
    grad_mixed = jnp.einsum("td,cd->tc", grad_y, w_out, preferred_element_type=jnp.float32).astype(
        jnp.bfloat16
    )
    grad_packed = attend_backward(packed, probabilities, grad_mixed)
    grad_qkv = jnp.einsum(
        "td,tcf->dcf", first_full, grad_packed, preferred_element_type=jnp.float32
    )
    grad_first = collect(
        jnp.einsum("tcf,dcf->td", grad_packed, w_qkv, preferred_element_type=jnp.float32)
    )
    norm_value, norm_pull = jax.vjp(norm_rows, residual, gain_rows[0], gain_rows[1])
    grad_residual, grad_gain_one, grad_bias_one = norm_pull(grad_first)
    grad_gain_rows = jnp.stack([grad_gain_one, grad_bias_one, grad_gain_two, grad_bias_two])
    return (grad_residual + grad_middle, (grad_qkv, grad_out_w, grad_fc, grad_proj), grad_gain_rows)


def section_forward(start_rows, matrices, gain_stack, wide_stack, allowed):

    def layer_step(residual, layer_items):
        return forward_layer(residual, layer_items[0], layer_items[1], allowed)

    return lax.scan(layer_step, start_rows, (matrices, gain_stack, wide_stack))


def section_backward(saved, gradient, matrices, gain_stack):

    def layer_step(carried, layer_items):
        grad_rows, grad_mats, grad_gain_rows = backward_layer(
            layer_items[0], carried, layer_items[1], layer_items[2]
        )
        return (grad_rows, (grad_mats, grad_gain_rows))

    return lax.scan(layer_step, gradient, (saved, matrices, gain_stack), reverse=True)


def embed_rows(row_ids, vocab_table, position_rows, vocab_start):
    vocab_rows = vocab_table.shape[0]
    local_ids = row_ids - vocab_start
    inside = (local_ids >= 0) & (local_ids < vocab_rows)
    picked_rows = jnp.take(vocab_table, jnp.clip(local_ids, 0, vocab_rows - 1), axis=0)
    picked_rows = jnp.where(inside[:, None], picked_rows.astype(jnp.float32), 0.0)
    return collect(picked_rows) + position_rows.astype(jnp.float32)


def embed_backward(grad_rows, row_ids, vocab_start, vocab_rows):
    full_grad = spread(grad_rows.astype(jnp.bfloat16))
    local_ids = row_ids - vocab_start
    inside = (local_ids >= 0) & (local_ids < vocab_rows)
    picked_rows = jnp.where(inside[:, None], full_grad.astype(jnp.float32), 0.0)
    target_rows = jnp.clip(local_ids, 0, vocab_rows - 1)
    return jnp.zeros((vocab_rows, full_grad.shape[1]), jnp.float32).at[target_rows].add(picked_rows)


def head_local(full_rows, vocab_table, target_local):
    logits = jnp.einsum("td,vd->tv", full_rows, vocab_table, preferred_element_type=jnp.float32)
    row_top = jnp.max(logits, 1)
    row_sums = jnp.sum(jnp.exp(logits - row_top[:, None]), 1)
    columns = jnp.arange(vocab_table.shape[0])
    target_hits = jnp.sum(jnp.where(columns[None, :] == target_local[:, None], logits, 0.0), 1)
    return (logits, row_top, row_sums, target_hits)


def head_skip(full_rows, vocab_table, target_local):
    length = full_rows.shape[0]
    zero_rows = jnp.zeros((length,), jnp.float32)
    return (
        jnp.zeros((length, vocab_table.shape[0]), jnp.float32),
        zero_rows,
        jnp.ones((length,), jnp.float32),
        zero_rows,
    )


def join_parts(first_part, second_part):
    row_top = jnp.maximum(first_part[0], second_part[0])
    row_sums = first_part[1] * jnp.exp(first_part[0] - row_top) + second_part[1] * jnp.exp(
        second_part[0] - row_top
    )
    return (row_top, row_sums, first_part[2] + second_part[2])


def head_backward(logits, log_total, full_rows, vocab_table, target_local, row_weight):
    columns = jnp.arange(vocab_table.shape[0])
    soft = jnp.exp(logits - log_total[:, None])
    gradient = (row_weight * (1.0 + 2.0 * ZLOSS * log_total))[:, None] * soft
    gradient = gradient - jnp.where(
        columns[None, :] == target_local[:, None], row_weight[:, None], 0.0
    )
    gradient = gradient.astype(jnp.bfloat16)
    table_part = jnp.einsum("tv,td->vd", gradient, full_rows, preferred_element_type=jnp.float32)
    normed_part = jnp.einsum("tv,vd->td", gradient, vocab_table, preferred_element_type=jnp.float32)
    return (table_part, normed_part)


def head_quiet(logits, log_total, full_rows, vocab_table, target_local, row_weight):
    return (jnp.zeros(vocab_table.shape, jnp.float32), jnp.zeros(full_rows.shape, jnp.float32))


def adamw_update(master, first, second, gradient, rate, decay):
    first_new = BETA_ONE * first + (1.0 - BETA_ONE) * gradient
    second_new = BETA_TWO * second + (1.0 - BETA_TWO) * gradient * gradient
    ratio = (
        first_new
        / (1.0 - BETA_ONE**STEP)
        / (jnp.sqrt(second_new / (1.0 - BETA_TWO**STEP)) + EPS_ADAM)
    )
    return (master - rate * (ratio + decay * master), first_new, second_new)


def per_device(
    token_ids,
    segments,
    valid,
    attn_qkv,
    attn_qkv_first,
    attn_qkv_second,
    attn_out,
    attn_out_first,
    attn_out_second,
    mlp_in,
    mlp_in_first,
    mlp_in_second,
    mlp_out,
    mlp_out_first,
    mlp_out_second,
    embed_table,
    embed_table_first,
    embed_table_second,
    position_table,
    position_table_first,
    position_table_second,
    norm_params,
    norm_params_first,
    norm_params_second,
    final_norm,
    final_norm_first,
    final_norm_second,
):
    section_index = lax.axis_index("pipe")
    section_count = lax.axis_size("pipe")
    seq_index = lax.axis_index("seq")
    micro_count = token_ids.shape[0]
    length = token_ids.shape[1]
    shard_rows = length // lax.axis_size("seq")
    layers_here = attn_qkv.shape[0]
    matrices = (
        lax.all_gather(attn_qkv.astype(jnp.bfloat16), "dp", axis=1, tiled=True),
        lax.all_gather(attn_out.astype(jnp.bfloat16), "dp", axis=2, tiled=True),
        lax.all_gather(mlp_in.astype(jnp.bfloat16), "dp", axis=1, tiled=True),
        lax.all_gather(mlp_out.astype(jnp.bfloat16), "dp", axis=2, tiled=True),
    )
    wide_stack = (matrices[1], matrices[3])
    vocab_table, position_rows = (
        lax.all_gather(embed_table.astype(jnp.bfloat16), "dp", axis=1, tiled=True),
        lax.all_gather(position_table.astype(jnp.bfloat16), "dp", axis=1, tiled=True),
    )
    norm_all, final_rows = (
        lax.all_gather(norm_params, ("pipe", "dp", "seq"), axis=2, tiled=True),
        lax.all_gather(final_norm, ("pipe", "dp", "seq"), axis=1, tiled=True),
    )
    gain_stack = lax.dynamic_slice_in_dim(norm_all, section_index * layers_here, layers_here, 0)
    vocab_rows = vocab_table.shape[0]
    vocab_start = seq_index * vocab_rows
    row_start = seq_index * shard_rows
    position = jnp.arange(length)
    token_weight = valid.astype(jnp.float32) * (position < length - 1).astype(jnp.float32)[None, :]
    targets = jnp.roll(token_ids, -1, axis=1)
    is_first = section_index == 0
    is_last = section_index == section_count - 1
    ticks = micro_count + section_count - 1
    grad_mats = tuple((jnp.zeros(matrix_item.shape, jnp.float32) for matrix_item in matrices))
    grad_gains = jnp.zeros(gain_stack.shape, jnp.float32)
    grad_table = jnp.zeros(vocab_table.shape, jnp.float32)
    grad_positions = jnp.zeros(position_rows.shape, jnp.float32)
    grad_final = jnp.zeros(final_rows.shape, jnp.float32)
    loss_total = jnp.zeros((), jnp.float32)
    penalty_total = jnp.zeros((), jnp.float32)
    saved_ticks = []
    head_ticks = []
    received = jnp.zeros((shard_rows, vocab_table.shape[1]), jnp.float32)
    for tick_index in range(ticks):
        micro = tick_index - section_index
        micro_slot = jnp.clip(micro, 0, micro_count - 1)
        live_flag = (micro >= 0) & (micro < micro_count)
        row_ids = lax.dynamic_index_in_dim(token_ids, micro_slot, 0, keepdims=False)
        row_segments = lax.dynamic_index_in_dim(segments, micro_slot, 0, keepdims=False)
        row_weight = lax.dynamic_index_in_dim(token_weight, micro_slot, 0, keepdims=False)
        target_local = (
            lax.dynamic_index_in_dim(targets, micro_slot, 0, keepdims=False) - vocab_start
        )
        allowed = (position[:, None] >= position[None, :]) & (
            row_segments[:, None] == row_segments[None, :]
        )
        start_rows = embed_rows(row_ids, vocab_table, position_rows, vocab_start)
        if tick_index > 0:
            start_rows = jnp.where(is_first, start_rows, received)
        output, saved = section_forward(start_rows, matrices, gain_stack, wide_stack, allowed)
        saved_ticks.append(saved)
        final_value, final_pull = jax.vjp(norm_rows, output, final_rows[0], final_rows[1])
        full_rows = spread(final_value.astype(jnp.bfloat16))
        head_on = is_last & live_flag
        logits, row_top, row_sums, target_hits = lax.cond(
            head_on, head_local, head_skip, full_rows, vocab_table, target_local
        )
        row_top, row_sums, target_hits = joined((row_top, row_sums, target_hits), "seq", join_parts)
        log_total = row_top + jnp.log(row_sums)
        token_penalty = row_weight * ZLOSS * log_total * log_total
        token_loss = row_weight * (log_total - target_hits) + token_penalty
        own_loss = jnp.sum(lax.dynamic_slice_in_dim(token_loss, row_start, shard_rows))
        own_penalty = jnp.sum(lax.dynamic_slice_in_dim(token_penalty, row_start, shard_rows))
        loss_total = loss_total + jnp.where(head_on, own_loss, 0.0)
        penalty_total = penalty_total + jnp.where(head_on, own_penalty, 0.0)
        table_part, normed_part = lax.cond(
            head_on,
            head_backward,
            head_quiet,
            logits,
            log_total,
            full_rows,
            vocab_table,
            target_local,
            row_weight,
        )
        grad_table = grad_table + table_part
        head_grad, gain_part, bias_part = final_pull(collect(normed_part))
        head_ticks.append(head_grad)
        grad_final = grad_final + jnp.where(head_on, jnp.stack([gain_part, bias_part]), 0.0)
        if tick_index + 1 < ticks:
            received = from_behind(output.astype(jnp.bfloat16), "pipe", 1).astype(output.dtype)
    received_back = jnp.zeros_like(received)
    for back_index in range(ticks):
        source = ticks - 1 - back_index
        micro = micro_count - 1 - back_index + (section_count - 1 - section_index)
        micro_slot = jnp.clip(micro, 0, micro_count - 1)
        live_flag = (micro >= 0) & (micro < micro_count)
        gradient = head_ticks[source]
        if back_index > 0:
            gradient = jnp.where(is_last, gradient, received_back)
        grad_rows, layer_parts = section_backward(
            saved_ticks[source], gradient, matrices, gain_stack
        )
        mat_parts, gain_parts = layer_parts
        grad_mats = tuple(
            (
                total_item + jnp.where(live_flag, part_item, 0.0)
                for total_item, part_item in zip(grad_mats, mat_parts)
            )
        )
        grad_gains = grad_gains + jnp.where(live_flag, gain_parts, 0.0)
        row_ids = lax.dynamic_index_in_dim(token_ids, micro_slot, 0, keepdims=False)
        embed_on = live_flag & is_first
        table_back = embed_backward(grad_rows, row_ids, vocab_start, vocab_rows)
        grad_table = grad_table + jnp.where(embed_on, table_back, 0.0)
        grad_positions = grad_positions + jnp.where(embed_on, grad_rows, 0.0)
        if back_index + 1 < ticks:
            received_back = from_behind(grad_rows.astype(jnp.bfloat16), "pipe", -1).astype(
                grad_rows.dtype
            )
    grad_norm_all = lax.dynamic_update_slice_in_dim(
        jnp.zeros(norm_all.shape, jnp.float32), grad_gains, section_index * layers_here, 0
    )
    norm_grad, final_grad = (
        lax.psum_scatter(grad_norm_all, ("pipe", "dp", "seq"), scatter_dimension=2, tiled=True),
        lax.psum_scatter(grad_final, ("pipe", "dp", "seq"), scatter_dimension=1, tiled=True),
    )
    grad_table, grad_positions = (
        lax.psum(grad_table.astype(jnp.bfloat16), "pipe").astype(jnp.float32),
        lax.psum(grad_positions.astype(jnp.bfloat16), "pipe").astype(jnp.float32),
    )
    qkv_grad, out_grad, fc_grad, proj_grad, table_grad, position_grad = (
        lax.psum_scatter(
            grad_mats[0].astype(jnp.bfloat16), "dp", scatter_dimension=1, tiled=True
        ).astype(jnp.float32),
        lax.psum_scatter(
            grad_mats[1].astype(jnp.bfloat16), "dp", scatter_dimension=2, tiled=True
        ).astype(jnp.float32),
        lax.psum_scatter(
            grad_mats[2].astype(jnp.bfloat16), "dp", scatter_dimension=1, tiled=True
        ).astype(jnp.float32),
        lax.psum_scatter(
            grad_mats[3].astype(jnp.bfloat16), "dp", scatter_dimension=2, tiled=True
        ).astype(jnp.float32),
        lax.psum_scatter(
            grad_table.astype(jnp.bfloat16), "dp", scatter_dimension=1, tiled=True
        ).astype(jnp.float32),
        lax.psum_scatter(
            grad_positions.astype(jnp.bfloat16), "dp", scatter_dimension=1, tiled=True
        ).astype(jnp.float32),
    )
    gradients = (
        qkv_grad,
        out_grad,
        fc_grad,
        proj_grad,
        table_grad,
        position_grad,
        norm_grad,
        final_grad,
    )
    squares = jnp.zeros((), jnp.float32)
    for index in range(8):
        part_square = jnp.sum(gradients[index] * gradients[index])
        if index == 4 or index == 5:
            part_square = part_square / section_count
        squares = squares + part_square
    own_weight = jnp.sum(lax.dynamic_slice_in_dim(token_weight, row_start, shard_rows, 1))
    count_part = jnp.where(is_first, own_weight, 0.0)
    squares_all, loss_sum, penalty_sum, token_count = lax.psum(
        (squares, loss_total, penalty_total, count_part), ("pipe", "dp", "seq")
    )
    grad_norm = jnp.sqrt(squares_all) / token_count
    clip_factor = jnp.minimum(1.0, CLIP / (grad_norm + 1e-06))
    step_scale = clip_factor / token_count
    masters = (
        attn_qkv,
        attn_out,
        mlp_in,
        mlp_out,
        embed_table,
        position_table,
        norm_params,
        final_norm,
    )
    moments = (
        (attn_qkv_first, attn_qkv_second),
        (attn_out_first, attn_out_second),
        (mlp_in_first, mlp_in_second),
        (mlp_out_first, mlp_out_second),
        (embed_table_first, embed_table_second),
        (position_table_first, position_table_second),
        (norm_params_first, norm_params_second),
        (final_norm_first, final_norm_second),
    )
    results = []
    for index in range(8):
        results.append(
            adamw_update(
                masters[index],
                moments[index][0],
                moments[index][1],
                gradients[index] * step_scale,
                RATES[index],
                DECAYS[index],
            )
        )
    loss_parts = jnp.stack([loss_sum, token_count])
    return (
        loss_parts,
        penalty_sum,
        grad_norm,
        results[0][0],
        results[0][1],
        results[0][2],
        results[1][0],
        results[1][1],
        results[1][2],
        results[2][0],
        results[2][1],
        results[2][2],
        results[3][0],
        results[3][1],
        results[3][2],
        results[4][0],
        results[4][1],
        results[4][2],
        results[5][0],
        results[5][1],
        results[5][2],
        results[6][0],
        results[6][1],
        results[6][2],
        results[7][0],
        results[7][1],
        results[7][2],
    )


def solution(mesh):
    in_specs = (
        P("dp", None),
        P("dp", None),
        P("dp", None),
        P("pipe", "dp", None, "seq"),
        P("pipe", "dp", None, "seq"),
        P("pipe", "dp", None, "seq"),
        P("pipe", "seq", "dp"),
        P("pipe", "seq", "dp"),
        P("pipe", "seq", "dp"),
        P("pipe", "dp", "seq"),
        P("pipe", "dp", "seq"),
        P("pipe", "dp", "seq"),
        P("pipe", "seq", "dp"),
        P("pipe", "seq", "dp"),
        P("pipe", "seq", "dp"),
        P("seq", "dp"),
        P("seq", "dp"),
        P("seq", "dp"),
        P("seq", "dp"),
        P("seq", "dp"),
        P("seq", "dp"),
        P(None, None, ("pipe", "dp", "seq")),
        P(None, None, ("pipe", "dp", "seq")),
        P(None, None, ("pipe", "dp", "seq")),
        P(None, ("pipe", "dp", "seq")),
        P(None, ("pipe", "dp", "seq")),
        P(None, ("pipe", "dp", "seq")),
    )
    out_specs = (
        P(),
        P(),
        P(),
        P("pipe", "dp", None, "seq"),
        P("pipe", "dp", None, "seq"),
        P("pipe", "dp", None, "seq"),
        P("pipe", "seq", "dp"),
        P("pipe", "seq", "dp"),
        P("pipe", "seq", "dp"),
        P("pipe", "dp", "seq"),
        P("pipe", "dp", "seq"),
        P("pipe", "dp", "seq"),
        P("pipe", "seq", "dp"),
        P("pipe", "seq", "dp"),
        P("pipe", "seq", "dp"),
        P("seq", "dp"),
        P("seq", "dp"),
        P("seq", "dp"),
        P("seq", "dp"),
        P("seq", "dp"),
        P("seq", "dp"),
        P(None, None, ("pipe", "dp", "seq")),
        P(None, None, ("pipe", "dp", "seq")),
        P(None, None, ("pipe", "dp", "seq")),
        P(None, ("pipe", "dp", "seq")),
        P(None, ("pipe", "dp", "seq")),
        P(None, ("pipe", "dp", "seq")),
    )
    return jax.shard_map(
        per_device, mesh=mesh, in_specs=in_specs, out_specs=out_specs, check_vma=False
    )
```

profile of v0, /device:TPU:0, one launch (start us, length us, event | category | flops | bytes accessed | tf_op | source)
XLA Modules:
  0.0 3622.3 jit_solution(10084489695169015034)
XLA Ops:
  16.8 435.7 %all-gather.33.cloned.1.call-done = bf16[12576,1024]{1,0:T(8,128)(2,1)} async-done(((bf16[12576,256]{1,0:T(8,128)(2,1)}), bf16[12576,1024]{1,0:T(8,128)(2,1)}) %all-gather.33.cloned.1.call-update) | async-done | bytes 25755664 | tf_op jit(solution)/shard_map/all_gather | solution.py:324
  472.3 42.0 %all_gather.146 = f32[2,4,1024]{1,0,2:T(2,128)S(1)} all-gather(f32[2,4,32]{1,0,2:T(2,128)S(1)} %copy.150), channel_id=1, replica_groups=mesh['pipe'=2,'dp'=4,'seq'=4] {'pipe','dp','seq'}, dimensions={2}, use_global_device_ids=true | all-gather | bytes 33792 | tf_op jit(solution)/shard_map/all_gather | solution.py:328
  603.3 30.6 reduce-scatter.33.cloned.1.call-done
  639.2 42.6 %all-gather.41.cloned.1.call-done = bf16[1,1024,1024]{2,1,0:T(8,128)(2,1)} async-done(((bf16[1,256,1024]{2,1,0:T(8,128)(2,1)}), bf16[1,1024,1024]{2,1,0:T(8,128)(2,1)}) %all-gather.41.cloned.1.call-update) | async-done | bytes 2097168 | tf_op jit(solution)/shard_map/all_gather | solution.py:319
  711.9 41.8 %all-gather.43.cloned.1.call-done = bf16[1,1024,1024]{2,1,0:T(8,128)(2,1)} async-done(((bf16[1,1024,256]{2,1,0:T(8,128)(2,1)}), bf16[1,1024,1024]{2,1,0:T(8,128)(2,1)}) %all-gather.43.cloned.1.call-update) | async-done | bytes 2097168 | tf_op jit(solution)/shard_map/all_gather | solution.py:320
  796.0 29.0 reduce-scatter.37.cloned.1.call-done
  878.2 31.5 reduce-scatter.39.cloned.1.call-done
  983.0 28.2 reduce-scatter.43.cloned.1.call-done
  1063.0 31.5 reduce-scatter.45.cloned.1.call-done
  1132.2 40.7 %all-gather.9 = f32[32,32,2]{1,2,0:T(2,128)S(1)} all-gather(f32[1,32,2]{1,2,0:T(2,128)S(1)} %bitcast.424), channel_id=1, replica_groups=mesh['pipe'=2,'dp'=4,'seq'=4] {'pipe','dp','seq'}, dimensions={0}, use_global_device_ids=true | all-gather | bytes 8448 | tf_op jit(solution)/shard_map/all_gather | solution.py:329
  1232.4 26.8 conditional.11
  1367.2 150.9 %reduce-scatter.53.cloned.1.call-done = bf16[256,1024]{1,0:T(8,128)(2,1)} async-done(((bf16[1024,1024]{1,0:T(8,128)(2,1)}), bf16[256,1024]{1,0:T(8,128)(2,1)}) %reduce-scatter.53.cloned.1.call-update) | async-done | bytes 524304 | tf_op jit(solution)/shard_map/reduce_scatter | solution.py:49
  1518.0 228.1 %reduce-scatter.49.cloned.1.call-done = bf16[256,1024]{1,0:T(8,128)(2,1)} async-done(((bf16[1024,1024]{1,0:T(8,128)(2,1)}), bf16[256,1024]{1,0:T(8,128)(2,1)}) %reduce-scatter.49.cloned.1.call-update) | async-done | bytes 524304 | tf_op jit(solution)/shard_map/reduce_scatter | solution.py:49
  1791.7 31.6 reduce-scatter.51.cloned.1.call-done
  1891.3 31.5 reduce-scatter.55.cloned.1.call-done
  1979.2 31.5 reduce-scatter.57.cloned.1.call-done
  2079.1 31.5 reduce-scatter.61.cloned.1.call-done
  2167.1 31.5 reduce-scatter.63.cloned.1.call-done
  2267.0 30.2 reduce-scatter.73.cloned.1.call-done
  2325.3 31.6 scatter_custom_fusion
  2361.0 30.5 scatter_custom_fusion.1
  2395.8 31.0 scatter_custom_fusion.2
  2426.8 87.5 %add_convert_fusion = bf16[12576,1024]{1,0:T(8,128)(2,1)} fusion(f32[12576,1024]{1,0:T(8,128)} %scatter_custom_fusion.2, f32[12576,1024]{1,0:T(8,128)} %scatter_custom_fusion.1, f32[12576,1024]{1,0:T(8,128)} %scatter_custom_fusion, f32[12576,1024]{1,0:T(8,128)} %get-tuple-element.612, f32[12576,1024]{1,0:T(8,128)} %get-tuple-element.610, ...), kind=kLoop, calls=%fused_computation.39 | loop fusion | flops 115900416 | bytes 334823424 | tf_op jit(solution)/shard_map/convert_element_type | solution.py:437
  2559.9 378.2 %reduce-scatter.75.cloned.1.call-done = bf16[12576,256]{1,0:T(8,128)(2,1)} async-done(((bf16[12576,1024]{1,0:T(8,128)(2,1)}), bf16[12576,256]{1,0:T(8,128)(2,1)}) %reduce-scatter.75.cloned.1.call-update) | async-done | bytes 6438928 | tf_op jit(solution)/shard_map/reduce_scatter | solution.py:453
  2950.4 126.3 %reduce-scatter.81.cloned.1.call-done = f32[32,2]{1,0:T(8,128)} async-done(((f32[1024,2]{1,0:T(8,128)}), f32[32,2]{1,0:T(8,128)}) %reduce-scatter.81.cloned.1.call-update) | async-done | bytes 272
  3078.1 40.8 %reduce-scatter.69.cloned.1.call-done = bf16[1,256,1024]{2,1,0:T(8,128)(2,1)} async-done(((bf16[1,1024,1024]{2,1,0:T(8,128)(2,1)}), bf16[1,256,1024]{2,1,0:T(8,128)(2,1)}) %reduce-scatter.69.cloned.1.call-update) | async-done | bytes 524304 | tf_op jit(solution)/shard_map/reduce_scatter | solution.py:447
  3120.9 44.1 %reduce-scatter.71.cloned.1.call-done = bf16[1,1024,256]{2,1,0:T(8,128)(2,1)} async-done(((bf16[1,1024,1024]{2,1,0:T(8,128)(2,1)}), bf16[1,1024,256]{2,1,0:T(8,128)(2,1)}) %reduce-scatter.71.cloned.1.call-update) | async-done | bytes 524304 | tf_op jit(solution)/shard_map/reduce_scatter | solution.py:450
  3190.3 34.8 reduce-scatter.65.cloned.1.call-done
  3229.4 131.0 %reduce-scatter.79.cloned.1.call-done = f32[32,8]{1,0:T(8,128)} async-done(((f32[1024,8]{1,0:T(8,128)}), f32[32,8]{1,0:T(8,128)}) %reduce-scatter.79.cloned.1.call-update) | async-done | bytes 1040
  3361.9 157.2 %all-reduce.4.cloned.1.call-done = (bf16[12576,256]{1,0:T(8,128)(2,1)}, bf16[256,256]{1,0:T(8,128)(2,1)}) async-done(((bf16[12576,256]{1,0:T(8,128)(2,1)}, bf16[256,256]{1,0:T(8,128)(2,1)}), (bf16[12576,256]{1,0:T(8,128)(2,1)}, bf16[256,256]{1,0:T(8,128)(2,1)})) %all-reduce.4.cloned.1.call-update) | async-done | bytes 6570000 | tf_op jit(solution)/shard_map/psum | solution.py:437
  3529.4 40.7 %all-reduce = (f32[]{:T(128)}, f32[1]{0:T(128)}, f32[]{:T(128)}, f32[]{:T(128)}) all-reduce(f32[]{:T(128)S(6)} %select_n.365, f32[1]{0:T(128)} %bitcast.48, f32[]{:T(128)S(6)} %add.798, f32[]{:T(128)S(6)} %add.833), channel_id=1, replica_groups=mesh['pipe'=2,'dp'=4,'seq'=4] {'pipe','dp','seq'}, use_global_device_ids=true, to_apply=%region_59.61 | all-reduce | flops 4 | bytes 32 | tf_op jit(solution)/shard_map/psum | solution.py:478
  3576.5 29.2 multiply_subtract_fusion
  (992 shorter events, 1188.5 us)
Async XLA Ops:
  7.2 445.2 %all-gather.33.cloned.1.call-start = ((), (), s32[]{:S(2)}) async-start(), calls=%async_computation.26 | async-start | bytes 32194560 | tf_op jit(solution)/shard_map/all_gather | solution.py:324
  15.3 536.7 %reduce-scatter.31.cloned.1.call-start = ((), (), s32[]{:S(2)}) async-start(), calls=%async_computation.27 | async-start | bytes 2621440 | tf_op jit(solution)/shard_map/reduce_scatter | solution.py:49
  471.1 102.1 %all-gather.37.cloned.1.call-start = ((), (), s32[]{:S(2)}) async-start(), calls=%async_computation.29 | async-start | bytes 1966080 | tf_op jit(solution)/shard_map/all_gather | solution.py:317
  472.1 105.7 %all-gather.35.cloned.1.call-start = ((), (), s32[]{:S(2)}) async-start(), calls=%async_computation.28 | async-start | bytes 2621440 | tf_op jit(solution)/shard_map/while/body/eval_jaxpr/all_gather | solution.py:45
  556.8 77.0 %reduce-scatter.33.cloned.1.call-start = ((), (), s32[]{:S(2)}) async-start(), calls=%async_computation.30 | async-start | bytes 2621440 | tf_op jit(solution)/shard_map/while/body/eval_jaxpr/reduce_scatter | solution.py:49
  602.3 79.6 %all-gather.41.cloned.1.call-start = ((), (), s32[]{:S(2)}) async-start(), calls=%async_computation.32 | async-start | bytes 2621440 | tf_op jit(solution)/shard_map/all_gather | solution.py:319
  603.2 102.1 %all-gather.39.cloned.1.call-start = ((), (), s32[]{:S(2)}) async-start(), calls=%async_computation.31 | async-start | bytes 2621440 | tf_op jit(solution)/shard_map/while/body/eval_jaxpr/all_gather | solution.py:45
  636.6 117.1 %all-gather.43.cloned.1.call-start = ((), (), s32[]{:S(2)}) async-start(), calls=%async_computation.33 | async-start | bytes 2621440 | tf_op jit(solution)/shard_map/all_gather | solution.py:320
  638.7 151.7 %reduce-scatter.35.cloned.1.call-start = ((), (), s32[]{:S(2)}) async-start(), calls=%async_computation.34 | async-start | bytes 2621440 | tf_op jit(solution)/shard_map/while/body/eval_jaxpr/reduce_scatter | solution.py:49
  828.9 80.8 %reduce-scatter.39.cloned.1.call-start = ((), (), s32[]{:S(2)}) async-start(), calls=%async_computation.38 | async-start | bytes 2621440 | tf_op jit(solution)/shard_map/while/body/eval_jaxpr/reduce_scatter | solution.py:49
  1015.1 79.5 %reduce-scatter.45.cloned.1.call-start = ((), (), s32[]{:S(2)}) async-start(), calls=%async_computation.44 | async-start | bytes 2621440 | tf_op jit(solution)/shard_map/while/body/eval_jaxpr/reduce_scatter | solution.py:49
  1097.1 77.8 %reduce-scatter.47.cloned.1.call-start = ((), (), s32[]{:S(2)}) async-start(), calls=%async_computation.46 | async-start | bytes 2621440 | tf_op jit(solution)/shard_map/while/body/eval_jaxpr/reduce_scatter | solution.py:49
  1178.2 81.0 %all-gather.51.cloned.1.call-start = ((), (), s32[]{:S(2)}) async-start(), calls=%async_computation.41 | async-start | bytes 2621440 | tf_op jit(solution)/shard_map/all_gather | solution.py:45
  1179.0 134.7 %all-gather.57.cloned.1.call-start = ((), (), s32[]{:S(2)}) async-start(), calls=%async_computation.47 | async-start | bytes 2621440 | tf_op jit(solution)/shard_map/all_gather | solution.py:45
  1179.7 187.4 %reduce-scatter.59.cloned.1.call-start = ((), (), s32[]{:S(2)}) async-start(), calls=%async_computation.57 | async-start | bytes 2621440 | tf_op jit(solution)/shard_map/reduce_scatter | solution.py:49
  1259.1 258.9 %reduce-scatter.53.cloned.1.call-start = ((), (), s32[]{:S(2)}) async-start(), calls=%async_computation.52 | async-start | bytes 2621440 | tf_op jit(solution)/shard_map/reduce_scatter | solution.py:49
  1313.6 432.6 %reduce-scatter.49.cloned.1.call-start = ((), (), s32[]{:S(2)}) async-start(), calls=%async_computation.48 | async-start | bytes 2621440 | tf_op jit(solution)/shard_map/reduce_scatter | solution.py:49
  1367.1 410.0 %all-gather.59.cloned.1.call-start = ((), (), s32[]{:S(2)}) async-start(), calls=%async_computation.49 | async-start | bytes 2621440 | tf_op jit(solution)/shard_map/while/body/eval_jaxpr/all_gather | solution.py:45
  1829.1 93.7 %reduce-scatter.55.cloned.1.call-start = ((), (), s32[]{:S(2)}) async-start(), calls=%async_computation.53 | async-start | bytes 2621440 | tf_op jit(solution)/shard_map/while/body/eval_jaxpr/reduce_scatter | solution.py:49
  2016.8 93.8 %reduce-scatter.61.cloned.1.call-start = ((), (), s32[]{:S(2)}) async-start(), calls=%async_computation.58 | async-start | bytes 2621440 | tf_op jit(solution)/shard_map/while/body/eval_jaxpr/reduce_scatter | solution.py:49
  2204.9 92.3 %reduce-scatter.73.cloned.1.call-start = ((), (), s32[]{:S(2)}) async-start(), calls=%async_computation.68 | async-start | bytes 2621440 | tf_op jit(solution)/shard_map/while/body/eval_jaxpr/reduce_scatter | solution.py:49
  2266.4 90.6 %all-gather.73.cloned.1.call-start = ((), (), s32[]{:S(2)}) async-start(), calls=%async_computation.67 | async-start | bytes 2621440 | tf_op jit(solution)/shard_map/all_gather | solution.py:45
  2266.9 124.9 %all-gather.75.cloned.1.call-start = ((), (), s32[]{:S(2)}) async-start(), calls=%async_computation.69 | async-start | bytes 2621440 | tf_op jit(solution)/shard_map/all_gather | solution.py:45
  2302.6 257.2 %reduce-scatter.77.cloned.1.call-start = ((), (), s32[]{:S(2)}) async-start(), calls=%async_computation.71 | async-start | bytes 655360 | tf_op jit(solution)/shard_map/reduce_scatter | solution.py:456
  2391.5 546.5 %reduce-scatter.75.cloned.1.call-start = ((), (), s32[]{:S(2)}) async-start(), calls=%async_computation.70 | async-start | bytes 32194560 | tf_op jit(solution)/shard_map/reduce_scatter | solution.py:453
  2514.4 562.3 %reduce-scatter.81.cloned.1.call-start = ((), (), s32[]{:S(2)}) async-start(), calls=%async_computation.73 | async-start | bytes 540672
  2516.2 602.8 %reduce-scatter.69.cloned.1.call-start = ((), (), s32[]{:S(2)}) async-start(), calls=%async_computation.64 | async-start | bytes 2621440 | tf_op jit(solution)/shard_map/reduce_scatter | solution.py:447
  2528.0 637.0 %reduce-scatter.71.cloned.1.call-start = ((), (), s32[]{:S(2)}) async-start(), calls=%async_computation.65 | async-start | bytes 2621440 | tf_op jit(solution)/shard_map/reduce_scatter | solution.py:450
  2540.3 648.4 %reduce-scatter.67.cloned.1.call-start = ((), (), s32[]{:S(2)}) async-start(), calls=%async_computation.63 | async-start | bytes 655360 | tf_op jit(solution)/shard_map/reduce_scatter | solution.py:444
  2550.1 674.9 %reduce-scatter.65.cloned.1.call-start = ((), (), s32[]{:S(2)}) async-start(), calls=%async_computation.62 | async-start | bytes 1966080 | tf_op jit(solution)/shard_map/reduce_scatter | solution.py:441
  2557.4 803.0 %reduce-scatter.79.cloned.1.call-start = ((), (), s32[]{:S(2)}) async-start(), calls=%async_computation.72 | async-start | bytes 540672
  2559.8 959.4 %all-reduce.4.cloned.1.call-start = ((), (), s32[]{:S(2)}) async-start(), calls=%async_computation.74 | async-start | bytes 13139968 | tf_op jit(solution)/shard_map/psum | solution.py:437
  (286 other events, 23888.7 us)
Sparse Core Ops, SparseCore 0:
  15.5 436.9 all-gather.32
  471.2 34.5 reduce-scatter.30
  508.0 45.7 all-gather.36
  602.4 31.4 reduce-scatter.32
  635.8 45.9 all-gather.40
  707.4 46.2 all-gather.42
  760.7 29.6 reduce-scatter.34
  793.5 31.4 reduce-scatter.36
  878.2 31.4 reduce-scatter.38
  945.9 31.4 reduce-scatter.40
  979.8 31.3 reduce-scatter.42
  1063.0 31.4 reduce-scatter.44
  1132.3 31.5 reduce-scatter.46
  1199.0 22.6 all-gather.50
  1259.3 31.6 reduce-scatter.58
  1313.7 204.3 reduce-scatter.52
  1520.7 225.4 reduce-scatter.48
  1791.8 31.4 reduce-scatter.50
  1891.4 31.4 reduce-scatter.54
  1979.3 31.4 reduce-scatter.56
  2016.9 22.5 all-gather.64
  2079.1 31.4 reduce-scatter.60
  2167.2 31.4 reduce-scatter.62
  2205.0 22.5 all-gather.68
  2265.7 31.4 reduce-scatter.72
  2514.5 423.4 reduce-scatter.74
  2940.8 135.8 reduce-scatter.80
  3079.0 39.8 reduce-scatter.68
  3121.8 43.1 reduce-scatter.70
  3191.4 33.5 reduce-scatter.64
  3227.7 132.6 reduce-scatter.78
  3363.0 156.1 all-reduce.3
  (17 shorter events, 371.8 us)
where the time goes:
time: 3630 us; the launch traced here: 3620 us
  waiting for transfers between devices  2500 us (69%)
  other arithmetic  373 us (10%)
  matrix products  264 us (7%)
  local copies, waits for them, and re-layouts  217 us (6%)
  blocking collectives  207 us (6%)
    reduce_scatter x18, waiting for transfers between devices, collect(): lax.psum_scatter(values.astype(jnp.bfloat16), 'seq', scatter_dimension=0,...  735 us
    all_gather x1, waiting for transfers between devices, per_device(): lax.all_gather(embed_table.astype(jnp.bfloat16), 'dp', axis=1, tiled=True)  436 us
    reduce_scatter x1, waiting for transfers between devices, per_device(): lax.psum_scatter(grad_table.astype(jnp.bfloat16), 'dp', scatter_dimension...  378 us
    all_gather x18, waiting for transfers between devices, spread(): return lax.all_gather(values, 'seq', axis=0, tiled=True)  283 us
    unnamed x51, waiting for transfers between devices  261 us
    psum x1, waiting for transfers between devices, per_device(): lax.psum(grad_table.astype(jnp.bfloat16), 'pipe').astype(jnp.float32)  157 us
    another operation x18, local copies, waits for them, and re-layouts  108 us
    scatter-add x3, other arithmetic, embed_backward(): jnp.zeros((vocab_rows, full_grad.shape[1]), jnp.float32).at[target_rows]  93.1 us
  transfers between devices with their start and end apart: 53, of which 42 were waited for; matrix products, arithmetic and copies ran while one was open for 13% of the time, Pallas kernels for 0%

commit v1 on v0

v1 whole, which is shorter than its diff:
```python
import jax
import jax.numpy as jnp
from jax import lax
from jax.sharding import PartitionSpec as P

HEAD = 64
STEP = 10


EPS_NORM = 1e-05
ZLOSS = 0.001
CLIP = 0.01
BETA_ONE = 0.9
BETA_TWO = 0.95
EPS_ADAM = 1e-08
RATES = (0.03, 0.1, 0.03, 0.015, 0.05, 0.15, 0.7, 0.7)
DECAYS = (0.1, 0.1, 0.1, 0.1, 0.1, 0.0, 0.0, 0.0)
F32 = jnp.float32
BF16 = jnp.bfloat16


def swap(block, axis, mask):
    route = [(i, i ^ mask) for i in range(lax.axis_size(axis))]
    return lax.ppermute(block, axis, route)


def masks_down(size):
    found = []
    mask = size // 2
    while mask >= 1:
        found.append(mask)
        mask //= 2
    return found


def reverse_bits(value, size):
    result = 0
    mask = 1
    while mask < size:
        result = result * 2 + (value & mask) // mask
        mask *= 2
    return result


def spread(block):
    for mask in masks_down(lax.axis_size("seq")):
        block = jnp.concatenate([block, swap(block, "seq", mask)], 0)
    return block


def collect(block):
    for mask in reversed(masks_down(lax.axis_size("seq"))):
        half = block.shape[0] // 2
        sent = swap(block[half:].astype(BF16), "seq", mask)
        block = block[:half].astype(F32) + sent.astype(F32)
    return block


def sum_everywhere(block, axes=("seq", "dp", "pipe")):
    for axis in axes:
        for mask in reversed(masks_down(lax.axis_size(axis))):
            block = block + swap(block, axis, mask)
    return block


def norm_rows(values, gain, bias):
    center = values - jnp.mean(values, -1, keepdims=True)
    spread_sq = jnp.mean(center * center, -1, keepdims=True)
    return center * lax.rsqrt(spread_sq + EPS_NORM) * gain + bias


def gelu_tanh(values):
    return jax.nn.gelu(values, approximate=True)


def split_heads(packed):
    length, columns = packed.shape
    third = columns // 3
    heads = third // HEAD
    return tuple(
        packed[:, k * third : (k + 1) * third].reshape(length, heads, HEAD) for k in range(3)
    )


def attend_forward(packed, allowed):
    queries, key_rows, value_rows = split_heads(packed)
    length, heads, _ = queries.shape
    scores = jnp.einsum(
        "qhe,khe->hqk", queries, key_rows, preferred_element_type=F32
    ) * HEAD ** (-0.5)
    scores = jnp.where(allowed[None], scores, -1e30)
    row_top = jnp.max(scores, -1, keepdims=True)
    exponent = jnp.exp(scores - row_top)
    probabilities = exponent / jnp.sum(exponent, -1, keepdims=True)
    mixed_rows = jnp.einsum(
        "hqk,khe->qhe", probabilities.astype(BF16), value_rows, preferred_element_type=F32
    )
    return (probabilities, mixed_rows.reshape(length, heads * HEAD).astype(BF16))


def attend_backward(packed, probabilities, grad_mixed):
    queries, key_rows, value_rows = split_heads(packed)
    length, heads, _ = queries.shape
    columns = heads * HEAD
    grad_rows = grad_mixed.reshape(length, heads, HEAD)
    grad_values = jnp.einsum(
        "hqk,qhe->khe", probabilities.astype(BF16), grad_rows, preferred_element_type=F32
    )
    grad_soft = jnp.einsum("qhe,khe->hqk", grad_rows, value_rows, preferred_element_type=F32)
    grad_scores = probabilities * (
        grad_soft - jnp.sum(probabilities * grad_soft, -1, keepdims=True)
    )
    grad_scores = grad_scores.astype(BF16)
    factor = HEAD ** (-0.5)
    grad_queries = (
        jnp.einsum("hqk,khe->qhe", grad_scores, key_rows, preferred_element_type=F32) * factor
    )
    grad_keys = (
        jnp.einsum("hqk,qhe->khe", grad_scores, queries, preferred_element_type=F32) * factor
    )
    return jnp.concatenate(
        [
            grad_queries.reshape(length, columns),
            grad_keys.reshape(length, columns),
            grad_values.reshape(length, columns),
        ],
        1,
    ).astype(BF16)


def forward_layer(residual, matrices, gain_rows, allowed):
    w_qkv, w_out, w_fc, w_proj = matrices
    normed = norm_rows(residual, gain_rows[0], gain_rows[1])
    first_full = spread(normed.astype(BF16))
    packed = jnp.dot(first_full, w_qkv, preferred_element_type=F32).astype(BF16)
    probabilities, mixed_rows = attend_forward(packed, allowed)
    branch = jnp.einsum("tc,dc->td", mixed_rows, w_out, preferred_element_type=F32)
    middle = residual + collect(branch)
    second = norm_rows(middle, gain_rows[2], gain_rows[3])
    second_full = spread(second.astype(BF16))
    hidden = jnp.dot(second_full, w_fc, preferred_element_type=F32)
    active = gelu_tanh(hidden).astype(BF16)
    branch = jnp.einsum("tf,df->td", active, w_proj, preferred_element_type=F32)
    output = middle + collect(branch)
    saved = (
        residual,
        first_full,
        packed,
        probabilities,
        mixed_rows,
        middle,
        second_full,
        hidden,
        active,
    )
    return output, saved


def backward_layer(saved, grad_out, matrices, gain_rows):
    w_qkv, w_out, w_fc, w_proj = matrices
    residual, first_full, packed, probabilities, mixed_rows, middle, second_full, hidden, active = (
        saved
    )
    grad_z = spread(grad_out.astype(BF16))
    grad_active = jnp.dot(grad_z, w_proj, preferred_element_type=F32)
    _, gelu_pull = jax.vjp(gelu_tanh, hidden)
    grad_hidden = gelu_pull(grad_active)[0].astype(BF16)
    grad_second = collect(jnp.einsum("tf,df->td", grad_hidden, w_fc, preferred_element_type=F32))
    grad_proj = jnp.einsum("td,tf->df", grad_z, active, preferred_element_type=F32).astype(BF16)
    grad_fc = jnp.einsum(
        "td,tf->df", second_full, grad_hidden, preferred_element_type=F32
    ).astype(BF16)
    _, norm_pull = jax.vjp(norm_rows, middle, gain_rows[2], gain_rows[3])
    grad_middle, grad_gain_two, grad_bias_two = norm_pull(grad_second)
    grad_middle = grad_middle + grad_out
    grad_y = spread(grad_middle.astype(BF16))
    grad_mixed = jnp.dot(grad_y, w_out, preferred_element_type=F32).astype(BF16)
    grad_packed = attend_backward(packed, probabilities, grad_mixed)
    grad_first = collect(jnp.einsum("tc,dc->td", grad_packed, w_qkv, preferred_element_type=F32))
    grad_out_w = jnp.einsum("td,tc->dc", grad_y, mixed_rows, preferred_element_type=F32)
    grad_qkv = jnp.einsum("td,tc->dc", first_full, grad_packed, preferred_element_type=F32)
    grad_attn = jnp.concatenate([grad_qkv, grad_out_w], 1).astype(BF16)
    _, norm_pull = jax.vjp(norm_rows, residual, gain_rows[0], gain_rows[1])
    grad_residual, grad_gain_one, grad_bias_one = norm_pull(grad_first)
    grad_gain_rows = jnp.stack([grad_gain_one, grad_bias_one, grad_gain_two, grad_bias_two])
    return (grad_residual + grad_middle, (grad_attn, grad_fc, grad_proj), grad_gain_rows)


def exchange_blocks(blocks, axis):
    return [blocks[0]] + [swap(blocks[m], axis, m) for m in range(1, len(blocks))]


def place_columns(blocks, index):
    width = blocks[0].shape[1]
    whole = jnp.zeros((blocks[0].shape[0], width * len(blocks)), blocks[0].dtype)
    for m, block in enumerate(blocks):
        whole = lax.dynamic_update_slice_in_dim(whole, block, (index ^ m) * width, 1)
    return whole


def take_columns(whole, index, count):
    width = whole.shape[1] // count
    return [
        lax.dynamic_slice_in_dim(whole, (index ^ m) * width, width, 1) for m in range(count)
    ]


def head_block(rows, table, bias):
    logits = jnp.einsum("td,vd->tv", rows, table, preferred_element_type=F32) + bias[None, :]
    row_top = jnp.max(logits, 1)
    exponent = jnp.exp(logits - row_top[:, None])
    row_sum = jnp.sum(exponent, 1)
    low = exponent.astype(BF16)
    mixed = jnp.dot(low, table, preferred_element_type=F32)
    return low, mixed, row_top, row_sum


def head_table_gradient(low, scale, weight, target, rows):
    columns = jnp.arange(low.shape[1])
    gradient = scale[:, None] * low.astype(F32) - jnp.where(
        columns[None, :] == target[:, None], weight[:, None], 0.0
    )
    return jnp.einsum("tv,td->vd", gradient.astype(BF16), rows, preferred_element_type=F32)


def merge_stats(stats):
    top, total = stats
    for axis, place in (("seq", 1), ("dp", 0)):
        size = lax.axis_size(axis)
        for mask in reversed(masks_down(size)):
            shift = reverse_bits(mask, size) if axis == "seq" else mask
            order = jnp.array([k ^ shift for k in range(size)])
            pair = jnp.take(swap(jnp.stack([top, total]), axis, mask), order, axis=place + 1)
            top_new = jnp.maximum(top, pair[0])
            total = total * jnp.exp(top - top_new) + pair[1] * jnp.exp(pair[0] - top_new)
            top = top_new
    return top + jnp.log(total)


def adamw_update(master, first, second, gradient, rate, decay):
    first_new = BETA_ONE * first + (1.0 - BETA_ONE) * gradient
    second_new = BETA_TWO * second + (1.0 - BETA_TWO) * gradient * gradient
    ratio = (
        first_new
        / (1.0 - BETA_ONE**STEP)
        / (jnp.sqrt(second_new / (1.0 - BETA_TWO**STEP)) + EPS_ADAM)
    )
    return (master - rate * (ratio + decay * master), first_new, second_new)


def per_device(
    token_ids,
    segments,
    valid,
    attn_qkv,
    attn_qkv_first,
    attn_qkv_second,
    attn_out,
    attn_out_first,
    attn_out_second,
    mlp_in,
    mlp_in_first,
    mlp_in_second,
    mlp_out,
    mlp_out_first,
    mlp_out_second,
    embed_table,
    embed_table_first,
    embed_table_second,
    position_table,
    position_table_first,
    position_table_second,
    norm_params,
    norm_params_first,
    norm_params_second,
    final_norm,
    final_norm_first,
    final_norm_second,
):
    section, replica, lane = lax.axis_index("pipe"), lax.axis_index("dp"), lax.axis_index("seq")
    sections, replicas, lanes = (lax.axis_size(name) for name in ("pipe", "dp", "seq"))
    length = token_ids.shape[1]
    assert sections == 2 and token_ids.shape[0] == sections and attn_qkv.shape[0] == 1
    shard_rows = length // lanes
    slice_rows, slice_columns = embed_table.shape
    width = slice_columns * replicas
    part_rows = -(-slice_rows // (replicas * 128)) * 128
    half_rows = part_rows // 2
    assert part_rows * (replicas - 1) < slice_rows
    lane_order = [reverse_bits(k, lanes) for k in range(lanes)]
    lane_blocks = lane ^ jnp.array(lane_order)

    norm_mine = jnp.concatenate([norm_params.reshape(-1, norm_params.shape[2]), final_norm], 0)
    norm_columns = norm_mine.shape[1]
    norm_all = lax.all_gather(norm_mine, ("pipe", "dp", "seq"), axis=1, tiled=True)
    gain_stack = norm_all[:-2].reshape(norm_params.shape[0], 4, width)
    final_rows = norm_all[-2:]

    own_ids = lax.dynamic_index_in_dim(token_ids, section, 0, keepdims=False)
    own_valid = lax.dynamic_index_in_dim(valid, section, 0, keepdims=False)
    row_segments = lax.dynamic_index_in_dim(segments, section, 0, keepdims=False)
    coded = own_ids * 2 + own_valid
    coded_all = jnp.stack([coded] + [swap(coded, "dp", m) for m in range(1, replicas)])
    ids_all = coded_all // 2
    position = jnp.arange(length)
    weight_all = jnp.where(position < length - 1, coded_all % 2, 0).astype(F32)
    targets_all = jnp.roll(ids_all, -1, axis=1)

    def by_lane(values):
        return jnp.take(values.reshape(-1, lanes, shard_rows), lane_blocks, axis=1)

    ids_lane, weight_lane, targets_lane = by_lane(ids_all), by_lane(weight_all), by_lane(targets_all)

    def two_layers(matrix):
        low = matrix.astype(BF16)
        half = low.shape[0] // 2
        kept = lax.dynamic_slice_in_dim(low, section * half, half, 0)
        sent = lax.dynamic_slice_in_dim(low, (1 - section) * half, half, 0)
        other = swap(sent, "pipe", 1)
        return [jnp.where(section == layer, kept, other) for layer in range(2)]

    qkv_columns = attn_qkv.shape[2] * attn_qkv.shape[3]
    attn_shard = jnp.concatenate(
        [attn_qkv[0].reshape(-1, qkv_columns), attn_out[0].T], 1
    )
    pieces = [two_layers(attn_shard), two_layers(mlp_in[0]), two_layers(mlp_out[0].T)]

    def layer_matrices(layer):
        attn, fc, proj = (
            lax.all_gather(piece[layer], ("dp", "pipe"), axis=0, tiled=True) for piece in pieces
        )
        return attn[:, :qkv_columns], attn[:, qkv_columns:], fc, proj

    matrices = [layer_matrices(0), layer_matrices(1)]

    vocab_start = lane * slice_rows
    wanted = jnp.transpose(ids_lane, (1, 0, 2)).reshape(-1) - vocab_start
    inside = (wanted >= 0) & (wanted < slice_rows)
    picked = jnp.take(embed_table, jnp.clip(wanted, 0, slice_rows - 1), axis=0)
    picked = jnp.where(inside[:, None], picked, 0.0).astype(BF16)
    picked = collect(picked).astype(BF16).reshape(replicas, shard_rows, slice_columns)
    embed_rows = place_columns(exchange_blocks(list(picked), "dp"), replica)
    position_low = position_table.astype(BF16)
    position_rows = place_columns(
        exchange_blocks([position_low] * replicas, "dp"), replica
    )
    start_rows = embed_rows.astype(F32) + position_rows.astype(F32)
    next_first = lax.ppermute(embed_rows[:1], "seq", [(k, k - 1) for k in range(1, lanes)])
    target_rows = jnp.concatenate([embed_rows[1:], next_first], 0).astype(F32)

    table_low = jnp.pad(
        embed_table.astype(BF16), ((0, part_rows * replicas - slice_rows), (0, 0))
    )
    table_parts = [
        lax.dynamic_slice_in_dim(table_low, (replica ^ m) * part_rows, part_rows, 0)
        for m in range(replicas)
    ]
    table = place_columns(exchange_blocks(table_parts, "dp"), replica)
    part_start = vocab_start + replica * part_rows
    part_count = jnp.minimum(part_rows, slice_rows - replica * part_rows)
    table_bias = jnp.where(jnp.arange(part_rows) < part_count, 0.0, -1e30).astype(F32)

    row_place = (lane_blocks[:, None] * shard_rows + jnp.arange(shard_rows)[None, :]).reshape(-1)
    row_document = jnp.take(row_segments.reshape(lanes, shard_rows), lane_blocks, axis=0).reshape(-1)
    allowed = (row_place[:, None] >= row_place[None, :]) & (
        row_document[:, None] == row_document[None, :]
    )
    rows = start_rows
    saved = []
    for layer in range(2):
        rows, kept = forward_layer(rows, matrices[layer], gain_stack[layer], allowed)
        saved.append(kept)
    final_value, final_pull = jax.vjp(norm_rows, rows, final_rows[0], final_rows[1])
    final_low = final_value.astype(BF16)

    full = [spread(block) for block in exchange_blocks([final_low] * replicas, "dp")]
    heads = [head_block(block, table, table_bias) for block in full]
    stat_shape = (replicas, lanes, shard_rows)
    row_top = jnp.stack([head[2] for head in heads]).reshape(stat_shape)
    row_sum = jnp.stack([head[3] for head in heads]).reshape(stat_shape)
    log_total = merge_stats((row_top, row_sum))
    scale = weight_lane * (1.0 + 2.0 * ZLOSS * log_total) * jnp.exp(row_top - log_total)
    own_weight, own_log = weight_lane[0, 0], log_total[0, 0]
    target_logit = jnp.sum(final_low.astype(F32) * target_rows, 1)
    own_penalty = own_weight * ZLOSS * own_log * own_log
    own_loss = own_weight * (own_log - target_logit) + own_penalty

    scale_flat = scale.reshape(replicas, length)
    head_parts = [
        collect(scale_flat[m][:, None] * heads[m][1]).astype(BF16) for m in range(replicas)
    ]
    head_parts = exchange_blocks(head_parts, "dp")
    grad_final_rows = sum(part.astype(F32) for part in head_parts)
    grad_final_rows = grad_final_rows - own_weight[:, None] * target_rows
    gradient, final_gain_part, final_bias_part = final_pull(grad_final_rows)
    grad_final = jnp.stack([final_gain_part, final_bias_part])

    target_part = targets_lane.reshape(replicas, length) - part_start
    weight_flat = weight_lane.reshape(replicas, length)
    table_gradient = sum(
        head_table_gradient(
            heads[m][0], scale_flat[m], weight_flat[m], target_part[m], full[m]
        )
        for m in range(replicas)
    ).astype(BF16)
    half_kept = lax.dynamic_slice_in_dim(table_gradient, section * half_rows, half_rows, 0)
    half_sent = lax.dynamic_slice_in_dim(table_gradient, (1 - section) * half_rows, half_rows, 0)
    half_sum = (
        half_kept.astype(F32) + swap(half_sent, "pipe", 1).astype(F32)
    ).astype(BF16)
    half_back = jnp.stack(
        exchange_blocks(take_columns(half_sum, replica, replicas), "dp")
    )
    half_other = swap(half_back, "pipe", 1)
    grad_table = jnp.zeros((replicas, 2, half_rows, slice_columns), BF16)
    for m in range(replicas):
        for half, block in ((section, half_back[m]), (1 - section, half_other[m])):
            grad_table = lax.dynamic_update_slice(
                grad_table, block[None, None], (replica ^ m, half, 0, 0)
            )
    grad_table = grad_table.reshape(-1, slice_columns)[:slice_rows].astype(F32)

    scattered = [None, None]
    grad_gains = [None, None]
    for layer in (1, 0):
        gradient, mat_parts, grad_gains[layer] = backward_layer(
            saved[layer], gradient, matrices[layer], gain_stack[layer]
        )
        scattered[layer] = jnp.concatenate(
            [
                lax.psum_scatter(part, ("dp", "pipe"), scatter_dimension=0, tiled=True)
                for part in mat_parts
            ],
            1,
        )
    matrix_kept = jnp.where(section == 0, scattered[0], scattered[1])
    matrix_sent = jnp.where(section == 0, scattered[1], scattered[0])
    matrix_other = swap(matrix_sent, "pipe", 1)
    matrix_grad = jnp.where(
        section == 0,
        jnp.concatenate([matrix_kept, matrix_other], 0),
        jnp.concatenate([matrix_other, matrix_kept], 0),
    ).astype(F32)
    attn_columns = attn_shard.shape[1]
    fc_columns = mlp_in.shape[2]
    qkv_grad = matrix_grad[:, :qkv_columns].reshape(attn_qkv.shape)
    out_grad = matrix_grad[:, qkv_columns:attn_columns].T[None]
    fc_grad = matrix_grad[:, attn_columns : attn_columns + fc_columns][None]
    proj_grad = matrix_grad[:, attn_columns + fc_columns :].T[None]

    back = exchange_blocks(take_columns(gradient.astype(BF16), replica, replicas), "dp")
    back = jnp.concatenate(back, 0)
    back_other = swap(back, "pipe", 1)
    back_both = jnp.where(
        section == 0,
        jnp.concatenate([back, back_other], 0),
        jnp.concatenate([back_other, back], 0),
    )
    position_grad = jnp.sum(
        back_both.astype(F32).reshape(-1, shard_rows, slice_columns), 0
    )
    back_rows = spread(back_both)
    coded_other = swap(coded_all, "pipe", 1)
    ids_both = jnp.where(
        section == 0,
        jnp.concatenate([ids_all, coded_other // 2], 0),
        jnp.concatenate([coded_other // 2, ids_all], 0),
    )
    back_wanted = jnp.transpose(by_lane(ids_both), (1, 0, 2)).reshape(-1) - vocab_start
    back_inside = (back_wanted >= 0) & (back_wanted < slice_rows)
    table_grad = grad_table.at[jnp.clip(back_wanted, 0, slice_rows - 1)].add(
        jnp.where(back_inside[:, None], back_rows.astype(F32), 0.0)
    )

    norm_grad_all = jnp.concatenate([grad_gains[0], grad_gains[1], grad_final], 0)
    norm_grad_all = sum_everywhere(norm_grad_all)
    norm_place = ((section * replicas + replica) * lanes + lane) * norm_columns
    norm_grad_mine = lax.dynamic_slice_in_dim(norm_grad_all, norm_place, norm_columns, 1)
    norm_grad = norm_grad_mine[:-2].reshape(norm_params.shape)
    final_grad = norm_grad_mine[-2:]

    gradients = (
        qkv_grad,
        out_grad,
        fc_grad,
        proj_grad,
        table_grad,
        position_grad,
        norm_grad,
        final_grad,
    )
    squares = jnp.zeros((), F32)
    for index in range(8):
        part_square = jnp.sum(gradients[index] * gradients[index])
        if index == 4 or index == 5:
            part_square = part_square / sections
        squares = squares + part_square
    sums = jnp.stack([squares, jnp.sum(own_loss), jnp.sum(own_penalty), jnp.sum(own_weight)])
    sums = sum_everywhere(sums)
    loss_sum, penalty_sum, token_count = sums[1], sums[2], sums[3]
    grad_norm = jnp.sqrt(sums[0]) / token_count
    clip_factor = jnp.minimum(1.0, CLIP / (grad_norm + 1e-06))
    step_scale = clip_factor / token_count
    masters = (
        attn_qkv,
        attn_out,
        mlp_in,
        mlp_out,
        embed_table,
        position_table,
        norm_params,
        final_norm,
    )
    moments = (
        (attn_qkv_first, attn_qkv_second),
        (attn_out_first, attn_out_second),
        (mlp_in_first, mlp_in_second),
        (mlp_out_first, mlp_out_second),
        (embed_table_first, embed_table_second),
        (position_table_first, position_table_second),
        (norm_params_first, norm_params_second),
        (final_norm_first, final_norm_second),
    )
    results = []
    for index in range(8):
        results.extend(
            adamw_update(
                masters[index],
                moments[index][0],
                moments[index][1],
                gradients[index] * step_scale,
                RATES[index],
                DECAYS[index],
            )
        )
    loss_parts = jnp.stack([loss_sum, token_count])
    return (loss_parts, penalty_sum, grad_norm, *results)


def solution(mesh):
    row_spec = P("dp", None)
    qkv_spec = P("pipe", "dp", None, "seq")
    into_spec = P("pipe", "dp", "seq")
    out_spec = P("pipe", "seq", "dp")
    table_spec = P("seq", "dp")
    norm_spec = P(None, None, ("pipe", "dp", "seq"))
    final_spec = P(None, ("pipe", "dp", "seq"))
    kinds = (
        qkv_spec,
        out_spec,
        into_spec,
        out_spec,
        table_spec,
        table_spec,
        norm_spec,
        final_spec,
    )
    triples = tuple(spec for spec in kinds for _ in range(3))
    return jax.shard_map(
        per_device,
        mesh=mesh,
        in_specs=(row_spec, row_spec, row_spec) + triples,
        out_specs=(P(), P(), P()) + triples,
        check_vma=False,
    )
```

time: 3630 us -> 1660 us (0.46)
  waiting for transfers between devices: 2500 us -> 741 us
  blocking collectives: 207 us -> 39.5 us
  other arithmetic: 373 us -> 253 us
  matrix products: 264 us -> 353 us
  starting transfers between devices: 14.6 us -> 97.3 us
  local copies, waits for them, and re-layouts: 217 us -> 138 us
    reduce_scatter x24 -> x0, waiting for transfers between devices: 1250 us -> none  [the longest x18 735 us: collect(): lax.psum_scatter(values.astype(jnp.bfloat16), 'seq', scatter_dimension=0,...]
    all_gather x22 -> x6, waiting for transfers between devices: 803 us -> 97.5 us  [layer_matrices(): lax.all_gather(piece[layer], ('dp', 'pipe'), axis=0, tiled=True)]
    ppermute x4 -> x99, waiting for transfers between devices: 28.5 us -> 640 us  [the longest x98 640 us: swap(): return lax.ppermute(block, axis, route)]
    unnamed x51 -> x18, waiting for transfers between devices: 261 us -> 4.01 us
    psum x1 -> x0, waiting for transfers between devices: 157 us -> none  [per_device(): lax.psum(grad_table.astype(jnp.bfloat16), 'pipe').astype(jnp.float32)]
    all_gather x13 -> x1, blocking collectives: 167 us -> 39.5 us  [per_device(): lax.all_gather(norm_mine, ('pipe', 'dp', 'seq'), axis=1, tiled=True)]
    another operation x18 -> x4, local copies, waits for them, and re-layouts: 108 us -> 2.03 us  [the longest x1 1.88 us: per_device(): jnp.stack(exchange_blocks(take_columns(half_sum, replica, replicas), 'dp'))]
    convert_element_type x31 -> x23, other arithmetic: 156 us -> 50.5 us  [the longest x2 16.4 us: attend_backward(): grad_scores = grad_scores.astype(BF16)]
  transfers between devices with their start and end apart: 53 -> 111, of which waited for: 42 -> 62; matrix products, arithmetic and copies ran while one was open for 13% -> 28% of each run, Pallas kernels for 0% -> 0%
where the time goes in v1:
time: 1660 us; the launch traced here: 1650 us
  waiting for transfers between devices  741 us (45%)
  matrix products  353 us (21%)
  other arithmetic  253 us (15%)
  local copies, waits for them, and re-layouts  138 us (8%)
  starting transfers between devices  97.3 us (6%)
  blocking collectives  39.5 us (2%)
  between operations  27.1 us (2%)
    ppermute x98, waiting for transfers between devices, swap(): return lax.ppermute(block, axis, route)  640 us
    all_gather x6, waiting for transfers between devices, layer_matrices(): lax.all_gather(piece[layer], ('dp', 'pipe'), axis=0, tiled=True)  97.5 us
    ppermute x98, starting transfers between devices, swap(): return lax.ppermute(block, axis, route)  93.6 us
    dot_general x4, matrix products, head_table_gradient(): jnp.einsum('tv,td->vd', gradient.astype(BF16), rows, preferred_element_ty...  77 us
    scatter-add x1, other arithmetic, per_device(): grad_table.at[jnp.clip(back_wanted, 0, slice_rows - 1)]  58.9 us
    dot_general x4, matrix products, head_block(): jnp.einsum('td,vd->tv', rows, table, preferred_element_type=F32)  57.1 us
    unnamed x508, local copies, waits for them, and re-layouts  56.6 us
    sub x8, other arithmetic, adamw_update(): return (master - rate * (ratio + decay * master), first_new, second_new)  46.1 us
  transfers between devices with their start and end apart: 111, of which 62 were waited for; matrix products, arithmetic and copies ran while one was open for 28% of the time, Pallas kernels for 0%

profile of v1, /device:TPU:0, one launch (start us, length us, event | category | flops | bytes accessed | tf_op | source)
XLA Modules:
  0.0 1649.6 jit_solution(14532634108531956990)
XLA Ops:
  21.1 20.6 %gather_fusion = bf16[4096,256]{1,0:T(8,128)(2,1)} fusion(f32[12576,256]{1,0:T(8,128)} %param.53, s32[4096]{0:T(1024)S(1)} %broadcast_clamp_fusion), kind=kCustom, calls=%fused_computation.6 | custom fusion | bytes 4210688 | tf_op jit(solution)/shard_map/jit(_take)/gather | solution.py:339
  56.7 39.5 %all-gather = f32[32,32,10]{1,2,0:T(8,128)S(1)} all-gather(f32[1,32,10]{1,2,0:T(8,128)S(1)} %maximum_bitcast_fusion), channel_id=1, replica_groups=mesh['pipe'=2,'dp'=4,'seq'=4] {'pipe','dp','seq'}, dimensions={0}, use_global_device_ids=true | all-gather | bytes 42240 | tf_op jit(solution)/shard_map/all_gather | solution.py:295
  151.0 12.5 all-gather.8.cloned.1.call-done
  211.3 11.7 collective-permute-done.16
  233.5 36.0 %all-gather.12.cloned.1.call-done = bf16[1024,1024]{0,1:T(8,128)(2,1)} async-done(((bf16[128,1024]{0,1:T(8,128)(2,1)}), bf16[1024,1024]{0,1:T(8,128)(2,1)}) %all-gather.12.cloned.1.call-update) | async-done | bytes 2097168 | tf_op jit(solution)/shard_map/all_gather | solution.py:330
  284.6 12.5 collective-permute-done.21
  299.5 11.8 collective-permute-done.22
  312.6 15.0 all-gather.14.cloned.1.call-done
  358.8 12.3 collective-permute-done.25
  374.7 11.8 collective-permute-done.26
  396.9 34.1 %all-gather.18.cloned.1.call-done = bf16[1024,1024]{0,1:T(8,128)(2,1)} async-done(((bf16[128,1024]{0,1:T(8,128)(2,1)}), bf16[1024,1024]{0,1:T(8,128)(2,1)}) %all-gather.18.cloned.1.call-update) | async-done | bytes 2097168 | tf_op jit(solution)/shard_map/all_gather | solution.py:330
  470.2 61.7 %collective-permute-done.32 = bf16[3200,256]{1,0:T(8,128)(2,1)} collective-permute-done((bf16[3200,256]{1,0:T(8,128)(2,1)}, bf16[3200,256]{1,0:T(8,128)(2,1)}, u32[]{:S(2)}, u32[]{:S(2)}) %collective-permute-start.32) | collective-permute-done | bytes 1638432 | tf_op jit(solution)/shard_map/ppermute | solution.py:24
  535.3 55.7 %collective-permute-done.33 = bf16[3200,256]{1,0:T(8,128)(2,1)} collective-permute-done((bf16[3200,256]{1,0:T(8,128)(2,1)}, bf16[3200,256]{1,0:T(8,128)(2,1)}, u32[]{:S(2)}, u32[]{:S(2)}) %collective-permute-start.33) | collective-permute-done | bytes 1638432 | tf_op jit(solution)/shard_map/ppermute | solution.py:24
  593.1 44.2 %collective-permute-done.38 = bf16[256,1024]{1,0:T(8,128)(2,1)S(1)} collective-permute-done((bf16[256,1024]{1,0:T(8,128)(2,1)S(1)}, bf16[256,1024]{1,0:T(8,128)(2,1)S(1)}, u32[]{:S(2)}, u32[]{:S(2)}) %collective-permute-start.38) | collective-permute-done | bytes 524320 | tf_op jit(solution)/shard_map/ppermute | solution.py:24
  675.8 11.8 add_reduce_fusion.3
  708.4 24.8 %fusion.6 = (f32[1024]{0:T(1024)S(1)}, f32[1024]{0:T(1024)S(1)}, f32[1024]{0:T(1024)S(1)}, f32[1024]{0:T(1024)S(1)}, f32[1024,3200]{1,0:T(8,128)}) fusion(f32[1024,3200]{1,0:T(8,128)} %get-tuple-element.303, f32[1024]{0:T(1024)S(1)} %get-tuple-element.302, f32[3200]{0:T(1024)S(1)} %fusion.165, f32[1024,3200]{1,0:T(8,128)} %fusion.258, ...), kind=kOutput, calls=%fused_computation.46 | convolution fusion | flops 6740373504 | bytes 61112832 | tf_op jit(solution)/shard_map/td,vd->tv/dot_general | solution.py:209
  733.3 14.4 fusion.8
  766.3 12.6 convolution_multiply_fusion
  781.6 11.5 convolution_multiply_fusion.1
  862.8 13.1 collective-permute-done.55
  908.5 12.7 collective-permute-done.63
  927.8 19.2 %fusion.24 = f32[3200,1024]{1,0:T(8,128)} fusion(bf16[1024,1024]{1,0:T(8,128)(2,1)S(1)} %copy-done.114, f32[1024]{0:T(1024)S(1)} %bitcast.518, s32[1024]{0:T(1024)S(1)} %bitcast.525, f32[1024]{0:T(1024)S(1)} %bitcast.520, f32[1024,3200]{1,0:T(8,128)} %fusion.258, f32[1024]{0:T(1024)S(1)} %get-tuple-element.157, f32[3200]{0:T(1024)S(1)} %fusion.165), kind=kOutput, calls=%fused_computation.66 | convolution fusion | flops 6740377600 | bytes 28340736 | tf_op jit(solution)/shard_map/tv,td->vd/dot_general | solution.py:223
  947.2 15.8 fusion.23
  1006.3 19.1 %fusion.22 = f32[3200,1024]{1,0:T(8,128)} fusion(f32[1024]{0:T(1024)S(1)} %bitcast.512, s32[1024]{0:T(1024)S(1)} %bitcast.523, f32[1024]{0:T(1024)S(1)} %bitcast.514, bf16[512,1024]{1,0:T(8,128)(2,1)S(1)} %copy-done.205, bf16[256,1024]{1,0:T(8,128)(2,1)S(1)} %copy-done.101, bf16[256,1024]{1,0:T(8,128)(2,1)S(1)} %copy-done.57, ...), kind=kOutput, calls=%fused_computation.64 | convolution fusion | flops 6746669056 | bytes 28340736 | tf_op jit(solution)/shard_map/tv,td->vd/dot_general | solution.py:223
  1045.9 22.8 %add_convert_fusion = bf16[3200,1024]{1,0:T(8,128)(2,1)} fusion(f32[3200,1024]{1,0:T(8,128)} %fusion.24, f32[3200,1024]{1,0:T(8,128)} %fusion.22, f32[3200,1024]{1,0:T(8,128)} %fusion.23, bf16[1024,1024]{1,0:T(8,128)(2,1)} %copy-done.120, f32[1024]{0:T(1024)S(1)} %bitcast.509, s32[1024]{0:T(1024)S(1)} %bitcast.522, f32[1024]{0:T(1024)S(1)} %bitcast.511, ...), kind=kOutput, calls=%fused_computation.22 | convolution fusion | flops 6753484800 | bytes 61108736 | tf_op jit(solution)/shard_map/tv,td->vd/dot_general | solution.py:223
  1092.0 69.3 %collective-permute-done.80 = s32[4,1024]{1,0:T(4,128)S(1)} collective-permute-done((s32[4,1024]{1,0:T(4,128)S(1)}, s32[4,1024]{1,0:T(4,128)S(1)}, u32[]{:S(2)}, u32[]{:S(2)}) %collective-permute-start.80) | collective-permute-done | bytes 16416 | tf_op jit(solution)/shard_map/ppermute | solution.py:24
  1224.5 47.9 %collective-permute-done.77 = bf16[1600,256]{1,0:T(8,128)(2,1)} collective-permute-done((bf16[1600,256]{1,0:T(8,128)(2,1)}, bf16[1600,256]{1,0:T(8,128)(2,1)}, u32[]{:S(2)}, u32[]{:S(2)}) %collective-permute-start.77) | collective-permute-done | bytes 819232 | tf_op jit(solution)/shard_map/ppermute | solution.py:24
  1283.9 15.2 multiply_reduce_fusion
  1319.4 44.4 %collective-permute-done.79 = bf16[4,1600,256]{2,1,0:T(8,128)(2,1)} collective-permute-done((bf16[4,1600,256]{2,1,0:T(8,128)(2,1)}, bf16[4,1600,256]{2,1,0:T(8,128)(2,1)}, u32[]{:S(2)}, u32[]{:S(2)}) %collective-permute-start.79) | collective-permute-done | bytes 3276832 | tf_op jit(solution)/shard_map/ppermute | solution.py:24
  1399.8 12.6 collective-permute-done.84
  1488.9 58.9 %scatter_custom_fusion = f32[12576,256]{1,0:T(8,128)} fusion(f32[12576,256]{1,0:T(8,128)} %slice_convert_fusion, s32[8192]{0:T(1024)} %bitcast.483, bf16[4096,256]{1,0:T(8,128)(2,1)} %collective-permute-done.88, bf16[]{:T(256)} %constant.402, bf16[2048,256]{1,0:T(8,128)(2,1)} %copy-done.36, bf16[2048,256]{1,0:T(8,128)(2,1)} %copy-done.15, ...), kind=kCustom, calls=%fused_computation.53 | custom fusion | flops 16777216 | bytes 17081344 | tf_op jit(solution)/shard_map/scatter-add | solution.py:471
  1605.4 31.7 %multiply_subtract_fusion = (f32[12576,256]{1,0:T(8,128)}, f32[12576,256]{1,0:T(8,128)}, f32[12576,256]{1,0:T(8,128)}) fusion(f32[12576,256]{1,0:T(8,128)} %param.53, f32[12576,256]{1,0:T(8,128)} %scatter_custom_fusion, f32[]{:T(128)S(6)} %div.317, f32[12576,256]{1,0:T(8,128)} %param.54, f32[12576,256]{1,0:T(8,128)} %param.55), kind=kLoop, calls=%fused_computation.36 | loop fusion | flops 51511296 | bytes 90144768 | tf_op jit(solution)/shard_map/sub | solution.py:248
  (1028 shorter events, 785.2 us)
Async XLA Ops:
  7.2 156.3 %all-gather.8.cloned.1.call-start = ((), (), s32[]{:S(2)}) async-start(), calls=%async_computation.6 | async-start | bytes 2359296 | tf_op jit(solution)/shard_map/all_gather | solution.py:330
  47.9 48.5 %collective-permute-start.3 = (bf16[2048,256]{1,0:T(8,128)(2,1)}, bf16[2048,256]{1,0:T(8,128)(2,1)}, u32[]{:S(2)}, u32[]{:S(2)}) collective-permute-start(bf16[2048,256]{1,0:T(8,128)(2,1)} %slice.556), channel_id=1, source_target_pairs={{0,1},{1,0},{2,3},{3,2},{4,5},{5,4},{6,7},{7,6},{8,9},{9,8},{10,11... | collective-permute-start | bytes 3145736 | tf_op jit(solution)/shard_map/ppermute | solution.py:24
  48.0 50.2 %collective-permute-start.8 = (bf16[256,256]{1,0:T(8,128)(2,1)S(1)}, bf16[256,256]{1,0:T(8,128)(2,1)}, u32[]{:S(2)}, u32[]{:S(2)}) collective-permute-start(bf16[256,256]{1,0:T(8,128)(2,1)S(1)} %get-tuple-element.223), channel_id=1, source_target_pairs={{0,4},{4,0},{8,12},{12,8},{1,5},{5,1},{9,13},{13,9},{2,6},{6,2},{1... | collective-permute-start | bytes 393224 | tf_op jit(solution)/shard_map/ppermute | solution.py:24
  48.0 65.8 %collective-permute-start.9 = (bf16[256,256]{1,0:T(8,128)(2,1)S(1)}, bf16[256,256]{1,0:T(8,128)(2,1)}, u32[]{:S(2)}, u32[]{:S(2)}) collective-permute-start(bf16[256,256]{1,0:T(8,128)(2,1)S(1)} %get-tuple-element.223), channel_id=1, source_target_pairs={{0,8},{4,12},{8,0},{12,4},{1,9},{5,13},{9,1},{13,5},{2,10},{6,14},... | collective-permute-start | bytes 393224 | tf_op jit(solution)/shard_map/ppermute | solution.py:24
  50.1 64.7 %collective-permute-start.10 = (bf16[256,256]{1,0:T(8,128)(2,1)S(1)}, bf16[256,256]{1,0:T(8,128)(2,1)}, u32[]{:S(2)}, u32[]{:S(2)}) collective-permute-start(bf16[256,256]{1,0:T(8,128)(2,1)S(1)} %get-tuple-element.223), channel_id=1, source_target_pairs={{0,12},{4,8},{8,4},{12,0},{1,13},{5,9},{9,5},{13,1},{2,14},{6,10},... | collective-permute-start | bytes 393224 | tf_op jit(solution)/shard_map/ppermute | solution.py:24
  54.5 44.8 %collective-permute-start.13 = (bf16[128,1024]{0,1:T(8,128)(2,1)}, bf16[128,1024]{0,1:T(8,128)(2,1)}, u32[]{:S(2)}, u32[]{:S(2)}) collective-permute-start(bf16[128,1024]{0,1:T(8,128)(2,1)} %fusion.135), channel_id=1, source_target_pairs={{0,16},{16,0},{1,17},{17,1},{2,18},{18,2},{3,19},{19,3},{4,20},{20... | collective-permute-start | bytes 786440 | tf_op jit(solution)/shard_map/ppermute | solution.py:24
  101.1 123.0 %all-gather.10.cloned.1.call-start = ((), (), s32[]{:S(2)}) async-start(), calls=%async_computation.7 | async-start | bytes 2359296 | tf_op jit(solution)/shard_map/all_gather | solution.py:330
  150.7 118.8 %all-gather.12.cloned.1.call-start = ((), (), s32[]{:S(2)}) async-start(), calls=%async_computation.8 | async-start | bytes 2359296 | tf_op jit(solution)/shard_map/all_gather | solution.py:330
  202.1 125.4 %all-gather.14.cloned.1.call-start = ((), (), s32[]{:S(2)}) async-start(), calls=%async_computation.9 | async-start | bytes 2359296 | tf_op jit(solution)/shard_map/all_gather | solution.py:330
  278.2 109.4 %all-gather.16.cloned.1.call-start = ((), (), s32[]{:S(2)}) async-start(), calls=%async_computation.10 | async-start | bytes 2359296 | tf_op jit(solution)/shard_map/all_gather | solution.py:330
  312.1 119.0 %all-gather.18.cloned.1.call-start = ((), (), s32[]{:S(2)}) async-start(), calls=%async_computation.11 | async-start | bytes 2359296 | tf_op jit(solution)/shard_map/all_gather | solution.py:330
  358.6 1080.7 %reduce-scatter.29.cloned.1.call-start = ((), (), s32[]{:S(2)}) async-start(), calls=%async_computation.17 | async-start | bytes 2359296
  458.5 73.4 %collective-permute-start.32 = (bf16[3200,256]{1,0:T(8,128)(2,1)}, bf16[3200,256]{1,0:T(8,128)(2,1)}, u32[]{:S(2)}, u32[]{:S(2)}) collective-permute-start(bf16[3200,256]{1,0:T(8,128)(2,1)} %get-tuple-element.227), channel_id=1, source_target_pairs={{0,4},{4,0},{8,12},{12,8},{1,5},{5,1},{9,13},{13,9},{2,6},{6,2},{1... | collective-permute-start | bytes 4915208 | tf_op jit(solution)/shard_map/ppermute | solution.py:24
  458.5 132.6 %collective-permute-start.33 = (bf16[3200,256]{1,0:T(8,128)(2,1)}, bf16[3200,256]{1,0:T(8,128)(2,1)}, u32[]{:S(2)}, u32[]{:S(2)}) collective-permute-start(bf16[3200,256]{1,0:T(8,128)(2,1)} %get-tuple-element.228), channel_id=1, source_target_pairs={{0,8},{4,12},{8,0},{12,4},{1,9},{5,13},{9,1},{13,5},{2,10},{6,14},... | collective-permute-start | bytes 4915208 | tf_op jit(solution)/shard_map/ppermute | solution.py:24
  460.5 178.2 %collective-permute-start.34 = (bf16[3200,256]{1,0:T(8,128)(2,1)}, bf16[3200,256]{1,0:T(8,128)(2,1)}, u32[]{:S(2)}, u32[]{:S(2)}) collective-permute-start(bf16[3200,256]{1,0:T(8,128)(2,1)} %get-tuple-element.226), channel_id=1, source_target_pairs={{0,12},{4,8},{8,4},{12,0},{1,13},{5,9},{9,5},{13,1},{2,14},{6,10},... | collective-permute-start | bytes 4915208 | tf_op jit(solution)/shard_map/ppermute | solution.py:24
  468.7 168.6 %collective-permute-start.38 = (bf16[256,1024]{1,0:T(8,128)(2,1)S(1)}, bf16[256,1024]{1,0:T(8,128)(2,1)S(1)}, u32[]{:S(2)}, u32[]{:S(2)}) collective-permute-start(bf16[256,1024]{1,0:T(8,128)(2,1)S(1)} %get-tuple-element.209), channel_id=1, source_target_pairs={{0,8},{4,12},{8,0},{12,4},{1,9},{5,13},{9,1},{13,5},{2,10},{6,14},... | collective-permute-start | bytes 1572872 | tf_op jit(solution)/shard_map/ppermute | solution.py:24
  533.7 107.5 %collective-permute-start.30 = (bf16[256,1024]{1,0:T(8,128)(2,1)S(1)}, bf16[256,1024]{1,0:T(8,128)(2,1)S(1)}, u32[]{:S(2)}, u32[]{:S(2)}) collective-permute-start(bf16[256,1024]{1,0:T(8,128)(2,1)S(1)} %get-tuple-element.209), channel_id=1, source_target_pairs={{0,2},{1,3},{2,0},{3,1},{4,6},{5,7},{6,4},{7,5},{8,10},{9,11},{10,... | collective-permute-start | bytes 1572872 | tf_op jit(solution)/shard_map/ppermute | solution.py:24
  535.2 105.2 %collective-permute-start.41 = (bf16[256,1024]{1,0:T(8,128)(2,1)S(1)}, bf16[256,1024]{1,0:T(8,128)(2,1)S(1)}, u32[]{:S(2)}, u32[]{:S(2)}) collective-permute-start(bf16[256,1024]{1,0:T(8,128)(2,1)S(1)} %get-tuple-element.209), channel_id=1, source_target_pairs={{0,12},{4,8},{8,4},{12,0},{1,13},{5,9},{9,5},{13,1},{2,14},{6,10},... | collective-permute-start | bytes 1572872 | tf_op jit(solution)/shard_map/ppermute | solution.py:24
  592.8 48.5 %collective-permute-start.35 = (bf16[256,1024]{1,0:T(8,128)(2,1)S(1)}, bf16[256,1024]{1,0:T(8,128)(2,1)S(1)}, u32[]{:S(2)}, u32[]{:S(2)}) collective-permute-start(bf16[256,1024]{1,0:T(8,128)(2,1)S(1)} %get-tuple-element.209), channel_id=1, source_target_pairs={{0,4},{4,0},{8,12},{12,8},{1,5},{5,1},{9,13},{13,9},{2,6},{6,2},{1... | collective-permute-start | bytes 1572872 | tf_op jit(solution)/shard_map/ppermute | solution.py:24
  969.5 470.9 %reduce-scatter.27.cloned.1.call-start = ((), (), s32[]{:S(2)}) async-start(), calls=%async_computation.16 | async-start | bytes 2359296
  1032.7 409.0 %reduce-scatter.25.cloned.1.call-start = ((), (), s32[]{:S(2)}) async-start(), calls=%async_computation.15 | async-start | bytes 2359296
  1072.9 102.5 %collective-permute-start.75 = (bf16[1600,1024]{1,0:T(8,128)(2,1)}, bf16[1600,1024]{1,0:T(8,128)(2,1)}, u32[]{:S(2)}, u32[]{:S(2)}) collective-permute-start(bf16[1600,1024]{1,0:T(8,128)(2,1)} %constant_dynamic-slice_fusion.8), channel_id=1, source_target_pairs={{0,16},{16,0},{1,17},{17,1},{2,18},{18,2},{3,19},{19,3},{4,20},{20... | collective-permute-start | bytes 9830408 | tf_op jit(solution)/shard_map/ppermute | solution.py:24
  1080.6 80.6 %collective-permute-start.80 = (s32[4,1024]{1,0:T(4,128)S(1)}, s32[4,1024]{1,0:T(4,128)S(1)}, u32[]{:S(2)}, u32[]{:S(2)}) collective-permute-start(s32[4,1024]{1,0:T(4,128)S(1)} %copy-done.172), channel_id=1, source_target_pairs={{0,16},{16,0},{1,17},{17,1},{2,18},{18,2},{3,19},{19,3},{4,20},{20... | collective-permute-start | bytes 49160 | tf_op jit(solution)/shard_map/ppermute | solution.py:24
  1083.6 78.4 %collective-permute-start.69 = (bf16[512,1024]{1,0:T(8,128)(2,1)}, bf16[512,1024]{1,0:T(8,128)(2,1)}, u32[]{:S(2)}, u32[]{:S(2)}) collective-permute-start(bf16[512,1024]{1,0:T(8,128)(2,1)} %pad_maximum_fusion.25), channel_id=1, source_target_pairs={{0,1},{1,0},{2,3},{3,2},{4,5},{5,4},{6,7},{7,6},{8,9},{9,8},{10,11... | collective-permute-start | bytes 3145736 | tf_op jit(solution)/shard_map/ppermute | solution.py:24
  1091.5 351.3 %reduce-scatter.23.cloned.1.call-start = ((), (), s32[]{:S(2)}) async-start(), calls=%async_computation.14 | async-start | bytes 2359296
  1184.4 88.0 %collective-permute-start.77 = (bf16[1600,256]{1,0:T(8,128)(2,1)}, bf16[1600,256]{1,0:T(8,128)(2,1)}, u32[]{:S(2)}, u32[]{:S(2)}) collective-permute-start(bf16[1600,256]{1,0:T(8,128)(2,1)} %get-tuple-element.232), channel_id=1, source_target_pairs={{0,8},{4,12},{8,0},{12,4},{1,9},{5,13},{9,1},{13,5},{2,10},{6,14},... | collective-permute-start | bytes 2457608 | tf_op jit(solution)/shard_map/ppermute | solution.py:24
  1184.4 88.0 %collective-permute-start.76 = (bf16[1600,256]{1,0:T(8,128)(2,1)}, bf16[1600,256]{1,0:T(8,128)(2,1)}, u32[]{:S(2)}, u32[]{:S(2)}) collective-permute-start(bf16[1600,256]{1,0:T(8,128)(2,1)} %get-tuple-element.233), channel_id=1, source_target_pairs={{0,4},{4,0},{8,12},{12,8},{1,5},{5,1},{9,13},{13,9},{2,6},{6,2},{1... | collective-permute-start | bytes 2457608 | tf_op jit(solution)/shard_map/ppermute | solution.py:24
  1194.4 249.5 %reduce-scatter.21.cloned.1.call-start = ((), (), s32[]{:S(2)}) async-start(), calls=%async_computation.13 | async-start | bytes 2359296
  1219.0 62.6 %collective-permute-start.73 = (bf16[512,1024]{1,0:T(8,128)(2,1)S(1)}, bf16[512,1024]{1,0:T(8,128)(2,1)}, u32[]{:S(2)}, u32[]{:S(2)}) collective-permute-start(bf16[512,1024]{1,0:T(8,128)(2,1)S(1)} %pad_maximum_fusion.26), channel_id=1, source_target_pairs={{0,1},{1,0},{2,3},{3,2},{4,5},{5,4},{6,7},{7,6},{8,9},{9,8},{10,11... | collective-permute-start | bytes 3145736 | tf_op jit(solution)/shard_map/ppermute | solution.py:24
  1275.6 88.3 %collective-permute-start.79 = (bf16[4,1600,256]{2,1,0:T(8,128)(2,1)}, bf16[4,1600,256]{2,1,0:T(8,128)(2,1)}, u32[]{:S(2)}, u32[]{:S(2)}) collective-permute-start(bf16[4,1600,256]{2,1,0:T(8,128)(2,1)} %pad_maximum_fusion), channel_id=1, source_target_pairs={{0,16},{16,0},{1,17},{17,1},{2,18},{18,2},{3,19},{19,3},{4,20},{20... | collective-permute-start | bytes 9830408 | tf_op jit(solution)/shard_map/ppermute | solution.py:24
  1281.6 176.2 %reduce-scatter.19.cloned.1.call-start = ((), (), s32[]{:S(2)}) async-start(), calls=%async_computation.12 | async-start | bytes 2359296
  1319.4 50.7 %collective-permute-start.81 = (bf16[512,1024]{1,0:T(8,128)(2,1)S(1)}, bf16[512,1024]{1,0:T(8,128)(2,1)S(1)}, u32[]{:S(2)}, u32[]{:S(2)}) collective-permute-start(bf16[512,1024]{1,0:T(8,128)(2,1)S(1)} %slice.854), channel_id=1, source_target_pairs={{0,1},{1,0},{2,3},{3,2},{4,5},{5,4},{6,7},{7,6},{8,9},{9,8},{10,11... | collective-permute-start | bytes 3145736 | tf_op jit(solution)/shard_map/ppermute | solution.py:24
  (317 other events, 7467.0 us)
Sparse Core Ops, SparseCore 0:
  101.2 62.2 all-gather.7
  166.1 49.8 all-gather.9
  218.6 50.8 all-gather.11
  278.3 49.1 all-gather.13
  330.0 49.2 all-gather.15
  381.7 49.2 all-gather.17
  969.6 66.1 reduce-scatter.28
  1039.4 71.6 reduce-scatter.26
  1114.6 72.5 reduce-scatter.24
  1194.6 96.7 reduce-scatter.22
  1294.9 76.7 reduce-scatter.20
  1381.7 76.0 reduce-scatter.18

commit v2 on v1

v2 whole, which is shorter than its diff:
```python
import jax
import jax.numpy as jnp
from jax import lax
from jax.experimental import pallas as pl
from jax.experimental.layout import Layout, with_layout_constraint
from jax.experimental.pallas import tpu as pltpu
from jax.sharding import PartitionSpec as P

HEAD = 64
STEP = 10


EPS_NORM = 1e-05
ZLOSS = 0.001
CLIP = 0.01
BETA_ONE = 0.9
BETA_TWO = 0.95
EPS_ADAM = 1e-08
RATES = (0.03, 0.1, 0.03, 0.015, 0.05, 0.15, 0.7, 0.7)
DECAYS = (0.1, 0.1, 0.1, 0.1, 0.1, 0.0, 0.0, 0.0)
F32 = jnp.float32
BF16 = jnp.bfloat16


def swap(block, axis, mask):
    route = [(i, i ^ mask) for i in range(lax.axis_size(axis))]
    return lax.ppermute(block, axis, route)


def masks_down(size):
    found = []
    mask = size // 2
    while mask >= 1:
        found.append(mask)
        mask //= 2
    return found


def reverse_bits(value, size):
    result = 0
    mask = 1
    while mask < size:
        result = result * 2 + (value & mask) // mask
        mask *= 2
    return result


def spread(block, held=()):
    for step, mask in enumerate(masks_down(lax.axis_size("seq"))):
        received = swap(block, "seq", mask)
        if held:
            received = after(received, *held[step])
        block = jnp.concatenate([block, received], 0)
    return block


def collect(block, steps=0, skip=0, held=None):
    masks = masks_down(lax.axis_size("seq"))[::-1]
    for mask in masks[skip : steps or len(masks)]:
        half = block.shape[0] // 2
        sent = swap(block[half:].astype(BF16), "seq", mask)
        if held is not None:
            sent = after(sent, held)
        block = block[:half].astype(F32) + sent.astype(F32)
    return block


def from_all(block, axis):
    size = lax.axis_size(axis)
    found = jnp.stack([block] + [swap(block, axis, mask) for mask in range(1, size)])
    return jnp.take(found, lax.axis_index(axis) ^ jnp.arange(size), axis=0)


def sum_everywhere(block):
    for axis in ("seq", "pipe", "dp"):
        block = jnp.sum(from_all(block, axis), 0)
    return block


def norm_rows(values, gain, bias):
    center = values - jnp.mean(values, -1, keepdims=True)
    spread_sq = jnp.mean(center * center, -1, keepdims=True)
    return center * lax.rsqrt(spread_sq + EPS_NORM) * gain + bias


def gelu_tanh(values):
    return jax.nn.gelu(values, approximate=True)


def head_pairs(values):
    tile, columns = values.shape
    place = lax.broadcasted_iota(jnp.int32, (tile, columns), 1)
    wide = values.astype(F32)
    return jnp.concatenate(
        [jnp.where(place < HEAD, wide, 0.0), jnp.where(place < HEAD, 0.0, wide)], 0
    )


def join_pair(values):
    columns, double = values.shape
    tile = double // 2
    place = lax.broadcasted_iota(jnp.int32, (columns, tile), 0)
    return jnp.where(place < HEAD, values[:, :tile], values[:, tile:]).T


def pair_allowed(place_row, document_row, place_column, document_column):
    allowed = (place_column[...] <= place_row[...]) & (document_column[...] == document_row[...])
    return jnp.concatenate([allowed, allowed], 1)


def across(left, right):
    return lax.dot_general(left, right, (((1,), (1,)), ((), ())), preferred_element_type=F32)


def attend_kernel(
    packed_ref, place_row, document_row, place_column, document_column, out_ref, log_ref
):
    tile, columns = out_ref.shape
    here = pl.ds(pl.multiple_of(pl.program_id(0) * tile, tile), tile)
    allowed = pair_allowed(place_row, document_row, place_column, document_column)
    for pair in range(columns // 128):
        span = slice(pair * 128, pair * 128 + 128)
        key_span = slice(columns + pair * 128, columns + pair * 128 + 128)
        value_span = slice(2 * columns + pair * 128, 2 * columns + pair * 128 + 128)
        queries = (head_pairs(packed_ref[here, span]) * HEAD ** (-0.5)).astype(BF16)
        scores = jnp.where(allowed, across(packed_ref[:, key_span], queries), -1e30)
        top = jnp.max(scores, 0, keepdims=True)
        exponent = jnp.exp(scores - top)
        total = jnp.sum(exponent, 0, keepdims=True)
        log_ref[pair, 0] = top + jnp.log(total)
        mixed = jnp.dot(
            packed_ref[:, value_span].T, exponent.astype(BF16), preferred_element_type=F32
        )
        out_ref[:, span] = join_pair(mixed / total).astype(out_ref.dtype)


def row_specs(length, tile):
    return [
        pl.BlockSpec((1, tile), lambda t: (0, t)),
        pl.BlockSpec((1, tile), lambda t: (0, t)),
        pl.BlockSpec((length, 1), lambda t: (0, 0)),
        pl.BlockSpec((length, 1), lambda t: (0, 0)),
    ]


def both_ways(rows):
    place, document = rows
    return place[None, :], document[None, :], place[:, None], document[:, None]


def attend_forward(packed, columns, rows):
    length, stored = packed.shape
    pairs = columns // 128
    tile = min(256, length)
    steps = length // tile
    return pl.pallas_call(
        attend_kernel,
        grid=(steps,),
        in_specs=[pl.BlockSpec((length, stored), lambda t: (0, 0))] + row_specs(length, tile),
        out_specs=[
            pl.BlockSpec((tile, columns), lambda t: (t, 0)),
            pl.BlockSpec((pairs, 1, 1, 2 * tile), lambda t: (0, t, 0, 0)),
        ],
        out_shape=[
            jax.ShapeDtypeStruct((length, columns), BF16),
            jax.ShapeDtypeStruct((pairs, steps, 1, 2 * tile), F32),
        ],
        compiler_params=pltpu.CompilerParams(vmem_limit_bytes=48 * 1024 * 1024),
        cost_estimate=pl.CostEstimate(
            flops=4 * length * length * columns,
            bytes_accessed=2 * length * (stored + columns),
            transcendentals=length * length * pairs * 2,
        ),
    )(packed, *both_ways(rows))


def attend_back_kernel(
    packed_ref,
    grad_ref,
    log_ref,
    place_row,
    document_row,
    place_column,
    document_column,
    out_ref,
    key_total,
    value_total,
):
    tile, columns = grad_ref.shape
    step = pl.program_id(0)
    here = pl.ds(pl.multiple_of(step * tile, tile), tile)
    allowed = pair_allowed(place_row, document_row, place_column, document_column)
    factor = HEAD ** (-0.5)

    @pl.when(step == 0)
    def _():
        key_total[...] = jnp.zeros_like(key_total)
        value_total[...] = jnp.zeros_like(value_total)

    for pair in range(columns // 128):
        span = slice(pair * 128, pair * 128 + 128)
        key_span = slice(columns + pair * 128, columns + pair * 128 + 128)
        value_span = slice(2 * columns + pair * 128, 2 * columns + pair * 128 + 128)
        queries = (head_pairs(packed_ref[here, span]) * factor).astype(BF16)
        grads = head_pairs(grad_ref[:, span]).astype(BF16)
        keys = packed_ref[:, key_span]
        scores = jnp.where(allowed, across(keys, queries), -1e30)
        probabilities = jnp.exp(scores - log_ref[pair, 0])
        value_total[:, span] += jnp.dot(
            probabilities.astype(BF16), grads, preferred_element_type=F32
        )
        grad_soft = across(packed_ref[:, value_span], grads)
        mean = jnp.sum(probabilities * grad_soft, 0, keepdims=True)
        grad_scores = (probabilities * (grad_soft - mean)).astype(BF16)
        key_total[:, span] += jnp.dot(grad_scores, queries, preferred_element_type=F32)
        grad_queries = jnp.dot(keys.T, grad_scores, preferred_element_type=F32)
        out_ref[here, span] = (join_pair(grad_queries) * factor).astype(out_ref.dtype)

    @pl.when(step == pl.num_programs(0) - 1)
    def _():
        out_ref[:, columns : 2 * columns] = key_total[...].astype(out_ref.dtype)
        out_ref[:, 2 * columns : 3 * columns] = value_total[...].astype(out_ref.dtype)
        out_ref[:, 3 * columns :] = jnp.zeros(
            (out_ref.shape[0], out_ref.shape[1] - 3 * columns), out_ref.dtype
        )


def attend_backward(packed, log_sums, grad_mixed, rows):
    length, stored = packed.shape
    columns = grad_mixed.shape[1]
    pairs = columns // 128
    tile = min(256, length)
    steps = length // tile
    return pl.pallas_call(
        attend_back_kernel,
        grid=(steps,),
        in_specs=[
            pl.BlockSpec((length, stored), lambda t: (0, 0)),
            pl.BlockSpec((tile, columns), lambda t: (t, 0)),
            pl.BlockSpec((pairs, 1, 1, 2 * tile), lambda t: (0, t, 0, 0)),
        ]
        + row_specs(length, tile),
        out_specs=pl.BlockSpec((length, stored), lambda t: (0, 0)),
        out_shape=jax.ShapeDtypeStruct((length, stored), BF16),
        scratch_shapes=[pltpu.VMEM((length, columns), F32)] * 2,
        compiler_params=pltpu.CompilerParams(vmem_limit_bytes=48 * 1024 * 1024),
        cost_estimate=pl.CostEstimate(
            flops=10 * length * length * columns,
            bytes_accessed=4 * length * stored,
            transcendentals=length * length * pairs * 2,
        ),
    )(packed, grad_mixed, log_sums, *both_ways(rows))


def forward_attention(residual, w_attn, gain_rows, rows):
    columns = w_attn.shape[1] // 4
    normed = norm_rows(residual, gain_rows[0], gain_rows[1])
    first_full = spread(normed.astype(BF16))
    packed = jnp.dot(first_full, w_attn, preferred_element_type=F32).astype(BF16)
    mixed_rows, log_sums = attend_forward(packed, columns, rows)
    branch = jnp.einsum(
        "tc,dc->td", mixed_rows, w_attn[:, 3 * columns :], preferred_element_type=F32
    )
    return residual + collect(branch), (residual, first_full, packed, log_sums, mixed_rows)


def forward_feed(middle, w_fc, w_proj, gain_rows):
    second = norm_rows(middle, gain_rows[2], gain_rows[3])
    second_full = spread(second.astype(BF16))
    hidden = jnp.dot(second_full, w_fc, preferred_element_type=F32)
    active = gelu_tanh(hidden).astype(BF16)
    branch = jnp.einsum("tf,df->td", active, w_proj, preferred_element_type=F32)
    return middle + collect(branch), (middle, second_full, hidden, active)


def backward_feed(grad_out, saved, w_fc, w_proj, gain_rows):
    middle, second_full, hidden, active = saved
    grad_z = spread(grad_out.astype(BF16))
    grad_active = jnp.dot(grad_z, w_proj, preferred_element_type=F32)
    _, gelu_pull = jax.vjp(gelu_tanh, hidden)
    grad_hidden = gelu_pull(grad_active)[0].astype(BF16)
    grad_second = collect(
        jnp.einsum("tf,df->td", grad_hidden, w_fc, preferred_element_type=F32)
    )
    grad_fc = jnp.einsum("td,tf->df", second_full, grad_hidden, preferred_element_type=F32)
    grad_proj = jnp.einsum("td,tf->df", grad_z, active, preferred_element_type=F32)
    _, norm_pull = jax.vjp(norm_rows, middle, gain_rows[2], gain_rows[3])
    grad_middle, grad_gain, grad_bias = norm_pull(grad_second)
    return (
        grad_middle + grad_out,
        (grad_fc.astype(BF16), grad_proj.astype(BF16)),
        jnp.stack([grad_gain, grad_bias]),
    )


def backward_attention(grad_middle, saved, w_attn, gain_rows, rows):
    residual, first_full, packed, log_sums, mixed_rows = saved
    columns = w_attn.shape[1] // 4
    grad_y = spread(grad_middle.astype(BF16))
    grad_mixed = jnp.dot(
        grad_y, w_attn[:, 3 * columns :], preferred_element_type=F32
    ).astype(BF16)
    grad_packed = attend_backward(packed, log_sums, grad_mixed, rows)
    grad_first = collect(
        jnp.einsum("tc,dc->td", grad_packed, w_attn, preferred_element_type=F32)
    )
    grad_out_w = jnp.einsum("td,tc->dc", grad_y, mixed_rows, preferred_element_type=F32)
    grad_qkv = jnp.einsum(
        "td,tc->dc", first_full, grad_packed[:, : 3 * columns], preferred_element_type=F32
    )
    _, norm_pull = jax.vjp(norm_rows, residual, gain_rows[0], gain_rows[1])
    grad_residual, grad_gain, grad_bias = norm_pull(grad_first)
    return (
        grad_residual + grad_middle,
        jnp.concatenate([grad_qkv, grad_out_w], 1).astype(BF16),
        jnp.stack([grad_gain, grad_bias]),
    )


def block(go, step, *operands):
    shapes = jax.eval_shape(step, *operands)

    def idle(*_):
        return jax.tree.map(lambda leaf: jnp.zeros(leaf.shape, leaf.dtype), shapes)

    return lax.cond(go, step, idle, *operands)


def after(value, *others):
    return lax.optimization_barrier((value, *others))[0]


def together(*values):
    return lax.optimization_barrier(values)


def by_rows(matrix):
    return with_layout_constraint(matrix, Layout((0, 1)))


def exchange_blocks(blocks, axis):
    return [blocks[0]] + [swap(blocks[m], axis, m) for m in range(1, len(blocks))]


def place_columns(blocks, index):
    width = blocks[0].shape[1]
    whole = jnp.zeros((blocks[0].shape[0], width * len(blocks)), blocks[0].dtype)
    for m, block in enumerate(blocks):
        whole = lax.dynamic_update_slice_in_dim(whole, block, (index ^ m) * width, 1)
    return whole


def take_columns(whole, index, count):
    width = whole.shape[1] // count
    return [
        lax.dynamic_slice_in_dim(whole, (index ^ m) * width, width, 1) for m in range(count)
    ]


def row_of(column):
    return jnp.broadcast_to(column, (column.shape[0], 128)).T[:1]


def head_kernel(rows_ref, table_ref, bias_ref, low_ref, mixed_ref, top_ref, sum_ref):
    table = table_ref[...]
    logits = lax.dot_general(
        rows_ref[...], table, (((1,), (1,)), ((), ())), preferred_element_type=F32
    )
    logits = logits + bias_ref[...]
    row_top = jnp.max(logits, 1, keepdims=True)
    exponent = jnp.exp(logits - row_top)
    top_ref[...] = row_of(row_top)
    sum_ref[...] = row_of(jnp.sum(exponent, 1, keepdims=True))
    low = exponent.astype(BF16)
    low_ref[...] = low
    mixed_ref[...] = jnp.dot(low, table, preferred_element_type=F32).astype(mixed_ref.dtype)


def head_block(rows, table, bias):
    length, width = rows.shape
    part_rows = table.shape[0]
    tile = min(512, length)
    return pl.pallas_call(
        head_kernel,
        grid=(length // tile,),
        in_specs=[
            pl.BlockSpec((tile, width), lambda t: (t, 0)),
            pl.BlockSpec((part_rows, width), lambda t: (0, 0), pipeline_mode=pl.Buffered(1)),
            pl.BlockSpec((1, part_rows), lambda t: (0, 0), pipeline_mode=pl.Buffered(1)),
        ],
        out_specs=[
            pl.BlockSpec((tile, part_rows), lambda t: (t, 0)),
            pl.BlockSpec((tile, width), lambda t: (t, 0)),
            pl.BlockSpec((1, tile), lambda t: (0, t)),
            pl.BlockSpec((1, tile), lambda t: (0, t)),
        ],
        out_shape=[
            jax.ShapeDtypeStruct((length, part_rows), BF16),
            jax.ShapeDtypeStruct((length, width), F32),
            jax.ShapeDtypeStruct((1, length), F32),
            jax.ShapeDtypeStruct((1, length), F32),
        ],
        compiler_params=pltpu.CompilerParams(vmem_limit_bytes=56 * 1024 * 1024),
        cost_estimate=pl.CostEstimate(
            flops=4 * length * part_rows * width,
            bytes_accessed=2 * part_rows * (width + length) + 6 * length * width,
            transcendentals=length * part_rows,
        ),
    )(rows, table, bias)


def table_kernel(count, *refs):
    low_refs, row_refs, out_ref = refs[:count], refs[count : 2 * count], refs[2 * count]
    total = None
    for low_ref, row_ref in zip(low_refs, row_refs):
        product = lax.dot_general(
            low_ref[...], row_ref[...], (((0,), (0,)), ((), ())), preferred_element_type=F32
        )
        total = product if total is None else total + product
    out_ref[...] = total.astype(out_ref.dtype)


def table_gradient_of(lows, rows, first, count_tiles, tile):
    count = len(lows)
    length, part_rows = lows[0].shape
    width = rows[0].shape[1]
    return pl.pallas_call(
        lambda *refs: table_kernel(count, *refs),
        grid=(count_tiles,),
        in_specs=[pl.BlockSpec((length, tile), lambda v: (0, v + first))] * count
        + [pl.BlockSpec((length, width), lambda v: (0, 0), pipeline_mode=pl.Buffered(1))] * count,
        out_specs=pl.BlockSpec((tile, width), lambda v: (v, 0)),
        out_shape=jax.ShapeDtypeStruct((count_tiles * tile, width), BF16),
        compiler_params=pltpu.CompilerParams(vmem_limit_bytes=60 * 1024 * 1024),
        cost_estimate=pl.CostEstimate(
            flops=2 * count * length * count_tiles * tile * width,
            bytes_accessed=2 * count_tiles * tile * (width + count * length)
            + 2 * count * length * width,
            transcendentals=0,
        ),
    )(*lows, *rows)


def part_place(group, half, part_rows, slice_rows):
    wanted = group * part_rows + half * (part_rows // 2)
    return jnp.minimum(wanted, slice_rows - part_rows // 2), wanted


def scatter_kernel(count_ref, list_ref, near_ref, far_ref, rows_ref, out_ref, square_ref, wide):
    slice_rows = out_ref.shape[0]
    shift = (slice_rows - 1).bit_length()
    replicas, half_rows = near_ref.shape[:2]
    section, replica = lax.axis_index("pipe"), lax.axis_index("dp")
    out_ref[...] = jnp.zeros_like(out_ref)
    for m in range(replicas):
        for half, part in ((section, near_ref), (1 - section, far_ref)):
            start, _ = part_place(replica ^ m, half, 2 * half_rows, slice_rows)
            out_ref[pl.ds(pl.multiple_of(start, 8), half_rows), :] += part[m].astype(F32)
    wide[...] = rows_ref[...].astype(F32)

    def add_one(k):
        coded = list_ref[k]
        here = pl.ds(jnp.bitwise_and(coded, (1 << shift) - 1), 1)
        out_ref[here, :] += wide[pl.ds(lax.shift_right_logical(coded, shift), 1), :]

    def add_some(k, carry):
        for u in range(8):
            add_one(8 * k + u)
        return carry

    def add_last(k, carry):
        add_one(k)
        return carry

    count = count_ref[0]
    groups = lax.shift_right_logical(count, 3)
    lax.fori_loop(0, groups, add_some, 0)
    lax.fori_loop(8 * groups, count, add_last, 0)
    result = out_ref[...]
    square_ref[...] = jnp.sum(result * result, 0, keepdims=True)


def scatter_rows(listing, count, near, far, rows, slice_rows):
    columns = near.shape[2]
    whole = pl.BlockSpec(memory_space=pltpu.VMEM)
    scalars = pl.BlockSpec(memory_space=pltpu.SMEM)
    return pl.pallas_call(
        scatter_kernel,
        in_specs=[scalars, scalars, whole, whole, whole],
        out_specs=[whole, whole],
        out_shape=[
            jax.ShapeDtypeStruct((slice_rows, columns), F32),
            jax.ShapeDtypeStruct((1, columns), F32),
        ],
        scratch_shapes=[pltpu.VMEM(rows.shape, F32)],
        compiler_params=pltpu.CompilerParams(vmem_limit_bytes=60 * 1024 * 1024),
        cost_estimate=pl.CostEstimate(
            flops=4 * slice_rows * columns,
            bytes_accessed=8 * slice_rows * columns + 2 * rows.size,
            transcendentals=0,
        ),
    )(count, listing, near, far, rows)


def scatter_over(part, axes):
    return lax.psum_scatter(part, axes, scatter_dimension=0, tiled=True)


def merge_stats(stats):
    both = jnp.stack(stats)
    for axis, place in (("seq", 2), ("dp", 1)):
        size = lax.axis_size(axis)
        found = [both]
        for mask in range(1, size):
            shift = reverse_bits(mask, size) if axis == "seq" else mask
            order = jnp.array([k ^ shift for k in range(size)])
            found.append(jnp.take(swap(both, axis, mask), order, axis=place))
        top = found[0][0]
        for pair in found[1:]:
            top = jnp.maximum(top, pair[0])
        both = jnp.stack([top, sum(pair[1] * jnp.exp(pair[0] - top) for pair in found)])
    return both[0] + jnp.log(both[1])


def adamw_update(master, first, second, gradient, rate, decay):
    first_new = BETA_ONE * first + (1.0 - BETA_ONE) * gradient
    second_new = BETA_TWO * second + (1.0 - BETA_TWO) * gradient * gradient
    ratio = (
        first_new
        / (1.0 - BETA_ONE**STEP)
        / (jnp.sqrt(second_new / (1.0 - BETA_TWO**STEP)) + EPS_ADAM)
    )
    return (master - rate * (ratio + decay * master), first_new, second_new)


def per_device(
    token_ids,
    segments,
    valid,
    attn_qkv,
    attn_qkv_first,
    attn_qkv_second,
    attn_out,
    attn_out_first,
    attn_out_second,
    mlp_in,
    mlp_in_first,
    mlp_in_second,
    mlp_out,
    mlp_out_first,
    mlp_out_second,
    embed_table,
    embed_table_first,
    embed_table_second,
    position_table,
    position_table_first,
    position_table_second,
    norm_params,
    norm_params_first,
    norm_params_second,
    final_norm,
    final_norm_first,
    final_norm_second,
):
    section, replica, lane = lax.axis_index("pipe"), lax.axis_index("dp"), lax.axis_index("seq")
    sections, replicas, lanes = (lax.axis_size(name) for name in ("pipe", "dp", "seq"))
    length = token_ids.shape[1]
    assert sections == 2 and token_ids.shape[0] == sections and attn_qkv.shape[0] == 1
    shard_rows = length // lanes
    slice_rows, slice_columns = embed_table.shape
    width = slice_columns * replicas
    part_rows = -(-slice_rows // (replicas * 128)) * 128
    half_rows = part_rows // 2
    assert part_rows * (replicas - 1) < slice_rows
    lane_order = [reverse_bits(k, lanes) for k in range(lanes)]
    lane_blocks = lane ^ jnp.array(lane_order)

    norm_mine = jnp.concatenate([norm_params.reshape(-1, norm_params.shape[2]), final_norm], 0)
    norm_columns = norm_mine.shape[1]
    norm_all = norm_mine[None]
    for axis in ("seq", "dp", "pipe"):
        for mask in reversed(masks_down(lax.axis_size(axis))):
            norm_all = jnp.concatenate([norm_all, swap(norm_all, axis, mask)], 0)
    own_place = (section * replicas + replica) * lanes + lane
    norm_all = jnp.take(norm_all, own_place ^ jnp.arange(norm_all.shape[0]), axis=0)
    norm_all = jnp.transpose(norm_all, (1, 0, 2)).reshape(norm_mine.shape[0], width)
    gain_stack = norm_all[:-2].reshape(norm_params.shape[0], 4, width)
    final_rows = norm_all[-2:]

    own_ids = lax.dynamic_index_in_dim(token_ids, section, 0, keepdims=False)
    own_valid = lax.dynamic_index_in_dim(valid, section, 0, keepdims=False)
    row_segments = lax.dynamic_index_in_dim(segments, section, 0, keepdims=False)
    coded = own_ids * 2 + own_valid
    coded_all = jnp.stack([coded] + [swap(coded, "dp", m) for m in range(1, replicas)])
    ids_all = coded_all // 2
    position = jnp.arange(length)
    weight_all = jnp.where(position < length - 1, coded_all % 2, 0).astype(F32)
    targets_all = jnp.roll(ids_all, -1, axis=1)

    def by_lane(values):
        return jnp.take(values.reshape(-1, lanes, shard_rows), lane_blocks, axis=1)

    ids_lane, weight_lane, targets_lane = by_lane(ids_all), by_lane(weight_all), by_lane(targets_all)

    go = lax.optimization_barrier(jnp.int32(1)) > 0
    qkv_columns = attn_qkv.shape[2] * attn_qkv.shape[3]
    attn_columns = qkv_columns + attn_out.shape[1]
    shards = [
        jnp.concatenate([attn_qkv[0].reshape(-1, qkv_columns), attn_out[0].T], 1),
        mlp_in[0],
        mlp_out[0].T,
    ]
    gathered = [
        lax.all_gather(by_rows(shard.astype(BF16)), "dp", axis=0, tiled=True) for shard in shards
    ]

    def two_layers(mine):
        other = swap(mine, "pipe", 1)
        return jnp.where(section == 0, mine, other), jnp.where(section == 0, other, mine)

    w_attn, w_fc = two_layers(gathered[0]), two_layers(gathered[1])

    vocab_start = lane * slice_rows
    wanted = jnp.transpose(ids_lane, (1, 0, 2)).reshape(-1) - vocab_start
    inside = (wanted >= 0) & (wanted < slice_rows)
    picked = jnp.take(embed_table, jnp.clip(wanted, 0, slice_rows - 1), axis=0)
    picked = jnp.where(inside[:, None], picked, 0.0).astype(BF16)
    picked = collect(picked).astype(BF16).reshape(replicas, shard_rows, slice_columns)
    embed_rows = place_columns(exchange_blocks(list(picked), "dp"), replica)
    position_low = position_table.astype(BF16)
    position_rows = place_columns(
        exchange_blocks([position_low] * replicas, "dp"), replica
    )
    start_rows = embed_rows.astype(F32) + position_rows.astype(F32)
    next_first = lax.ppermute(embed_rows[:1], "seq", [(k, k - 1) for k in range(1, lanes)])
    target_rows = jnp.concatenate([embed_rows[1:], next_first], 0).astype(F32)

    coded_other = swap(coded_all, "pipe", 1)
    ids_both = jnp.where(
        section == 0,
        jnp.concatenate([ids_all, coded_other // 2], 0),
        jnp.concatenate([coded_other // 2, ids_all], 0),
    )
    back_wanted = jnp.transpose(by_lane(ids_both), (1, 0, 2)).reshape(-1) - vocab_start
    back_inside = (back_wanted >= 0) & (back_wanted < slice_rows)
    back_number = jnp.arange(back_wanted.shape[0])
    back_coded = back_number * (1 << (slice_rows - 1).bit_length()) + back_wanted
    back_listing = jnp.sort(jnp.where(back_inside, back_coded, 2**31 - 1))
    back_count = jnp.sum(back_inside.astype(jnp.int32))[None]
    start_rows, back_listing, back_count = together(start_rows, back_listing, back_count)

    table_f32 = after(embed_table, start_rows)
    table_parts = [
        lax.dynamic_slice_in_dim(
            table_f32,
            part_place(replica ^ m, section, part_rows, slice_rows)[0],
            half_rows,
            0,
        ).astype(BF16)
        for m in range(replicas)
    ]
    table_blocks = exchange_blocks(table_parts, "dp")
    bias_halves = []
    for half in (section, 1 - section):
        start, wanted = part_place(replica, half, part_rows, slice_rows)
        bias_halves.append(jnp.where(start + jnp.arange(half_rows) >= wanted, 0.0, -1e30))
    table_bias = jnp.concatenate(bias_halves).astype(F32)[None]

    row_place = (lane_blocks[:, None] * shard_rows + jnp.arange(shard_rows)[None, :]).reshape(-1)
    row_document = jnp.take(row_segments.reshape(lanes, shard_rows), lane_blocks, axis=0).reshape(-1)
    places = (row_place, row_document)
    rows = start_rows
    saved = []
    for layer in range(2):
        gains = gain_stack[layer]
        rows, kept_attn = block(go, forward_attention, rows, w_attn[layer], gains, places)
        if layer == 0:
            rows, gathered[2] = together(rows, gathered[2])
            w_proj = two_layers(gathered[2])
        rows, kept_feed = block(go, forward_feed, rows, w_fc[layer], w_proj[layer], gains)
        saved.append((kept_attn, kept_feed))
        if layer == 0:
            rows, *table_blocks = together(rows, *table_blocks)
            table_half = place_columns(table_blocks, replica)
            table_other = swap(table_half, "pipe", 1)
    table = jnp.concatenate([table_half, table_other], 0)
    final_value, final_pull = jax.vjp(norm_rows, rows, final_rows[0], final_rows[1])
    final_low = final_value.astype(BF16)

    full, heads = [], []
    steps = len(masks_down(lanes))
    for m, part in enumerate(exchange_blocks([final_low] * replicas, "dp")):
        held = [[heads[m - back][2]] if m >= back else [] for back in range(steps + 1, 0, -1)]
        full.append(spread(after(part, *held[0]), held[1:]))
        heads.append(block(go, head_block, full[m], table, table_bias))
    stat_shape = (replicas, lanes, shard_rows)
    row_top = jnp.stack([head[2] for head in heads]).reshape(stat_shape)
    row_sum = jnp.stack([head[3] for head in heads]).reshape(stat_shape)
    log_total = merge_stats((row_top, row_sum))
    scale = weight_lane * (1.0 + 2.0 * ZLOSS * log_total) * jnp.exp(row_top - log_total)
    own_weight, own_log = weight_lane[0, 0], log_total[0, 0]
    target_logit = jnp.sum(final_low.astype(F32) * target_rows, 1)
    own_penalty = own_weight * ZLOSS * own_log * own_log
    own_loss = own_weight * (own_log - target_logit) + own_penalty

    scale_flat = scale.reshape(replicas, length)
    weighted_parts = [scale_flat[m][:, None] * heads[m][1] for m in range(replicas)]
    first_sums = [collect(part, 1) for part in weighted_parts]
    tile = max(t for t in range(128, 641, 128) if part_rows % t == 0)
    first_tiles = half_rows // tile
    lows = [head[0] for head in heads]
    scaled = [
        after((scale_flat[m][:, None] * full[m].astype(F32)).astype(BF16), *first_sums)
        for m in range(replicas)
    ]
    late_tiles = part_rows // tile - first_tiles
    late = block(
        go,
        lambda lows, scaled: table_gradient_of(lows, scaled, first_tiles, late_tiles, tile),
        lows,
        scaled,
    )
    head_parts = [collect(part, 0, 1, late).astype(BF16) for part in first_sums]
    half_sent = late[half_rows - first_tiles * tile :]
    half_sent, *head_parts = together(half_sent, *head_parts)
    half_other = swap(half_sent, "pipe", 1)
    received_parts = exchange_blocks(head_parts, "dp")
    scaled[0] = after(scaled[0], *head_parts)
    early = block(
        go,
        lambda lows, scaled: table_gradient_of(lows, scaled, 0, first_tiles, tile),
        lows,
        scaled,
    )
    half_kept = jnp.concatenate([early, late[: half_rows - first_tiles * tile]], 0)
    head_parts = [received_parts[0]] + [after(part, early) for part in received_parts[1:]]
    grad_final_rows = sum(part.astype(F32) for part in head_parts)
    grad_final_rows = grad_final_rows - own_weight[:, None] * target_rows
    gradient, final_gain_part, final_bias_part = final_pull(grad_final_rows)
    grad_final = jnp.stack([final_gain_part, final_bias_part])

    weighted = own_weight[:, None] * final_low.astype(F32)
    before_first = lax.ppermute(
        weighted[-1:].astype(BF16), "seq", [(k, k + 1) for k in range(lanes - 1)]
    )
    target_part = jnp.concatenate([before_first.astype(F32), weighted[:-1]], 0)

    scattered = [[], []]
    grad_gains = [None, None]
    for layer in (1, 0):
        kept_attn, kept_feed = saved[layer]
        gains = gain_stack[layer]
        gradient, feed_parts, gains_feed = block(
            go, backward_feed, gradient, kept_feed, w_fc[layer], w_proj[layer], gains
        )
        if layer == 1:
            gradient, half_other, *feed_parts = together(gradient, half_other, *feed_parts)
            scattered[1].extend(scatter_over(part, ("dp", "pipe")) for part in feed_parts)
            half_sum = (
                half_kept.astype(F32) + half_other.astype(F32)
            ).astype(BF16)
            gradient, *half_parts = together(gradient, *take_columns(half_sum, replica, replicas))
            half_parts = exchange_blocks(half_parts, "dp")
        else:
            gradient, scattered[1][1], feed_parts, half_parts = together(
                gradient, scattered[1][1], feed_parts, half_parts
            )
            scattered[0].extend(scatter_over(part, "dp") for part in feed_parts)
            half_back = jnp.stack(half_parts)
            gradient, half_back = together(gradient, half_back)
            half_far = swap(half_back, "pipe", 1)
        gradient, attn_part, gains_attn = block(
            go, backward_attention, gradient, kept_attn, w_attn[layer], gains, places
        )
        scattered[layer].append(scatter_over(attn_part, "dp"))
        if layer == 1:
            gradient, scattered[1][0] = together(gradient, scattered[1][0])
        else:
            gradient, scattered[1][2] = together(gradient, scattered[1][2])
        grad_gains[layer] = jnp.concatenate([gains_attn, gains_feed], 0)
    sent_rows = jnp.concatenate(
        [(gradient - target_part).astype(BF16), gradient.astype(BF16)], 0
    )
    back = exchange_blocks(take_columns(sent_rows, replica, replicas), "dp")
    position_part = sum(part[shard_rows:].astype(F32) for part in back)
    position_grad = position_part + swap(position_part, "pipe", 1)
    back = jnp.concatenate([part[:shard_rows] for part in back], 0)
    back, half_far, scattered[0][0] = together(back, half_far, scattered[0][0])
    back_other = swap(back, "pipe", 1)
    back_other, scattered[0][1] = together(back_other, scattered[0][1])
    back_both = jnp.where(
        section == 0,
        jnp.concatenate([back, back_other], 0),
        jnp.concatenate([back_other, back], 0),
    )
    back_rows = spread(back_both)
    table_grad, table_square = scatter_rows(
        back_listing, back_count, half_back, half_far, back_rows, slice_rows
    )

    sent = [parts[0] for parts in zip(*scattered)]
    sent[2] = jnp.where(section == 0, scattered[1][2], scattered[0][2])
    feed_halves = [swap(half, "pipe", 1) for half in scattered[1][:2]]
    received = [swap(part, "pipe", 1) for part in sent]
    feed_grads = [
        jnp.where(
            section == 0,
            scattered[0][k].astype(F32) + received[k].astype(F32),
            jnp.concatenate([feed_halves[k], scattered[1][k]], 0).astype(F32),
        )
        for k in range(2)
    ]
    fc_part, proj_part = feed_grads
    attn_part = jnp.where(section == 0, scattered[0][2], scattered[1][2]).astype(
        F32
    ) + received[2].astype(F32)
    qkv_grad = attn_part[:, :qkv_columns].reshape(attn_qkv.shape)
    out_grad = attn_part[:, qkv_columns:].T[None]
    fc_grad = fc_part[None]
    proj_grad = proj_part.T[None]

    norm_grad_all = jnp.concatenate([grad_gains[0], grad_gains[1], grad_final], 0)
    squares = (
        jnp.sum(qkv_grad * qkv_grad)
        + jnp.sum(out_grad * out_grad)
        + jnp.sum(fc_grad * fc_grad)
        + jnp.sum(proj_grad * proj_grad)
        + (jnp.sum(table_square) + jnp.sum(position_grad * position_grad)) / sections
    )
    sums = jnp.stack([squares, jnp.sum(own_loss), jnp.sum(own_penalty), jnp.sum(own_weight)])
    sums = jnp.pad(sums, (0, width - sums.shape[0]))[None]
    summed = sum_everywhere(jnp.concatenate([norm_grad_all, sums], 0))
    norm_grad_all, sums = summed[:-1], summed[-1]
    norm_grad_mine = lax.dynamic_slice_in_dim(
        norm_grad_all, own_place * norm_columns, norm_columns, 1
    )
    gradients = (
        qkv_grad,
        out_grad,
        fc_grad,
        proj_grad,
        table_grad,
        position_grad,
        norm_grad_mine[:-2].reshape(norm_params.shape),
        norm_grad_mine[-2:],
    )
    squares = sums[0] + jnp.sum(norm_grad_all * norm_grad_all)
    loss_sum, penalty_sum, token_count = sums[1], sums[2], sums[3]
    grad_norm = jnp.sqrt(squares) / token_count
    clip_factor = jnp.minimum(1.0, CLIP / (grad_norm + 1e-06))
    step_scale = clip_factor / token_count
    masters = (
        attn_qkv,
        attn_out,
        mlp_in,
        mlp_out,
        embed_table,
        position_table,
        norm_params,
        final_norm,
    )
    moments = (
        (attn_qkv_first, attn_qkv_second),
        (attn_out_first, attn_out_second),
        (mlp_in_first, mlp_in_second),
        (mlp_out_first, mlp_out_second),
        (embed_table_first, embed_table_second),
        (position_table_first, position_table_second),
        (norm_params_first, norm_params_second),
        (final_norm_first, final_norm_second),
    )
    results = []
    for index in range(8):
        results.extend(
            adamw_update(
                masters[index],
                moments[index][0],
                moments[index][1],
                gradients[index] * step_scale,
                RATES[index],
                DECAYS[index],
            )
        )
    loss_parts = jnp.stack([loss_sum, token_count])
    return (loss_parts, penalty_sum, grad_norm, *results)


def solution(mesh):
    row_spec = P("dp", None)
    qkv_spec = P("pipe", "dp", None, "seq")
    into_spec = P("pipe", "dp", "seq")
    out_spec = P("pipe", "seq", "dp")
    table_spec = P("seq", "dp")
    norm_spec = P(None, None, ("pipe", "dp", "seq"))
    final_spec = P(None, ("pipe", "dp", "seq"))
    kinds = (
        qkv_spec,
        out_spec,
        into_spec,
        out_spec,
        table_spec,
        table_spec,
        norm_spec,
        final_spec,
    )
    triples = tuple(spec for spec in kinds for _ in range(3))
    return jax.shard_map(
        per_device,
        mesh=mesh,
        in_specs=(row_spec, row_spec, row_spec) + triples,
        out_specs=(P(), P(), P()) + triples,
        check_vma=False,
    )
```

time: 1660 us -> 1330 us (0.80)
  matrix products: 353 us -> 96.7 us
  Pallas kernels: 0 us -> 202 us
  waiting for transfers between devices: 741 us -> 541 us
  other arithmetic: 253 us -> 206 us
  blocking collectives: 39.5 us -> 0 us
  starting transfers between devices: 97.3 us -> 127 us
    dot_general x46 -> x24, matrix products: 331 us -> 96.7 us  [the longest x2 15.9 us: backward_feed(): grad_active = jnp.dot(grad_z, w_proj, preferred_element_type=F32)]
    ppermute x98 -> x108, waiting for transfers between devices: 640 us -> 421 us  [swap(): return lax.ppermute(block, axis, route)]
    pallas_call x0 -> x11, Pallas kernels: none -> 202 us  [the longest x4 84 us: head_block(): pl.pallas_call(head_kernel, grid=(length // tile,), in_specs=[pl.BlockSpe...]
    all_gather x6 -> x3, waiting for transfers between devices: 97.5 us -> 8.14 us  [per_device(): lax.all_gather(by_rows(shard.astype(BF16)), 'dp', axis=0, tiled=True)]
    scatter-add x1 -> x0, other arithmetic: 58.9 us -> none  [per_device(): grad_table.at[jnp.clip(back_wanted, 0, slice_rows - 1)]]
    reduce_scatter x0 -> x4, waiting for transfers between devices: none -> 54.6 us  [scatter_over(): return lax.psum_scatter(part, axes, scatter_dimension=0, tiled=True)]
    unnamed x18 -> x11, waiting for transfers between devices: 4.01 us -> 57.4 us
    all_gather x1 -> x0, blocking collectives: 39.5 us -> none  [per_device(): lax.all_gather(norm_mine, ('pipe', 'dp', 'seq'), axis=1, tiled=True)]
  transfers between devices with their start and end apart: 111 -> 119, of which waited for: 62 -> 63; matrix products, arithmetic and copies ran while one was open for 28% -> 23% of each run, Pallas kernels for 0% -> 12%
where the time goes in v2:
time: 1330 us; the launch traced here: 1320 us
  waiting for transfers between devices  541 us (41%)
  other arithmetic  206 us (15%)
  Pallas kernels  202 us (15%)
  starting transfers between devices  127 us (10%)
  local copies, waits for them, and re-layouts  122 us (9%)
  matrix products  96.7 us (7%)
  between operations  23.6 us (2%)
    ppermute x108, waiting for transfers between devices, swap(): return lax.ppermute(block, axis, route)  421 us
    ppermute x108, starting transfers between devices, swap(): return lax.ppermute(block, axis, route)  123 us
    pallas_call x4, Pallas kernels, head_block(): pl.pallas_call(head_kernel, grid=(length // tile,), in_specs=[pl.BlockSpe...  84 us
    unnamed x11, waiting for transfers between devices  57.4 us
    reduce_scatter x4, waiting for transfers between devices, scatter_over(): return lax.psum_scatter(part, axes, scatter_dimension=0, tiled=True)  54.6 us
    sub x8, other arithmetic, adamw_update(): return (master - rate * (ratio + decay * master), first_new, second_new)  46.4 us
    pallas_call x2, Pallas kernels, table_gradient_of(): pl.pallas_call(lambda *refs: table_kernel(count, *refs), grid=(count_tile...  41.7 us
    pallas_call x2, Pallas kernels, attend_backward(): pl.pallas_call(attend_back_kernel, grid=(steps,), in_specs=[pl.BlockSpec(...  34.3 us
  transfers between devices with their start and end apart: 119, of which 63 were waited for; matrix products, arithmetic and copies ran while one was open for 23% of the time, Pallas kernels for 12%

profile of v2, /device:TPU:0, one launch (start us, length us, event | category | flops | bytes accessed | tf_op | source)
XLA Modules:
  0.0 1320.5 jit_solution(12406438942208597091)
XLA Ops:
  30.7 20.8 %gather_fusion.1 = bf16[4096,256]{1,0:T(8,128)(2,1)} fusion(f32[12576,256]{1,0:T(8,128)} %param.83, s32[4096]{0:T(1024)S(1)} %broadcast_clamp_fusion), kind=kCustom, calls=%fused_computation.9 | custom fusion | bytes 4210688 | tf_op jit(solution)/shard_map/jit(_take)/gather | solution.py:626
  136.7 57.2 %conditional.14 = (f32[256,1024]{1,0:T(8,128)S(1)}, f32[256,1024]{1,0:T(8,128)S(1)}, bf16[1024,1024]{1,0:T(8,128)(2,1)}, bf16[1024,1024]{1,0:T(8,128)(2,1)}, f32...) conditional(s32[]{:T(128)} %convert_element_type.356, () %tuple.198, (f32[256,1024]{1,0:T(8,128)S(1)}, ...), branch_computations={%region_2.3_spmd, %region_3.6_spmd} | conditional | flops 3771728128 | bytes 59311344 | solution.py:326
  208.6 32.7 %collective-permute-done.51 = bf16[1024,1024]{1,0:T(8,128)(2,1)} collective-permute-done((bf16[1024,1024]{1,0:T(8,128)(2,1)}, bf16[1024,1024]{1,0:T(8,128)(2,1)}, u32[]{:S(2)}, u32[]{:S(2)}) %collective-permute-start.51) | collective-permute-done | bytes 2097184 | tf_op jit(solution)/shard_map/ppermute | solution.py:27
  245.1 46.2 %conditional.15 = (f32[256,1024]{1,0:T(8,128)S(1)}, f32[256,1024]{1,0:T(8,128)S(1)}, bf16[1024,1024]{1,0:T(8,128)(2,1)}, f32[1024,1024]{1,0:T(8,128)}, bf16[1024,1024]{1,0:T(8,128)(2,1)}) conditional(s32[]{:T(128)} %convert_element_type.356, () %tuple.197, (f32[256,1024]{1,0:T(8,128)S(1)}, f32[4,1024]{1,0:T(4,128)S(1)}, ...), branch_computations={%region_6.7_spmd, %region_7.10_spmd} | conditional | flops 4316987392 | bytes 70288648 | solution.py:326
  302.1 50.5 %conditional.16 = (f32[256,1024]{1,0:T(8,128)S(1)}, f32[256,1024]{1,0:T(8,128)S(1)}, bf16[1024,1024]{1,0:T(8,128)(2,1)}, bf16[1024,1024]{1,0:T(8,128)(2,1)}, f32...) conditional(s32[]{:T(128)} %convert_element_type.356, () %tuple.196, (f32[256,1024]{1,0:T(8,128)S(1)}, ...), branch_computations={%region_10.11_spmd, %region_11.14_spmd} | conditional | flops 3771728128 | bytes 73991464 | solution.py:326
  353.5 49.5 %conditional.17 = (f32[256,1024]{0,1:T(8,128)S(1)}, bf16[1024,1024]{0,1:T(8,128)(2,1)}, f32[1024,1024]{1,0:T(8,128)}, bf16[1024,1024]{1,0:T(8,128)(2,1)}, f32[256,1]{0,1:T(1,128)S(1)}, /*index=5*/f32[256,1024]{1,0:T(8,128)S(1)}) conditional(s32[]{:T(128)} %convert_element_type.356, () %tuple.195, (f32[256,1024]{1,0:T(8,128)S(1)}, ...), branch_computations={%region_14.15_spmd, %region_15.19_spmd} | conditional | flops 4317249536 | bytes 82872648 | solution.py:326
  439.5 19.2 %collective-permute-done.61 = bf16[256,1024]{1,0:T(8,128)(2,1)} collective-permute-done((bf16[256,1024]{1,0:T(8,128)(2,1)S(1)}, bf16[256,1024]{1,0:T(8,128)(2,1)}, u32[]{:S(2)}, u32[]{:S(2)}) %collective-permute-start.61) | collective-permute-done | bytes 524320 | tf_op jit(solution)/shard_map/ppermute | solution.py:27
  467.3 23.0 %conditional.18 = (bf16[1024,3200]{1,0:T(8,128)(2,1)}, f32[1024,1024]{1,0:T(8,128)}, f32[1,1024]{1,0:T(1,128)}, f32[1,4,256]{2,0,1:T(1,128)S(1)}, f32[1,1,4,256]...) conditional(s32[]{:T(128)} %convert_element_type.356, () %tuple.194, ...), branch_computations={%region_20.21_spmd, %region_21.22_spmd} | conditional | flops 13421772800 | bytes 19423288 | solution.py:326
  467.3 20.9 %branch_1_fun.17 = (bf16[1024,3200]{1,0:T(8,128)(2,1)}, f32[1024,1024]{1,0:T(8,128)}, f32[1,1024]{1,0:T(1,128)}, f32[1,1024]{1,0:T(1,128)}) custom-call(bf16[1024,1024]{1,0:T(8,128)(2,1)S(1)} %get-tuple-element.353.rows_ref, bf16[3200,1024]{1,0:T(8,128)(2,1)} %get-tuple-element.354.table_ref, f32[1,3200]{1,0:T(1,128)S(1)} %get-tuple-element.355.bias_ref), custom_call_target="tpu_custom_call" | custom-call | flops 13421772800 | bytes 19398656 | tf_op jit(solution)/shard_map/cond/branch_1_fun/pallas_call | solution.py:383
  495.5 23.0 %conditional.19 = (bf16[1024,3200]{1,0:T(8,128)(2,1)}, f32[1024,1024]{1,0:T(8,128)}, f32[1,1024]{1,0:T(1,128)}, f32[1,4,256]{2,0,1:T(1,128)S(1)}, f32[1,1,4,256]...) conditional(s32[]{:T(128)} %convert_element_type.356, () %tuple.208, ...), branch_computations={%region_22.23_spmd, %region_23.24_spmd} | conditional | flops 13421772800 | bytes 19423288 | solution.py:326
  495.6 21.0 %branch_1_fun.18 = (bf16[1024,3200]{1,0:T(8,128)(2,1)}, f32[1024,1024]{1,0:T(8,128)}, f32[1,1024]{1,0:T(1,128)}, f32[1,1024]{1,0:T(1,128)}) custom-call(bf16[1024,1024]{1,0:T(8,128)(2,1)S(1)} %get-tuple-element.360.rows_ref, bf16[3200,1024]{1,0:T(8,128)(2,1)} %get-tuple-element.361.table_ref, f32[1,3200]{1,0:T(1,128)S(1)} %get-tuple-element.362.bias_ref), custom_call_target="tpu_custom_call" | custom-call | flops 13421772800 | bytes 19398656 | tf_op jit(solution)/shard_map/cond/branch_1_fun/pallas_call | solution.py:383
  523.1 22.6 %conditional.20 = (bf16[1024,3200]{1,0:T(8,128)(2,1)}, f32[1024,1024]{1,0:T(8,128)}, f32[1,4,256]{2,0,1:T(1,128)}, f32[1,1,4,256]{3,1,2,0:T(1,128)S(1)}, f32[1,1...) conditional(s32[]{:T(128)} %convert_element_type.356, () %tuple.211, (bf16[1024,1024]{1,0:T(8,128)(2,1)S(1)}, ...), branch_computations={%region_24.25_spmd, %region_25.26_spmd} | conditional | flops 13421772800 | bytes 19415088 | solution.py:326
  523.1 21.2 %branch_1_fun.19 = (bf16[1024,3200]{1,0:T(8,128)(2,1)}, f32[1024,1024]{1,0:T(8,128)}, f32[1,1024]{1,0:T(1,128)}, f32[1,1024]{1,0:T(1,128)}) custom-call(bf16[1024,1024]{1,0:T(8,128)(2,1)S(1)} %get-tuple-element.367.rows_ref, bf16[3200,1024]{1,0:T(8,128)(2,1)} %get-tuple-element.368.table_ref, f32[1,3200]{1,0:T(1,128)S(1)} %get-tuple-element.369.bias_ref), custom_call_target="tpu_custom_call" | custom-call | flops 13421772800 | bytes 19398656 | tf_op jit(solution)/shard_map/cond/branch_1_fun/pallas_call | solution.py:383
  547.4 22.3 %conditional.21 = (bf16[1024,3200]{1,0:T(8,128)(2,1)}, f32[1024,1024]{1,0:T(8,128)}, f32[1,4,256]{2,0,1:T(1,128)}, f32[1,1,4,256]{3,1,2,0:T(1,128)S(1)}, f32[1,1...) conditional(s32[]{:T(128)} %convert_element_type.356, () %tuple.215, (bf16[1024,1024]{1,0:T(8,128)(2,1)S(1)}, ...), branch_computations={%region_26.27_spmd, %region_27.28_spmd} | conditional | flops 13421772800 | bytes 19415088 | solution.py:326
  547.4 20.9 %branch_1_fun.20 = (bf16[1024,3200]{1,0:T(8,128)(2,1)}, f32[1024,1024]{1,0:T(8,128)}, f32[1,1024]{1,0:T(1,128)}, f32[1,1024]{1,0:T(1,128)}) custom-call(bf16[1024,1024]{1,0:T(8,128)(2,1)S(1)} %get-tuple-element.374.rows_ref, bf16[3200,1024]{1,0:T(8,128)(2,1)} %get-tuple-element.375.table_ref, f32[1,3200]{1,0:T(1,128)S(1)} %get-tuple-element.376.bias_ref), custom_call_target="tpu_custom_call" | custom-call | flops 13421772800 | bytes 19398656 | tf_op jit(solution)/shard_map/cond/branch_1_fun/pallas_call | solution.py:383
  621.2 23.3 %conditional.22 = (bf16[1920,1024]{1,0:T(8,128)(2,1)}) conditional(s32[]{:T(128)} %convert_element_type.356, () %tuple.193, (bf16[1024,3200]{1,0:T(8,128)(2,1)}, bf16[1024,3200]{1,0:T(8,128)(2,1)}, bf16[1024,3200]{1,0:T(8,128)(2,1)}, bf16[1024,3200]{1,0:T(8,128)(2,1)}, bf16[1024,1024]{1,0:T(8,128)(2,1)}, /*index=5*/bf16[1024,1024]{1,0:T(8,128)(2,1)}, ...), branch_computations={%region_28.31_spmd, %region_29.32_spmd} | conditional | flops 16106127360 | bytes 28049416 | solution.py:326
  621.2 23.3 %branch_1_fun.21 = bf16[1920,1024]{1,0:T(8,128)(2,1)} custom-call(bf16[1024,3200]{1,0:T(8,128)(2,1)} %get-tuple-element.381.refs_0_, bf16[1024,3200]{1,0:T(8,128)(2,1)} %get-tuple-element.382.refs_1_, bf16[1024,3200]{1,0:T(8,128)(2,1)} %get-tuple-element.383.refs_2_, bf16[1024,3200]{1,0:T(8,128)(2,1)} %get-tuple-element.384.refs_3_, ...), custom_call_target="tpu_custom_call" | custom-call | flops 16106127360 | bytes 28049408 | tf_op jit(solution)/shard_map/cond/branch_1_fun/pallas_call | solution.py:427
  667.1 18.4 %conditional.23 = (bf16[1280,1024]{1,0:T(8,128)(2,1)}) conditional(s32[]{:T(128)} %convert_element_type.356, () %tuple.229, (bf16[1024,3200]{1,0:T(8,128)(2,1)}, bf16[1024,3200]{1,0:T(8,128)(2,1)}, bf16[1024,3200]{1,0:T(8,128)(2,1)}, bf16[1024,3200]{1,0:T(8,128)(2,1)}, bf16[1024,1024]{1,0:T(8,128)(2,1)}, /*index=5*/bf16[1024,1024]{1,0:T(8,128)(2,1)}, ...), branch_computations={%region_30.33_spmd, %region_31.34_spmd} | conditional | flops 10737418240 | bytes 21495816 | solution.py:326
  667.1 18.4 %branch_1_fun.22 = bf16[1280,1024]{1,0:T(8,128)(2,1)} custom-call(bf16[1024,3200]{1,0:T(8,128)(2,1)} %get-tuple-element.389.refs_0_, bf16[1024,3200]{1,0:T(8,128)(2,1)} %get-tuple-element.390.refs_1_, bf16[1024,3200]{1,0:T(8,128)(2,1)} %get-tuple-element.391.refs_2_, bf16[1024,3200]{1,0:T(8,128)(2,1)} %get-tuple-element.392.refs_3_, ...), custom_call_target="tpu_custom_call" | custom-call | flops 10737418240 | bytes 21495808 | tf_op jit(solution)/shard_map/cond/branch_1_fun/pallas_call | solution.py:427
  702.1 50.5 %conditional.24 = (f32[256,1024]{1,0:T(8,128)S(1)}, bf16[1024,1024]{0,1:T(8,128)(2,1)}, bf16[1024,1024]{1,0:T(8,128)(2,1)}, f32[2,1024]{1,0:T(2,128)S(1)}) conditional(s32[]{:T(128)} %convert_element_type.356, () %tuple.192, (f32[256,1024]{1,0:T(8,128)S(1)}, f32[256,1024]{1,0:T(8,128)S(1)}, f32[256]{0:T(256)S(1)}, f32[256,1024]{1,0:T(8,128)S(1)}, ...), branch_computations={%region_32.35_spmd, %region_33.44_spmd} | conditional | flops 8638433280 | bytes 152644096 | solution.py:326
  764.4 62.5 %conditional.25 = (f32[256,1024]{1,0:T(8,128)}, bf16[1024,1024]{0,1:T(8,128)(2,1)}, f32[2,1024]{1,0:T(2,128)S(1)}) conditional(s32[]{:T(128)} %convert_element_type.356, () %tuple.191, (f32[256,1024]{1,0:T(8,128)S(1)}, bf16[1024,1024]{1,0:T(8,128)(2,1)}, s32[4,256]{1,0:T(4,128)S(1)}, s32[4,256]{1,0:T(4,128)S(1)}, bf16[1024,1024]{1,0:T(8,128)(2,1)}, ...), branch_computations={%region_42.45_spmd, %region_43.52_spmd} | conditional | flops 7544243712 | bytes 127496704 | solution.py:326
  782.9 16.3 %branch_1_fun.23 = bf16[1024,1024]{1,0:T(8,128)(2,1)S(1)} custom-call(bf16[1024,1024]{1,0:T(8,128)(2,1)S(1)} %copy-done.55, bf16[1024,256]{1,0:T(8,128)(2,1)S(1)} %convolution_convert_fusion.5.grad_ref, f32[2,4,1,512]{3,2,1,0:T(1,128)S(1)} %get-tuple-element.413.log_ref, s32[1,1024]{1,0:T(1,128)S(1)} %bitcast.399, s32[1,1024]{1,0:T(1,128)S(1)} %bitcast.401, ...), custom_call_target="tpu_custom_call" | custom-call | flops 2684354560 | bytes 4194304 | tf_op jit(solution)/shard_map/cond/branch_1_fun/pallas_call | solution.py:234
  843.2 51.0 %conditional.26 = (f32[256,1024]{1,0:T(8,128)S(1)}, bf16[1024,1024]{0,1:T(8,128)(2,1)}, bf16[1024,1024]{1,0:T(8,128)(2,1)}, f32[2,1024]{1,0:T(2,128)S(1)}) conditional(s32[]{:T(128)} %convert_element_type.356, () %tuple.190, (f32[256,1024]{1,0:T(8,128)}, bf16[1024,1024]{1,0:T(8,128)(2,1)}, f32[1024,1024]{1,0:T(8,128)}, ...), branch_computations={%region_51.54_spmd, %region_52.61_spmd} | conditional | flops 8635549696 | bytes 76083424 | solution.py:326
  894.3 56.7 %reduce-scatter.21.cloned.1.call-done = bf16[128,1024]{1,0:T(8,128)(2,1)} async-done(((bf16[1024,1024]{1,0:T(8,128)(2,1)}), bf16[128,1024]{1,0:T(8,128)(2,1)}) %reduce-scatter.21.cloned.1.call-update) | async-done | bytes 262160
  961.9 64.7 %conditional.27 = (f32[256,1024]{1,0:T(8,128)}, bf16[1024,1024]{0,1:T(8,128)(2,1)}, f32[2,1024]{1,0:T(2,128)S(1)}) conditional(s32[]{:T(128)} %convert_element_type.356, () %tuple.189, (f32[256,1024]{1,0:T(8,128)S(1)}, bf16[1024,1024]{1,0:T(8,128)(2,1)}, s32[4,256]{1,0:T(4,128)S(1)}, s32[4,256]{1,0:T(4,128)S(1)}, bf16[1024,1024]{1,0:T(8,128)(2,1)}, ...), branch_computations={%region_60.63_spmd, %region_61.70_spmd} | conditional | flops 7544243712 | bytes 110719424 | solution.py:326
  980.9 18.0 %branch_1_fun.24 = bf16[1024,1024]{1,0:T(8,128)(2,1)S(1)} custom-call(bf16[1024,1024]{1,0:T(8,128)(2,1)} %get-tuple-element.428.packed_ref, bf16[1024,256]{1,0:T(8,128)(2,1)S(1)} %convolution_convert_fusion.9.grad_ref, f32[2,4,1,512]{3,2,1,0:T(1,128)S(1)} %get-tuple-element.431.log_ref, s32[1,1024]{1,0:T(1,128)S(1)} %bitcast.403, s32[1,1024]{1,0:T(1,128)S(1)} %bitcast.405, ...), custom_call_target="tpu_custom_call" | custom-call | flops 2684354560 | bytes 4194304 | tf_op jit(solution)/shard_map/cond/branch_1_fun/pallas_call | solution.py:234
  1036.6 14.5 %collective-permute-done.91 = bf16[512,256]{1,0:T(8,128)(2,1)S(1)} collective-permute-done((bf16[512,256]{1,0:T(8,128)(2,1)S(1)}, bf16[512,256]{1,0:T(8,128)(2,1)S(1)}, u32[]{:S(2)}, u32[]{:S(2)}) %collective-permute-start.91) | collective-permute-done | bytes 262176 | tf_op jit(solution)/shard_map/ppermute | solution.py:27
  1060.6 34.1 %reduce-scatter.17.cloned.1.call-done = bf16[256,1024]{0,1:T(8,128)(2,1)} async-done(((bf16[1024,1024]{0,1:T(8,128)(2,1)}), bf16[256,1024]{0,1:T(8,128)(2,1)}) %reduce-scatter.17.cloned.1.call-update) | async-done | bytes 524304 | tf_op jit(solution)/shard_map/reduce_scatter | solution.py:506
  1096.5 23.1 %collective-permute-done.100 = bf16[2048,256]{1,0:T(8,128)(2,1)S(1)} collective-permute-done((bf16[2048,256]{1,0:T(8,128)(2,1)S(1)}, bf16[2048,256]{1,0:T(8,128)(2,1)S(1)}, u32[]{:S(2)}, u32[]{:S(2)}) %collective-permute-start.100) | collective-permute-done | bytes 1048608 | tf_op jit(solution)/shard_map/ppermute | solution.py:27
  1122.8 20.4 %reduce-scatter.11.cloned.1.call-done = bf16[256,1024]{0,1:T(8,128)(2,1)} async-done(((bf16[1024,1024]{0,1:T(8,128)(2,1)}), bf16[256,1024]{0,1:T(8,128)(2,1)}) %reduce-scatter.11.cloned.1.call-update) | async-done | bytes 524304 | tf_op jit(solution)/shard_map/reduce_scatter | solution.py:506
  1197.8 21.4 %shard_map.529 = (f32[12576,256]{1,0:T(8,128)}, f32[1,256]{1,0:T(1,128)}) custom-call(s32[1]{0:T(128)} %bitcast.30.count_ref, s32[8192]{0:T(1024)} %get-tuple-element.714.list_ref, bf16[4,1600,256]{2,1,0:T(8,128)(2,1)} %pad_maximum_fusion.36.near_ref, bf16[4,1600,256]{2,1,0:T(8,128)(2,1)} %collective-permute-done.94.far_ref, ...), custom_call_target="tpu_custom_call" | custom-call | flops 12877824 | bytes 29949952 | tf_op jit(solution)/shard_map/pallas_call | solution.py:487
  1274.3 31.7 %multiply_subtract_fusion = (f32[12576,256]{1,0:T(8,128)}, f32[12576,256]{1,0:T(8,128)}, f32[12576,256]{1,0:T(8,128)}) fusion(f32[12576,256]{1,0:T(8,128)} %param.83, f32[12576,256]{1,0:T(8,128)} %get-tuple-element.718, f32[]{:T(128)S(6)} %div.278, f32[12576,256]{1,0:T(8,128)} %param.84, f32[12576,256]{1,0:T(8,128)} %param.85), kind=kLoop, calls=%fused_computation.208 | loop fusion | flops 51511296 | bytes 90144768 | tf_op jit(solution)/shard_map/sub | solution.py:533
  (883 shorter events, 860.9 us)
Async XLA Ops:
  7.2 75.2 %all-gather.4.cloned.1.call-start = ((), (), s32[]{:S(2)}) async-start(), calls=%async_computation.6 | async-start | bytes 2621440 | tf_op jit(solution)/shard_map/all_gather | solution.py:614
  9.9 120.9 %all-gather.8.cloned.1.call-start = ((), (), s32[]{:S(2)}) async-start(), calls=%async_computation.8 | async-start | bytes 2621440 | tf_op jit(solution)/shard_map/all_gather | solution.py:614
  10.9 183.1 %all-gather.6.cloned.1.call-start = ((), (), s32[]{:S(2)}) async-start(), calls=%async_computation.7 | async-start | bytes 2621440 | tf_op jit(solution)/shard_map/all_gather | solution.py:614
  18.6 69.1 %collective-permute-start.40 = (bf16[256,256]{1,0:T(8,128)(2,1)}, bf16[256,256]{1,0:T(8,128)(2,1)}, u32[]{:S(2)}, u32[]{:S(2)}) collective-permute-start(bf16[256,256]{1,0:T(8,128)(2,1)} %get-tuple-element.1154), channel_id=1, source_target_pairs={{0,4},{4,0},{8,12},{12,8},{1,5},{5,1},{9,13},{13,9},{2,6},{6,2},{1... | collective-permute-start | bytes 393224 | tf_op jit(solution)/shard_map/ppermute | solution.py:27
  20.6 821.5 %reduce-scatter.19.cloned.1.call-start = ((), (), s32[]{:S(2)}) async-start(), calls=%async_computation.13 | async-start | bytes 2359296
  25.4 74.6 %collective-permute-start.41 = (bf16[256,256]{1,0:T(8,128)(2,1)}, bf16[256,256]{1,0:T(8,128)(2,1)}, u32[]{:S(2)}, u32[]{:S(2)}) collective-permute-start(bf16[256,256]{1,0:T(8,128)(2,1)} %get-tuple-element.1154), channel_id=1, source_target_pairs={{0,8},{4,12},{8,0},{12,4},{1,9},{5,13},{9,1},{13,5},{2,10},{6,14},... | collective-permute-start | bytes 393224 | tf_op jit(solution)/shard_map/ppermute | solution.py:27
  28.9 74.9 %collective-permute-start.42 = (bf16[256,256]{1,0:T(8,128)(2,1)}, bf16[256,256]{1,0:T(8,128)(2,1)}, u32[]{:S(2)}, u32[]{:S(2)}) collective-permute-start(bf16[256,256]{1,0:T(8,128)(2,1)} %get-tuple-element.1154), channel_id=1, source_target_pairs={{0,12},{4,8},{8,4},{12,0},{1,13},{5,9},{9,5},{13,1},{2,14},{6,10},... | collective-permute-start | bytes 393224 | tf_op jit(solution)/shard_map/ppermute | solution.py:27
  82.4 49.8 %collective-permute-start.49 = (bf16[1024,1024]{1,0:T(8,128)(2,1)}, bf16[1024,1024]{1,0:T(8,128)(2,1)}, u32[]{:S(2)}, u32[]{:S(2)}) collective-permute-start(bf16[1024,1024]{1,0:T(8,128)(2,1)} %all-gather.4.cloned.1.call-done), channel_id=1, source_target_pairs={{0,16},{16,0},{1,17},{17,1},{2,18},{18,2},{3,19},{19,3},{4,20},{20... | collective-permute-start | bytes 6291464 | tf_op jit(solution)/shard_map/ppermute | solution.py:27
  130.8 73.8 %collective-permute-start.50 = (bf16[1024,1024]{1,0:T(8,128)(2,1)}, bf16[1024,1024]{1,0:T(8,128)(2,1)}, u32[]{:S(2)}, u32[]{:S(2)}) collective-permute-start(bf16[1024,1024]{1,0:T(8,128)(2,1)} %all-gather.8.cloned.1.call-done), channel_id=1, source_target_pairs={{0,16},{16,0},{1,17},{17,1},{2,18},{18,2},{3,19},{19,3},{4,20},{20... | collective-permute-start | bytes 6291464 | tf_op jit(solution)/shard_map/ppermute | solution.py:27
  194.0 47.3 %collective-permute-start.51 = (bf16[1024,1024]{1,0:T(8,128)(2,1)}, bf16[1024,1024]{1,0:T(8,128)(2,1)}, u32[]{:S(2)}, u32[]{:S(2)}) collective-permute-start(bf16[1024,1024]{1,0:T(8,128)(2,1)} %all-gather.6.cloned.1.call-done), channel_id=1, source_target_pairs={{0,16},{16,0},{1,17},{17,1},{2,18},{18,2},{3,19},{19,3},{4,20},{20... | collective-permute-start | bytes 6291464 | tf_op jit(solution)/shard_map/ppermute | solution.py:27
  200.2 91.2 %collective-permute-start.52 = (bf16[1600,256]{1,0:T(8,128)(2,1)}, bf16[1600,256]{1,0:T(8,128)(2,1)}, u32[]{:S(2)}, u32[]{:S(2)}) collective-permute-start(bf16[1600,256]{1,0:T(8,128)(2,1)} %get-tuple-element.1169), channel_id=1, source_target_pairs={{0,4},{4,0},{8,12},{12,8},{1,5},{5,1},{9,13},{13,9},{2,6},{6,2},{1... | collective-permute-start | bytes 2457608 | tf_op jit(solution)/shard_map/ppermute | solution.py:27
  200.2 91.2 %collective-permute-start.53 = (bf16[1600,256]{1,0:T(8,128)(2,1)}, bf16[1600,256]{1,0:T(8,128)(2,1)}, u32[]{:S(2)}, u32[]{:S(2)}) collective-permute-start(bf16[1600,256]{1,0:T(8,128)(2,1)} %get-tuple-element.1168), channel_id=1, source_target_pairs={{0,8},{4,12},{8,0},{12,4},{1,9},{5,13},{9,1},{13,5},{2,10},{6,14},... | collective-permute-start | bytes 2457608 | tf_op jit(solution)/shard_map/ppermute | solution.py:27
  202.2 89.2 %collective-permute-start.54 = (bf16[1600,256]{1,0:T(8,128)(2,1)}, bf16[1600,256]{1,0:T(8,128)(2,1)}, u32[]{:S(2)}, u32[]{:S(2)}) collective-permute-start(bf16[1600,256]{1,0:T(8,128)(2,1)} %get-tuple-element.1167), channel_id=1, source_target_pairs={{0,12},{4,8},{8,4},{12,0},{1,13},{5,9},{9,5},{13,1},{2,14},{6,10},... | collective-permute-start | bytes 2457608 | tf_op jit(solution)/shard_map/ppermute | solution.py:27
  300.7 160.1 %collective-permute-start.57 = (bf16[1600,1024]{1,0:T(8,128)(2,1)}, bf16[1600,1024]{1,0:T(8,128)(2,1)}, u32[]{:S(2)}, u32[]{:S(2)}) collective-permute-start(bf16[1600,1024]{1,0:T(8,128)(2,1)} %constant_dynamic-update-slice_fusion.15), channel_id=1, source_target_pairs={{0,16},{16,0},{1,17},{17,1},{2,18},{18,2},{3,19},{19,3},{4,20},{20... | collective-permute-start | bytes 9830408 | tf_op jit(solution)/shard_map/ppermute | solution.py:27
  421.0 38.5 %collective-permute-start.56 = (bf16[512,1024]{1,0:T(8,128)(2,1)}, bf16[512,1024]{1,0:T(8,128)(2,1)}, u32[]{:S(2)}, u32[]{:S(2)}) collective-permute-start(bf16[512,1024]{1,0:T(8,128)(2,1)} %pad_maximum_fusion.42), channel_id=1, source_target_pairs={{0,1},{1,0},{2,3},{3,2},{4,5},{5,4},{6,7},{7,6},{8,9},{9,8},{10,11... | collective-permute-start | bytes 3145736 | tf_op jit(solution)/shard_map/ppermute | solution.py:27
  437.9 53.7 %collective-permute-start.60 = (bf16[512,1024]{1,0:T(8,128)(2,1)}, bf16[512,1024]{1,0:T(8,128)(2,1)}, u32[]{:S(2)}, u32[]{:S(2)}) collective-permute-start(bf16[512,1024]{1,0:T(8,128)(2,1)} %pad_maximum_fusion.43), channel_id=1, source_target_pairs={{0,1},{1,0},{2,3},{3,2},{4,5},{5,4},{6,7},{7,6},{8,9},{9,8},{10,11... | collective-permute-start | bytes 3145736 | tf_op jit(solution)/shard_map/ppermute | solution.py:27
  438.0 52.3 %collective-permute-start.64 = (bf16[256,1024]{1,0:T(8,128)(2,1)S(1)}, bf16[256,1024]{1,0:T(8,128)(2,1)}, u32[]{:S(2)}, u32[]{:S(2)}) collective-permute-start(bf16[256,1024]{1,0:T(8,128)(2,1)S(1)} %get-tuple-element.1141), channel_id=1, source_target_pairs={{0,12},{4,8},{8,4},{12,0},{1,13},{5,9},{9,5},{13,1},{2,14},{6,10},... | collective-permute-start | bytes 1572872 | tf_op jit(solution)/shard_map/ppermute | solution.py:27
  609.7 39.1 %collective-permute-start.80 = (bf16[256,1024]{1,0:T(8,128)(2,1)S(1)}, bf16[256,1024]{1,0:T(8,128)(2,1)}, u32[]{:S(2)}, u32[]{:S(2)}) collective-permute-start(bf16[256,1024]{1,0:T(8,128)(2,1)S(1)} %slice.811), channel_id=1, source_target_pairs={{0,2},{1,3},{2,0},{3,1},{4,6},{5,7},{6,4},{7,5},{8,10},{9,11},{10,... | collective-permute-start | bytes 1572872 | tf_op jit(solution)/shard_map/ppermute | solution.py:27
  620.4 37.1 %collective-permute-start.77 = (bf16[256,1024]{1,0:T(8,128)(2,1)}, bf16[256,1024]{1,0:T(8,128)(2,1)}, u32[]{:S(2)}, u32[]{:S(2)}) collective-permute-start(bf16[256,1024]{1,0:T(8,128)(2,1)} %slice.814), channel_id=1, source_target_pairs={{0,2},{1,3},{2,0},{3,1},{4,6},{5,7},{6,4},{7,5},{8,10},{9,11},{10,... | collective-permute-start | bytes 1572872 | tf_op jit(solution)/shard_map/ppermute | solution.py:27
  659.5 93.1 %collective-permute-start.85 = (bf16[1600,1024]{1,0:T(8,128)(2,1)}, bf16[1600,1024]{1,0:T(8,128)(2,1)}, u32[]{:S(2)}, u32[]{:S(2)}) collective-permute-start(bf16[1600,1024]{1,0:T(8,128)(2,1)} %slice.579), channel_id=1, source_target_pairs={{0,16},{16,0},{1,17},{17,1},{2,18},{18,2},{3,19},{19,3},{4,20},{20... | collective-permute-start | bytes 9830408 | tf_op jit(solution)/shard_map/ppermute | solution.py:27
  661.2 38.5 %collective-permute-start.82 = (bf16[256,1024]{1,0:T(8,128)(2,1)}, bf16[256,1024]{1,0:T(8,128)(2,1)}, u32[]{:S(2)}, u32[]{:S(2)}) collective-permute-start(bf16[256,1024]{1,0:T(8,128)(2,1)} %fusion.74), channel_id=1, source_target_pairs={{0,8},{4,12},{8,0},{12,4},{1,9},{5,13},{9,1},{13,5},{2,10},{6,14},... | collective-permute-start | bytes 1572872 | tf_op jit(solution)/shard_map/ppermute | solution.py:27
  757.0 194.0 %reduce-scatter.21.cloned.1.call-start = ((), (), s32[]{:S(2)}) async-start(), calls=%async_computation.14 | async-start | bytes 2359296
  757.6 272.5 %reduce-scatter.13.cloned.1.call-start = ((), (), s32[]{:S(2)}) async-start(), calls=%async_computation.10 | async-start | bytes 2621440 | tf_op jit(solution)/shard_map/reduce_scatter | solution.py:506
  826.9 232.1 %reduce-scatter.15.cloned.1.call-start = ((), (), s32[]{:S(2)}) async-start(), calls=%async_computation.11 | async-start | bytes 2621440 | tf_op jit(solution)/shard_map/reduce_scatter | solution.py:506
  826.9 125.8 %collective-permute-start.86 = (bf16[1600,256]{1,0:T(8,128)(2,1)}, bf16[1600,256]{1,0:T(8,128)(2,1)}, u32[]{:S(2)}, u32[]{:S(2)}) collective-permute-start(bf16[1600,256]{1,0:T(8,128)(2,1)} %get-tuple-element.682), channel_id=1, source_target_pairs={{0,4},{4,0},{8,12},{12,8},{1,5},{5,1},{9,13},{13,9},{2,6},{6,2},{1... | collective-permute-start | bytes 2457608 | tf_op jit(solution)/shard_map/ppermute | solution.py:27
  839.6 113.1 %collective-permute-start.87 = (bf16[1600,256]{1,0:T(8,128)(2,1)}, bf16[1600,256]{1,0:T(8,128)(2,1)}, u32[]{:S(2)}, u32[]{:S(2)}) collective-permute-start(bf16[1600,256]{1,0:T(8,128)(2,1)} %get-tuple-element.683), channel_id=1, source_target_pairs={{0,8},{4,12},{8,0},{12,4},{1,9},{5,13},{9,1},{13,5},{2,10},{6,14},... | collective-permute-start | bytes 2457608 | tf_op jit(solution)/shard_map/ppermute | solution.py:27
  839.6 113.1 %collective-permute-start.88 = (bf16[1600,256]{1,0:T(8,128)(2,1)}, bf16[1600,256]{1,0:T(8,128)(2,1)}, u32[]{:S(2)}, u32[]{:S(2)}) collective-permute-start(bf16[1600,256]{1,0:T(8,128)(2,1)} %get-tuple-element.684), channel_id=1, source_target_pairs={{0,12},{4,8},{8,4},{12,0},{1,13},{5,9},{9,5},{13,1},{2,14},{6,10},... | collective-permute-start | bytes 2457608 | tf_op jit(solution)/shard_map/ppermute | solution.py:27
  952.8 141.9 %reduce-scatter.17.cloned.1.call-start = ((), (), s32[]{:S(2)}) async-start(), calls=%async_computation.12 | async-start | bytes 2621440 | tf_op jit(solution)/shard_map/reduce_scatter | solution.py:506
  956.8 186.5 %reduce-scatter.11.cloned.1.call-start = ((), (), s32[]{:S(2)}) async-start(), calls=%async_computation.9 | async-start | bytes 2621440 | tf_op jit(solution)/shard_map/reduce_scatter | solution.py:506
  961.4 97.6 %collective-permute-start.94 = (bf16[4,1600,256]{2,1,0:T(8,128)(2,1)}, bf16[4,1600,256]{2,1,0:T(8,128)(2,1)}, u32[]{:S(2)}, u32[]{:S(2)}) collective-permute-start(bf16[4,1600,256]{2,1,0:T(8,128)(2,1)} %pad_maximum_fusion.36.near_ref), channel_id=1, source_target_pairs={{0,16},{16,0},{1,17},{17,1},{2,18},{18,2},{3,19},{19,3},{4,20},{20... | collective-permute-start | bytes 9830408 | tf_op jit(solution)/shard_map/ppermute | solution.py:27
  1121.1 73.3 %collective-permute-start.101 = (bf16[4096,256]{1,0:T(8,128)(2,1)}, bf16[4096,256]{1,0:T(8,128)(2,1)}, u32[]{:S(2)}, u32[]{:S(2)}) collective-permute-start(bf16[4096,256]{1,0:T(8,128)(2,1)} %pad_maximum_fusion.41), channel_id=1, source_target_pairs={{0,1},{1,0},{2,3},{3,2},{4,5},{5,4},{6,7},{7,6},{8,9},{9,8},{10,11... | collective-permute-start | bytes 6291464 | tf_op jit(solution)/shard_map/ppermute | solution.py:27
  1147.2 36.8 %collective-permute-start.99 = (bf16[128,1024]{0,1:T(8,128)(2,1)}, bf16[128,1024]{0,1:T(8,128)(2,1)}, u32[]{:S(2)}, u32[]{:S(2)}) collective-permute-start(bf16[128,1024]{0,1:T(8,128)(2,1)} %copy.398), channel_id=1, source_target_pairs={{0,16},{16,0},{1,17},{17,1},{2,18},{18,2},{3,19},{19,3},{4,20},{20... | collective-permute-start | bytes 786440 | tf_op jit(solution)/shard_map/ppermute | solution.py:27
  (205 other events, 2860.7 us)
Sparse Core Ops, SparseCore 0:
  10.2 62.4 all-gather.3
  74.9 55.8 all-gather.7
  132.9 44.6 all-gather.5
  757.1 76.5 reduce-scatter.18
  837.7 113.2 reduce-scatter.20
  953.7 42.8 reduce-scatter.12
  999.0 49.0 reduce-scatter.14
  1050.3 44.2 reduce-scatter.16
  1097.7 45.5 reduce-scatter.10

commit v3 on v2

--- a/solution.py
+++ b/solution.py
@@ -45,23 +45,35 @@
     return result
 
 
-def spread(block, held=()):
-    for step, mask in enumerate(masks_down(lax.axis_size("seq"))):
+def spread(block, steps=None, held=()):
+    for mask in masks_down(lax.axis_size("seq"))[:steps]:
         received = swap(block, "seq", mask)
         if held:
-            received = after(received, *held[step])
+            received = after(received, *held)
         block = jnp.concatenate([block, received], 0)
     return block
 
 
-def collect(block, steps=0, skip=0, held=None):
-    masks = masks_down(lax.axis_size("seq"))[::-1]
-    for mask in masks[skip : steps or len(masks)]:
+def collect(block):
+    for mask in reversed(masks_down(lax.axis_size("seq"))):
         half = block.shape[0] // 2
         sent = swap(block[half:].astype(BF16), "seq", mask)
-        if held is not None:
-            sent = after(sent, held)
         block = block[:half].astype(F32) + sent.astype(F32)
+    return block
+
+
+def collect_scaled(block, scale):
+    half = block.shape[0] // 2
+    mask = masks_down(lax.axis_size("seq"))[-1]
+    sent = swap((block[half:].astype(F32) * scale[half:, None]).astype(BF16), "seq", mask)
+    return block[:half].astype(F32) * scale[:half, None] + sent.astype(F32)
+
+
+def collect_rest(block, held):
+    for mask in reversed(masks_down(lax.axis_size("seq"))[:-1]):
+        half = block.shape[0] // 2
+        sent = after(swap(block[half:].astype(BF16), "seq", mask), held)
+        block = block[:half] + sent.astype(F32)
     return block
 
 
@@ -361,10 +373,11 @@
     return jnp.broadcast_to(column, (column.shape[0], 128)).T[:1]
 
 
-def head_kernel(rows_ref, table_ref, bias_ref, low_ref, mixed_ref, top_ref, sum_ref):
+def head_kernel(first_ref, second_ref, table_ref, bias_ref, low_ref, mixed_ref, top_ref, sum_ref):
     table = table_ref[...]
+    rows = jnp.where(pl.program_id(0) == 0, first_ref[...], second_ref[...])
     logits = lax.dot_general(
-        rows_ref[...], table, (((1,), (1,)), ((), ())), preferred_element_type=F32
+        rows, table, (((1,), (1,)), ((), ())), preferred_element_type=F32
     )
     logits = logits + bias_ref[...]
     row_top = jnp.max(logits, 1, keepdims=True)
@@ -376,15 +389,16 @@
     mixed_ref[...] = jnp.dot(low, table, preferred_element_type=F32).astype(mixed_ref.dtype)
 
 
-def head_block(rows, table, bias):
-    length, width = rows.shape
+def head_block(first, second, table, bias):
+    tile, width = first.shape
+    length = 2 * tile
     part_rows = table.shape[0]
-    tile = min(512, length)
     return pl.pallas_call(
         head_kernel,
         grid=(length // tile,),
         in_specs=[
-            pl.BlockSpec((tile, width), lambda t: (t, 0)),
+            pl.BlockSpec((tile, width), lambda t: (0, 0), pipeline_mode=pl.Buffered(1)),
+            pl.BlockSpec((tile, width), lambda t: (0, 0), pipeline_mode=pl.Buffered(1)),
             pl.BlockSpec((part_rows, width), lambda t: (0, 0), pipeline_mode=pl.Buffered(1)),
             pl.BlockSpec((1, part_rows), lambda t: (0, 0), pipeline_mode=pl.Buffered(1)),
         ],
@@ -396,7 +410,7 @@
         ],
         out_shape=[
             jax.ShapeDtypeStruct((length, part_rows), BF16),
-            jax.ShapeDtypeStruct((length, width), F32),
+            jax.ShapeDtypeStruct((length, width), BF16),
             jax.ShapeDtypeStruct((1, length), F32),
             jax.ShapeDtypeStruct((1, length), F32),
         ],
@@ -406,15 +420,19 @@
             bytes_accessed=2 * part_rows * (width + length) + 6 * length * width,
             transcendentals=length * part_rows,
         ),
-    )(rows, table, bias)
+    )(first, second, table, bias)
 
 
 def table_kernel(count, *refs):
-    low_refs, row_refs, out_ref = refs[:count], refs[count : 2 * count], refs[2 * count]
+    low_refs, row_refs, out_ref = refs[:count], refs[count : 3 * count], refs[3 * count]
+    half = row_refs[0].shape[0]
     total = None
-    for low_ref, row_ref in zip(low_refs, row_refs):
+    for k, row_ref in enumerate(row_refs):
         product = lax.dot_general(
-            low_ref[...], row_ref[...], (((0,), (0,)), ((), ())), preferred_element_type=F32
+            low_refs[k // 2][k % 2 * half : (k % 2 + 1) * half, :],
+            row_ref[...],
+            (((0,), (0,)), ((), ())),
+            preferred_element_type=F32,
         )
         total = product if total is None else total + product
     out_ref[...] = total.astype(out_ref.dtype)
@@ -423,12 +441,13 @@
 def table_gradient_of(lows, rows, first, count_tiles, tile):
     count = len(lows)
     length, part_rows = lows[0].shape
-    width = rows[0].shape[1]
+    half, width = rows[0].shape
     return pl.pallas_call(
         lambda *refs: table_kernel(count, *refs),
         grid=(count_tiles,),
         in_specs=[pl.BlockSpec((length, tile), lambda v: (0, v + first))] * count
-        + [pl.BlockSpec((length, width), lambda v: (0, 0), pipeline_mode=pl.Buffered(1))] * count,
+        + [pl.BlockSpec((half, width), lambda v: (0, 0), pipeline_mode=pl.Buffered(1))]
+        * (2 * count),
         out_specs=pl.BlockSpec((tile, width), lambda v: (v, 0)),
         out_shape=jax.ShapeDtypeStruct((count_tiles * tile, width), BF16),
         compiler_params=pltpu.CompilerParams(vmem_limit_bytes=60 * 1024 * 1024),
@@ -446,7 +465,9 @@
     return jnp.minimum(wanted, slice_rows - part_rows // 2), wanted
 
 
-def scatter_kernel(count_ref, list_ref, near_ref, far_ref, rows_ref, out_ref, square_ref, wide):
+def scatter_kernel(
+    count_ref, list_ref, near_ref, far_ref, own_ref, other_ref, out_ref, square_ref, wide
+):
     slice_rows = out_ref.shape[0]
     shift = (slice_rows - 1).bit_length()
     replicas, half_rows = near_ref.shape[:2]
@@ -456,7 +477,11 @@
         for half, part in ((section, near_ref), (1 - section, far_ref)):
             start, _ = part_place(replica ^ m, half, 2 * half_rows, slice_rows)
             out_ref[pl.ds(pl.multiple_of(start, 8), half_rows), :] += part[m].astype(F32)
-    wide[...] = rows_ref[...].astype(F32)
+    count_rows = own_ref.shape[0]
+    wide[pl.ds(pl.multiple_of(section * count_rows, 8), count_rows), :] = own_ref[...].astype(F32)
+    wide[pl.ds(pl.multiple_of((1 - section) * count_rows, 8), count_rows), :] = other_ref[
+        ...
+    ].astype(F32)
 
     def add_one(k):
         coded = list_ref[k]
@@ -480,26 +505,26 @@
     square_ref[...] = jnp.sum(result * result, 0, keepdims=True)
 
 
-def scatter_rows(listing, count, near, far, rows, slice_rows):
+def scatter_rows(listing, count, near, far, own, other, slice_rows):
     columns = near.shape[2]
     whole = pl.BlockSpec(memory_space=pltpu.VMEM)
     scalars = pl.BlockSpec(memory_space=pltpu.SMEM)
     return pl.pallas_call(
         scatter_kernel,
-        in_specs=[scalars, scalars, whole, whole, whole],
+        in_specs=[scalars, scalars, whole, whole, whole, whole],
         out_specs=[whole, whole],
         out_shape=[
             jax.ShapeDtypeStruct((slice_rows, columns), F32),
             jax.ShapeDtypeStruct((1, columns), F32),
         ],
-        scratch_shapes=[pltpu.VMEM(rows.shape, F32)],
+        scratch_shapes=[pltpu.VMEM((2 * own.shape[0], columns), F32)],
         compiler_params=pltpu.CompilerParams(vmem_limit_bytes=60 * 1024 * 1024),
         cost_estimate=pl.CostEstimate(
             flops=4 * slice_rows * columns,
-            bytes_accessed=8 * slice_rows * columns + 2 * rows.size,
+            bytes_accessed=8 * slice_rows * columns + 4 * own.size,
             transcendentals=0,
         ),
-    )(count, listing, near, far, rows)
+    )(count, listing, near, far, own, other)
 
 
 def scatter_over(part, axes):
@@ -577,16 +602,9 @@
 
     norm_mine = jnp.concatenate([norm_params.reshape(-1, norm_params.shape[2]), final_norm], 0)
     norm_columns = norm_mine.shape[1]
-    norm_all = norm_mine[None]
-    for axis in ("seq", "dp", "pipe"):
-        for mask in reversed(masks_down(lax.axis_size(axis))):
-            norm_all = jnp.concatenate([norm_all, swap(norm_all, axis, mask)], 0)
+    norm_all = from_all(from_all(from_all(norm_mine, "pipe"), "dp"), "seq")
+    norm_all = jnp.transpose(norm_all, (2, 1, 0, 3, 4)).reshape(-1, *norm_mine.shape)
     own_place = (section * replicas + replica) * lanes + lane
-    norm_all = jnp.take(norm_all, own_place ^ jnp.arange(norm_all.shape[0]), axis=0)
-    norm_all = jnp.transpose(norm_all, (1, 0, 2)).reshape(norm_mine.shape[0], width)
-    gain_stack = norm_all[:-2].reshape(norm_params.shape[0], 4, width)
-    final_rows = norm_all[-2:]
-
     own_ids = lax.dynamic_index_in_dim(token_ids, section, 0, keepdims=False)
     own_valid = lax.dynamic_index_in_dim(valid, section, 0, keepdims=False)
     row_segments = lax.dynamic_index_in_dim(segments, section, 0, keepdims=False)
@@ -610,23 +628,36 @@
         mlp_in[0],
         mlp_out[0].T,
     ]
-    gathered = [
-        lax.all_gather(by_rows(shard.astype(BF16)), "dp", axis=0, tiled=True) for shard in shards
-    ]
-
-    def two_layers(mine):
-        other = swap(mine, "pipe", 1)
-        return jnp.where(section == 0, mine, other), jnp.where(section == 0, other, mine)
-
-    w_attn, w_fc = two_layers(gathered[0]), two_layers(gathered[1])
+    shards = [by_rows(shard.astype(BF16)) for shard in shards]
+
+    def both_layers(mine, other=None):
+        if other is None:
+            other = swap(mine, "pipe", 1)
+        return [jnp.where(section == 0, mine, other), jnp.where(section == 0, other, mine)]
+
+    def over_dp(shard):
+        return lax.all_gather(shard, "dp", axis=0, tiled=True)
+
+    attn_mine, fc_mine = over_dp(shards[0]), over_dp(shards[1])
+    proj_shards = both_layers(shards[2])
 
     vocab_start = lane * slice_rows
     wanted = jnp.transpose(ids_lane, (1, 0, 2)).reshape(-1) - vocab_start
     inside = (wanted >= 0) & (wanted < slice_rows)
     picked = jnp.take(embed_table, jnp.clip(wanted, 0, slice_rows - 1), axis=0)
     picked = jnp.where(inside[:, None], picked, 0.0).astype(BF16)
+    picked, norm_all, proj_shards, attn_mine = together(
+        picked, norm_all, proj_shards, attn_mine
+    )
+    attn_other = swap(attn_mine, "pipe", 1)
+    w_proj = [over_dp(shard) for shard in proj_shards]
     picked = collect(picked).astype(BF16).reshape(replicas, shard_rows, slice_columns)
-    embed_rows = place_columns(exchange_blocks(list(picked), "dp"), replica)
+    norm_all = jnp.transpose(norm_all, (1, 0, 2)).reshape(norm_mine.shape[0], width)
+    gain_stack = norm_all[:-2].reshape(norm_params.shape[0], 4, width)
+    final_rows = norm_all[-2:]
+    embed_blocks, attn_other = together(exchange_blocks(list(picked), "dp"), attn_other)
+    w_attn = both_layers(attn_mine, attn_other)
+    embed_rows = place_columns(embed_blocks, replica)
     position_low = position_table.astype(BF16)
     position_rows = place_columns(
         exchange_blocks([position_low] * replicas, "dp"), replica
@@ -641,7 +672,8 @@
         jnp.concatenate([ids_all, coded_other // 2], 0),
         jnp.concatenate([coded_other // 2, ids_all], 0),
     )
-    back_wanted = jnp.transpose(by_lane(ids_both), (1, 0, 2)).reshape(-1) - vocab_start
+    back_wanted = by_lane(ids_both).reshape(sections, replicas, lanes, shard_rows)
+    back_wanted = jnp.transpose(back_wanted, (0, 2, 1, 3)).reshape(-1) - vocab_start
     back_inside = (back_wanted >= 0) & (back_wanted < slice_rows)
     back_number = jnp.arange(back_wanted.shape[0])
     back_coded = back_number * (1 << (slice_rows - 1).bit_length()) + back_wanted
@@ -649,17 +681,9 @@
     back_count = jnp.sum(back_inside.astype(jnp.int32))[None]
     start_rows, back_listing, back_count = together(start_rows, back_listing, back_count)
 
-    table_f32 = after(embed_table, start_rows)
-    table_parts = [
-        lax.dynamic_slice_in_dim(
-            table_f32,
-            part_place(replica ^ m, section, part_rows, slice_rows)[0],
-            half_rows,
-            0,
-        ).astype(BF16)
-        for m in range(replicas)
-    ]
-    table_blocks = exchange_blocks(table_parts, "dp")
+    start_rows, fc_mine = together(start_rows, fc_mine)
+    w_fc = both_layers(fc_mine)
+
     bias_halves = []
     for half in (section, 1 - section):
         start, wanted = part_place(replica, half, part_rows, slice_rows)
@@ -675,24 +699,44 @@
         gains = gain_stack[layer]
         rows, kept_attn = block(go, forward_attention, rows, w_attn[layer], gains, places)
         if layer == 0:
-            rows, gathered[2] = together(rows, gathered[2])
-            w_proj = two_layers(gathered[2])
-        rows, kept_feed = block(go, forward_feed, rows, w_fc[layer], w_proj[layer], gains)
-        saved.append((kept_attn, kept_feed))
-        if layer == 0:
+            table_f32 = after(embed_table, rows)
+            table_parts = [
+                lax.dynamic_slice_in_dim(
+                    table_f32,
+                    part_place(replica ^ m, section, part_rows, slice_rows)[0],
+                    half_rows,
+                    0,
+                ).astype(BF16)
+                for m in range(replicas)
+            ]
+            rows, *table_parts = together(rows, *table_parts)
+            table_blocks = exchange_blocks(table_parts, "dp")
+        else:
+            rows, w_proj[1] = together(rows, w_proj[1])
             rows, *table_blocks = together(rows, *table_blocks)
             table_half = place_columns(table_blocks, replica)
             table_other = swap(table_half, "pipe", 1)
+        rows, kept_feed = block(go, forward_feed, rows, w_fc[layer], w_proj[layer], gains)
+        saved.append((kept_attn, kept_feed))
     table = jnp.concatenate([table_half, table_other], 0)
     final_value, final_pull = jax.vjp(norm_rows, rows, final_rows[0], final_rows[1])
     final_low = final_value.astype(BF16)
 
+    parts = exchange_blocks([final_low] * replicas, "dp")
+    steps = len(masks_down(lanes)) - 1
     full, heads = [], []
-    steps = len(masks_down(lanes))
-    for m, part in enumerate(exchange_blocks([final_low] * replicas, "dp")):
-        held = [[heads[m - back][2]] if m >= back else [] for back in range(steps + 1, 0, -1)]
-        full.append(spread(after(part, *held[0]), held[1:]))
-        heads.append(block(go, head_block, full[m], table, table_bias))
+    half = spread(parts[0], steps)
+
+    def head_step(half, table, bias, *coming):
+        other = swap(half, "seq", 1)
+        outputs = head_block(half, other, table, bias)
+        return (half, other), outputs, [spread(part, steps, (outputs[2],)) for part in coming]
+
+    for m in range(replicas):
+        rows, head, coming = block(go, head_step, half, table, table_bias, *parts[m + 1 : m + 2])
+        full.append(rows)
+        heads.append(head)
+        half = coming[0] if coming else None
     stat_shape = (replicas, lanes, shard_rows)
     row_top = jnp.stack([head[2] for head in heads]).reshape(stat_shape)
     row_sum = jnp.stack([head[3] for head in heads]).reshape(stat_shape)
@@ -704,14 +748,21 @@
     own_loss = own_weight * (own_log - target_logit) + own_penalty
 
     scale_flat = scale.reshape(replicas, length)
-    weighted_parts = [scale_flat[m][:, None] * heads[m][1] for m in range(replicas)]
-    first_sums = [collect(part, 1) for part in weighted_parts]
+    first_sums = [collect_scaled(heads[m][1], scale_flat[m]) for m in range(replicas)]
     tile = max(t for t in range(128, 641, 128) if part_rows % t == 0)
     first_tiles = half_rows // tile
     lows = [head[0] for head in heads]
+    half_length = length // 2
     scaled = [
-        after((scale_flat[m][:, None] * full[m].astype(F32)).astype(BF16), *first_sums)
+        after(
+            (
+                scale_flat[m][k * half_length : (k + 1) * half_length, None]
+                * full[m][k].astype(F32)
+            ).astype(BF16),
+            *first_sums,
+        )
         for m in range(replicas)
+        for k in range(2)
     ]
     late_tiles = part_rows // tile - first_tiles
     late = block(
@@ -720,7 +771,7 @@
         lows,
         scaled,
     )
-    head_parts = [collect(part, 0, 1, late).astype(BF16) for part in first_sums]
+    head_parts = [collect_rest(part, late).astype(BF16) for part in first_sums]
     half_sent = late[half_rows - first_tiles * tile :]
     half_sent, *head_parts = together(half_sent, *head_parts)
     half_other = swap(half_sent, "pipe", 1)
@@ -745,39 +796,68 @@
     )
     target_part = jnp.concatenate([before_first.astype(F32), weighted[:-1]], 0)
 
-    scattered = [[], []]
     grad_gains = [None, None]
-    for layer in (1, 0):
-        kept_attn, kept_feed = saved[layer]
-        gains = gain_stack[layer]
-        gradient, feed_parts, gains_feed = block(
-            go, backward_feed, gradient, kept_feed, w_fc[layer], w_proj[layer], gains
-        )
-        if layer == 1:
-            gradient, half_other, *feed_parts = together(gradient, half_other, *feed_parts)
-            scattered[1].extend(scatter_over(part, ("dp", "pipe")) for part in feed_parts)
-            half_sum = (
-                half_kept.astype(F32) + half_other.astype(F32)
-            ).astype(BF16)
-            gradient, *half_parts = together(gradient, *take_columns(half_sum, replica, replicas))
-            half_parts = exchange_blocks(half_parts, "dp")
-        else:
-            gradient, scattered[1][1], feed_parts, half_parts = together(
-                gradient, scattered[1][1], feed_parts, half_parts
-            )
-            scattered[0].extend(scatter_over(part, "dp") for part in feed_parts)
-            half_back = jnp.stack(half_parts)
-            gradient, half_back = together(gradient, half_back)
-            half_far = swap(half_back, "pipe", 1)
-        gradient, attn_part, gains_attn = block(
-            go, backward_attention, gradient, kept_attn, w_attn[layer], gains, places
-        )
-        scattered[layer].append(scatter_over(attn_part, "dp"))
-        if layer == 1:
-            gradient, scattered[1][0] = together(gradient, scattered[1][0])
-        else:
-            gradient, scattered[1][2] = together(gradient, scattered[1][2])
-        grad_gains[layer] = jnp.concatenate([gains_attn, gains_feed], 0)
+    moving = [list(range(1, replicas))[: replicas // 2], list(range(1, replicas))[replicas // 2 :]]
+    arrived = {}
+
+    def send_some(value, stage):
+        value, *sent = together(value, *[half_parts[m] for m in moving[stage]])
+        return value, {m: swap(part, "dp", m) for m, part in zip(moving[stage], sent)}
+
+    def column_half(matrix, half):
+        columns = matrix.shape[1] // 2
+        return lax.dynamic_slice_in_dim(matrix, half * columns, columns, 1)
+
+    def send_halves(value, matrices):
+        value, *sent = together(value, *[column_half(part, 1 - section) for part in matrices])
+        return value, [swap(part, "pipe", 1) for part in sent]
+
+    def sum_halves(value, matrices, coming):
+        sums = [
+            (column_half(part, section).astype(F32) + other.astype(F32)).astype(BF16)
+            for part, other in zip(matrices, coming)
+        ]
+        return together(value, *sums)
+
+    gradient, feed_late, gains_feed = block(
+        go, backward_feed, gradient, saved[1][1], w_fc[1], w_proj[1], gain_stack[1]
+    )
+    gradient, half_other, *feed_late = together(gradient, half_other, *feed_late)
+    half_sum = (half_kept.astype(F32) + half_other.astype(F32)).astype(BF16)
+    half_parts = take_columns(half_sum, replica, replicas)
+    gradient, flight = send_some(gradient, 0)
+    gradient, coming = send_halves(gradient, feed_late)
+    gradient, attn_late, gains_attn = block(
+        go, backward_attention, gradient, saved[1][0], w_attn[1], gain_stack[1], places
+    )
+    grad_gains[1] = jnp.concatenate([gains_attn, gains_feed], 0)
+    gradient, flight, coming, attn_late = together(gradient, flight, coming, attn_late)
+    arrived.update(flight)
+    gradient, flight = send_some(gradient, 1)
+    gradient, *sums = sum_halves(gradient, feed_late, coming)
+    feed_late = [scatter_over(part, "dp") for part in sums]
+    gradient, attn_coming = send_halves(gradient, [attn_late])
+    gradient, feed_early, gains_feed = block(
+        go, backward_feed, gradient, saved[0][1], w_fc[0], w_proj[0], gain_stack[0]
+    )
+    gradient, flight, attn_coming, *feed_early = together(
+        gradient, flight, attn_coming, *feed_early
+    )
+    arrived.update(flight)
+    half_back = jnp.stack([half_parts[0]] + [arrived[m] for m in range(1, replicas)])
+    gradient, half_back = together(gradient, half_back)
+    half_far = swap(half_back, "pipe", 1)
+    feed_early = [scatter_over(part, "dp") for part in feed_early]
+    gradient, attn_late = sum_halves(gradient, [attn_late], attn_coming)
+    attn_late = scatter_over(attn_late, "dp")
+    gradient, feed_late = together(gradient, feed_late)
+    gradient, attn_early, gains_attn = block(
+        go, backward_attention, gradient, saved[0][0], w_attn[0], gain_stack[0], places
+    )
+    grad_gains[0] = jnp.concatenate([gains_attn, gains_feed], 0)
+    gradient, attn_coming = send_halves(gradient, [attn_early])
+    late_halves = [swap(part, "pipe", 1) for part in feed_late]
+
     sent_rows = jnp.concatenate(
         [(gradient - target_part).astype(BF16), gradient.astype(BF16)], 0
     )
@@ -785,35 +865,37 @@
     position_part = sum(part[shard_rows:].astype(F32) for part in back)
     position_grad = position_part + swap(position_part, "pipe", 1)
     back = jnp.concatenate([part[:shard_rows] for part in back], 0)
-    back, half_far, scattered[0][0] = together(back, half_far, scattered[0][0])
+    back, attn_coming, half_far, feed_early[0] = together(
+        back, attn_coming, half_far, feed_early[0]
+    )
+    back, attn_early = sum_halves(back, [attn_early], attn_coming)
+    attn_early = scatter_over(attn_early, "dp")
     back_other = swap(back, "pipe", 1)
-    back_other, scattered[0][1] = together(back_other, scattered[0][1])
-    back_both = jnp.where(
+    own_rows = spread(back)
+    back_other, feed_early[1] = together(back_other, feed_early[1])
+    other_rows = spread(back_other)
+    table_grad, table_square = scatter_rows(
+        back_listing, back_count, half_back, half_far, own_rows, other_rows, slice_rows
+    )
+
+    feed_coming = [swap(part, "pipe", 1) for part in feed_early]
+    attn_late, attn_early, *feed_coming = together(
+        attn_late, attn_early, *feed_coming, table_square
+    )[:-1]
+    attn_coming = swap(jnp.where(section == 0, attn_late, attn_early), "pipe", 1)
+    attn_part = jnp.where(
         section == 0,
-        jnp.concatenate([back, back_other], 0),
-        jnp.concatenate([back_other, back], 0),
-    )
-    back_rows = spread(back_both)
-    table_grad, table_square = scatter_rows(
-        back_listing, back_count, half_back, half_far, back_rows, slice_rows
-    )
-
-    sent = [parts[0] for parts in zip(*scattered)]
-    sent[2] = jnp.where(section == 0, scattered[1][2], scattered[0][2])
-    feed_halves = [swap(half, "pipe", 1) for half in scattered[1][:2]]
-    received = [swap(part, "pipe", 1) for part in sent]
-    feed_grads = [
+        jnp.concatenate([attn_early, attn_coming], 1),
+        jnp.concatenate([attn_coming, attn_late], 1),
+    ).astype(F32)
+    fc_part, proj_part = (
         jnp.where(
             section == 0,
-            scattered[0][k].astype(F32) + received[k].astype(F32),
-            jnp.concatenate([feed_halves[k], scattered[1][k]], 0).astype(F32),
+            feed_early[k].astype(F32) + feed_coming[k].astype(F32),
+            jnp.concatenate([late_halves[k], feed_late[k]], 1).astype(F32),
         )
         for k in range(2)
-    ]
-    fc_part, proj_part = feed_grads
-    attn_part = jnp.where(section == 0, scattered[0][2], scattered[1][2]).astype(
-        F32
-    ) + received[2].astype(F32)
+    )
     qkv_grad = attn_part[:, :qkv_columns].reshape(attn_qkv.shape)
     out_grad = attn_part[:, qkv_columns:].T[None]
     fc_grad = fc_part[None]

time: 1330 us -> 1170 us (0.88)
  waiting for transfers between devices: 541 us -> 344 us
  local copies, waits for them, and re-layouts: 122 us -> 142 us
    ppermute x108 -> x116, waiting for transfers between devices: 421 us -> 326 us  [swap(): return lax.ppermute(block, axis, route)]
    unnamed x11 -> x10, waiting for transfers between devices: 57.4 us -> 0.68 us
    reduce_scatter x4 -> x6, waiting for transfers between devices: 54.6 us -> 8.59 us  [scatter_over(): return lax.psum_scatter(part, axes, scatter_dimension=0, tiled=True)]
    convert_element_type x8 -> x25, other arithmetic: 21.1 us -> 43.5 us  [the longest x7 13.5 us: per_device(): scaled = [after((scale_flat[m][k * half_length:(k + 1) * half_length, Non...]
    ppermute x108 -> x116, starting transfers between devices: 123 us -> 133 us  [swap(): return lax.ppermute(block, axis, route)]
    cond x111 -> x126, local copies, waits for them, and re-layouts: 18.5 us -> 27.2 us
    concatenate x22 -> x20, other arithmetic: 30.9 us -> 23 us  [spread(): block = jnp.concatenate([block, received], 0)]
    unnamed x170 -> x238, local copies, waits for them, and re-layouts: 26 us -> 33.6 us
  transfers between devices with their start and end apart: 119 -> 128, of which waited for: 63 -> 64; matrix products, arithmetic and copies ran while one was open for 23% -> 26% of each run, Pallas kernels for 12% -> 16%
where the time goes in v3:
time: 1170 us; the launch traced here: 1160 us
  waiting for transfers between devices  344 us (29%)
  other arithmetic  208 us (18%)
  Pallas kernels  208 us (18%)
  local copies, waits for them, and re-layouts  142 us (12%)
  starting transfers between devices  136 us (12%)
  matrix products  100 us (9%)
  between operations  24.1 us (2%)
    ppermute x116, waiting for transfers between devices, swap(): return lax.ppermute(block, axis, route)  326 us
    ppermute x116, starting transfers between devices, swap(): return lax.ppermute(block, axis, route)  133 us
    pallas_call x4, Pallas kernels, head_block(): pl.pallas_call(head_kernel, grid=(length // tile,), in_specs=[pl.BlockSpe...  84.9 us
    sub x8, other arithmetic, adamw_update(): return (master - rate * (ratio + decay * master), first_new, second_new)  46.2 us
    pallas_call x2, Pallas kernels, table_gradient_of(): pl.pallas_call(lambda *refs: table_kernel(count, *refs), grid=(count_tile...  41.5 us
    pallas_call x2, Pallas kernels, attend_backward(): pl.pallas_call(attend_back_kernel, grid=(steps,), in_specs=[pl.BlockSpec(...  36.2 us
    unnamed x238, local copies, waits for them, and re-layouts  33.6 us
    cond x126, local copies, waits for them, and re-layouts  27.2 us
  transfers between devices with their start and end apart: 128, of which 64 were waited for; matrix products, arithmetic and copies ran while one was open for 26% of the time, Pallas kernels for 16%

profile of v3, /device:TPU:0, one launch (start us, length us, event | category | flops | bytes accessed | tf_op | source)
XLA Modules:
  0.0 1164.5 jit_solution(3176574206387618594)
XLA Ops:
  32.4 20.6 %gather_fusion.1 = bf16[4096,256]{1,0:T(8,128)(2,1)} fusion(f32[12576,256]{1,0:T(8,128)} %param.83, s32[4096]{0:T(1024)S(1)} %broadcast_clamp_fusion), kind=kCustom, calls=%fused_computation.9 | custom fusion | bytes 4210688 | tf_op jit(solution)/shard_map/jit(_take)/gather | solution.py:647
  131.0 56.2 %conditional.14 = (f32[256,1024]{1,0:T(8,128)S(1)}, f32[256,1024]{1,0:T(8,128)S(1)}, bf16[1024,1024]{1,0:T(8,128)(2,1)}, bf16[1024,1024]{1,0:T(8,128)(2,1)}, f32...) conditional(s32[]{:T(128)} %convert_element_type.465, () %tuple.207, (f32[256,1024]{1,0:T(8,128)S(1)}, ...), branch_computations={%region_2.3_spmd, %region_3.6_spmd} | conditional | flops 3771728128 | bytes 59311372 | solution.py:338
  174.5 12.4 %collective-permute-done.10 = bf16[256,1024]{1,0:T(8,128)(2,1)S(1)} collective-permute-done((bf16[256,1024]{1,0:T(8,128)(2,1)S(1)}, bf16[256,1024]{1,0:T(8,128)(2,1)S(1)}, u32[]{:S(2)}, u32[]{:S(2)}) %collective-permute-start.10) | collective-permute-done | bytes 524320 | tf_op jit(solution)/shard_map/cond/branch_1_fun/ppermute | solution.py:27
  201.6 46.5 %conditional.15 = (f32[256,1024]{1,0:T(8,128)S(1)}, f32[256,1024]{1,0:T(8,128)S(1)}, bf16[1024,1024]{1,0:T(8,128)(2,1)}, f32[1024,1024]{1,0:T(8,128)}, bf16[1024,1024]{1,0:T(8,128)(2,1)}) conditional(s32[]{:T(128)} %convert_element_type.465, () %tuple.206, (f32[256,1024]{1,0:T(8,128)S(1)}, f32[4,1024]{1,0:T(4,128)S(1)}, ...), branch_computations={%region_6.7_spmd, %region_7.10_spmd} | conditional | flops 4316987392 | bytes 70288648 | solution.py:338
  235.4 12.4 %collective-permute-done.14 = bf16[256,1024]{1,0:T(8,128)(2,1)S(1)} collective-permute-done((bf16[256,1024]{1,0:T(8,128)(2,1)S(1)}, bf16[256,1024]{1,0:T(8,128)(2,1)S(1)}, u32[]{:S(2)}, u32[]{:S(2)}) %collective-permute-start.14) | collective-permute-done | bytes 524320 | tf_op jit(solution)/shard_map/cond/branch_1_fun/ppermute | solution.py:27
  249.1 56.8 %conditional.16 = (f32[256,1024]{1,0:T(8,128)S(1)}, f32[256,1024]{1,0:T(8,128)S(1)}, bf16[1024,1024]{1,0:T(8,128)(2,1)}, bf16[1024,1024]{1,0:T(8,128)(2,1)}, f32...) conditional(s32[]{:T(128)} %convert_element_type.465, () %tuple.205, (f32[256,1024]{1,0:T(8,128)S(1)}, ...), branch_computations={%region_10.11_spmd, %region_11.14_spmd} | conditional | flops 3771728128 | bytes 57214192 | solution.py:338
  293.1 12.4 %collective-permute-done.18 = bf16[256,1024]{1,0:T(8,128)(2,1)S(1)} collective-permute-done((bf16[256,1024]{1,0:T(8,128)(2,1)S(1)}, bf16[256,1024]{1,0:T(8,128)(2,1)S(1)}, u32[]{:S(2)}, u32[]{:S(2)}) %collective-permute-start.18) | collective-permute-done | bytes 524320 | tf_op jit(solution)/shard_map/cond/branch_1_fun/ppermute | solution.py:27
  317.8 49.1 %conditional.17 = (f32[256,1024]{0,1:T(8,128)S(1)}, bf16[1024,1024]{0,1:T(8,128)(2,1)}, f32[1024,1024]{1,0:T(8,128)}, bf16[1024,1024]{1,0:T(8,128)(2,1)}, f32[256,1]{0,1:T(1,128)S(1)}, /*index=5*/f32[256,1024]{1,0:T(8,128)S(1)}) conditional(s32[]{:T(128)} %convert_element_type.465, () %tuple.204, (f32[256,1024]{1,0:T(8,128)S(1)}, ...), branch_computations={%region_14.15_spmd, %region_15.19_spmd} | conditional | flops 4317249536 | bytes 82872648 | solution.py:338
  352.9 12.5 %collective-permute-done.22 = bf16[256,1024]{0,1:T(8,128)(2,1)S(1)} collective-permute-done((bf16[256,1024]{0,1:T(8,128)(2,1)S(1)}, bf16[256,1024]{0,1:T(8,128)(2,1)S(1)}, u32[]{:S(2)}, u32[]{:S(2)}) %collective-permute-start.22) | collective-permute-done | bytes 524320 | tf_op jit(solution)/shard_map/cond/branch_1_fun/ppermute | solution.py:27
  395.5 28.8 %conditional.18 = (bf16[1024,3200]{1,0:T(8,128)(2,1)}, bf16[1024,1024]{1,0:T(8,128)(2,1)}, f32[1,1024]{1,0:T(1,128)}, f32[1,1024]{1,0:T(1,128)}, bf16[512,1024]{...) conditional(s32[]{:T(128)} %convert_element_type.465, ...), branch_computations={%region_20.21_spmd, %region_21.22_spmd} | conditional | flops 13424918528 | bytes 46694652 | solution.py:338
  399.3 20.9 %branch_1_fun.12 = (bf16[1024,3200]{1,0:T(8,128)(2,1)}, bf16[1024,1024]{1,0:T(8,128)(2,1)}, f32[1,1024]{1,0:T(1,128)}, f32[1,1024]{1,0:T(1,128)}) custom-call(bf16[512,1024]{1,0:T(8,128)(2,1)} %copy-done.53, bf16[512,1024]{1,0:T(8,128)(2,1)} %copy-done.95, bf16[3200,1024]{1,0:T(8,128)(2,1)} %get-tuple-element.282.table_ref, ...), custom_call_target="tpu_custom_call" | custom-call | flops 13421772800 | bytes 19398656 | tf_op jit(solution)/shard_map/cond/branch_1_fun/pallas_call | solution.py:396
  426.3 30.3 %conditional.19 = (bf16[1024,3200]{1,0:T(8,128)(2,1)}, bf16[1024,1024]{1,0:T(8,128)(2,1)}, f32[1,1024]{1,0:T(1,128)}, f32[1,1024]{1,0:T(1,128)}, bf16[512,1024]{...) conditional(s32[]{:T(128)} %convert_element_type.465, ...), branch_computations={%region_22.23_spmd, %region_23.24_spmd} | conditional | flops 13424918528 | bytes 42500320 | solution.py:338
  430.1 21.3 %branch_1_fun.13 = (bf16[1024,3200]{1,0:T(8,128)(2,1)}, bf16[1024,1024]{1,0:T(8,128)(2,1)}, f32[1,1024]{1,0:T(1,128)}, f32[1,1024]{1,0:T(1,128)}) custom-call(bf16[512,1024]{1,0:T(8,128)(2,1)} %get-tuple-element.290.first_ref, bf16[512,1024]{1,0:T(8,128)(2,1)} %copy-done.97, bf16[3200,1024]{1,0:T(8,128)(2,1)} %get-tuple-element.291.table_ref, ...), custom_call_target="tpu_custom_call" | custom-call | flops 13421772800 | bytes 19398656 | tf_op jit(solution)/shard_map/cond/branch_1_fun/pallas_call | solution.py:396
  458.7 29.4 %conditional.20 = (bf16[1024,3200]{1,0:T(8,128)(2,1)}, bf16[1024,1024]{1,0:T(8,128)(2,1)}, f32[1,1024]{1,0:T(1,128)}, f32[1,1024]{1,0:T(1,128)}, bf16[512,1024]{...) conditional(s32[]{:T(128)} %convert_element_type.465, ...), branch_computations={%region_24.25_spmd, %region_25.26_spmd} | conditional | flops 13424918528 | bytes 42500320 | solution.py:338
  462.5 21.5 %branch_1_fun.14 = (bf16[1024,3200]{1,0:T(8,128)(2,1)}, bf16[1024,1024]{1,0:T(8,128)(2,1)}, f32[1,1024]{1,0:T(1,128)}, f32[1,1024]{1,0:T(1,128)}) custom-call(bf16[512,1024]{1,0:T(8,128)(2,1)} %get-tuple-element.299.first_ref, bf16[512,1024]{1,0:T(8,128)(2,1)} %copy-done.99, bf16[3200,1024]{1,0:T(8,128)(2,1)} %get-tuple-element.300.table_ref, ...), custom_call_target="tpu_custom_call" | custom-call | flops 13421772800 | bytes 19398656 | tf_op jit(solution)/shard_map/cond/branch_1_fun/pallas_call | solution.py:396
  490.2 30.6 %conditional.21 = (bf16[1024,3200]{1,0:T(8,128)(2,1)}, bf16[1024,1024]{1,0:T(8,128)(2,1)}, f32[1,1024]{1,0:T(1,128)}, f32[1,1024]{1,0:T(1,128)}, f32[512,1024]{1...) conditional(s32[]{:T(128)} %convert_element_type.465, ...), branch_computations={%region_26.27_spmd, %region_27.28_spmd} | conditional | flops 13422821376 | bytes 34111636 | solution.py:338
  494.2 21.2 %branch_1_fun.15 = (bf16[1024,3200]{1,0:T(8,128)(2,1)}, bf16[1024,1024]{1,0:T(8,128)(2,1)}, f32[1,1024]{1,0:T(1,128)}, f32[1,1024]{1,0:T(1,128)}) custom-call(bf16[512,1024]{1,0:T(8,128)(2,1)} %get-tuple-element.308.first_ref, bf16[512,1024]{1,0:T(8,128)(2,1)} %copy-done.101, bf16[3200,1024]{1,0:T(8,128)(2,1)} %get-tuple-element.309.table_ref, ...), custom_call_target="tpu_custom_call" | custom-call | flops 13421772800 | bytes 19398656 | tf_op jit(solution)/shard_map/cond/branch_1_fun/pallas_call | solution.py:396
  563.7 23.7 %conditional.22 = (bf16[1920,1024]{1,0:T(8,128)(2,1)}) conditional(s32[]{:T(128)} %convert_element_type.465, () %tuple.202, (bf16[1024,3200]{1,0:T(8,128)(2,1)}, bf16[1024,3200]{1,0:T(8,128)(2,1)}, bf16[1024,3200]{1,0:T(8,128)(2,1)}, bf16[1024,3200]{1,0:T(8,128)(2,1)}, bf16[512,1024]{1,0:T(8,128)(2,1)}, /*index=5*/bf16[512,1024]{1,0:T(8,128)(2,1)}, ...), branch_computations={%region_28.31_spmd, %region_29.32_spmd} | conditional | flops 16106127360 | bytes 28049416 | solution.py:338
  563.7 23.7 %branch_1_fun.16 = bf16[1920,1024]{1,0:T(8,128)(2,1)} custom-call(bf16[1024,3200]{1,0:T(8,128)(2,1)} %get-tuple-element.315.refs_0_, bf16[1024,3200]{1,0:T(8,128)(2,1)} %get-tuple-element.316.refs_1_, bf16[1024,3200]{1,0:T(8,128)(2,1)} %get-tuple-element.317.refs_2_, bf16[1024,3200]{1,0:T(8,128)(2,1)} %get-tuple-element.318.refs_3_, ...), custom_call_target="tpu_custom_call" | custom-call | flops 16106127360 | bytes 28049408 | tf_op jit(solution)/shard_map/cond/branch_1_fun/pallas_call | solution.py:445
  609.9 17.7 %conditional.23 = (bf16[1280,1024]{1,0:T(8,128)(2,1)}) conditional(s32[]{:T(128)} %convert_element_type.465, () %tuple.241, (bf16[1024,3200]{1,0:T(8,128)(2,1)}, bf16[1024,3200]{1,0:T(8,128)(2,1)}, bf16[1024,3200]{1,0:T(8,128)(2,1)}, bf16[1024,3200]{1,0:T(8,128)(2,1)}, bf16[512,1024]{1,0:T(8,128)(2,1)}, /*index=5*/bf16[512,1024]{1,0:T(8,128)(2,1)}, ...), branch_computations={%region_30.33_spmd, %region_31.34_spmd} | conditional | flops 10737418240 | bytes 21495816 | solution.py:338
  609.9 17.7 %branch_1_fun.17 = bf16[1280,1024]{1,0:T(8,128)(2,1)} custom-call(bf16[1024,3200]{1,0:T(8,128)(2,1)} %get-tuple-element.327.refs_0_, bf16[1024,3200]{1,0:T(8,128)(2,1)} %get-tuple-element.328.refs_1_, bf16[1024,3200]{1,0:T(8,128)(2,1)} %get-tuple-element.329.refs_2_, bf16[1024,3200]{1,0:T(8,128)(2,1)} %get-tuple-element.330.refs_3_, ...), custom_call_target="tpu_custom_call" | custom-call | flops 10737418240 | bytes 21495808 | tf_op jit(solution)/shard_map/cond/branch_1_fun/pallas_call | solution.py:445
  627.7 12.2 %collective-permute-done.84 = bf16[256,1024]{1,0:T(8,128)(2,1)} collective-permute-done((bf16[256,1024]{1,0:T(8,128)(2,1)}, bf16[256,1024]{1,0:T(8,128)(2,1)}, u32[]{:S(2)}, u32[]{:S(2)}) %collective-permute-start.84) | collective-permute-done | bytes 524320 | tf_op jit(solution)/shard_map/ppermute | solution.py:27
  642.2 52.1 %conditional.24 = (f32[256,1024]{1,0:T(8,128)S(1)}, bf16[1024,1024]{0,1:T(8,128)(2,1)S(1)}, bf16[1024,1024]{1,0:T(8,128)(2,1)}, f32[2,1024]{1,0:T(2,128)S(1)}) conditional(s32[]{:T(128)} %convert_element_type.465, () %tuple.201, (f32[256,1024]{1,0:T(8,128)S(1)}, f32[256,1024]{1,0:T(8,128)S(1)}, f32[256]{0:T(256)S(1)}, f32[256,1024]{1,0:T(8,128)S(1)}, ...), branch_computations={%region_32.35_spmd, %region_33.44_spmd} | conditional | flops 8638433280 | bytes 144255392 | solution.py:338
  711.2 12.3 %collective-permute-start.88 = (bf16[1600,256]{1,0:T(8,128)(2,1)}, bf16[1600,256]{1,0:T(8,128)(2,1)}, u32[]{:S(2)}, u32[]{:S(2)}) collective-permute-start(bf16[1600,256]{1,0:T(8,128)(2,1)} %get-tuple-element.687), channel_id=1, source_target_pairs={{0,4},{4,0},{8,12},{12,8},{1,5},{5,1},{9,13},{13,9},{2,6},{6,2},{1... | collective-permute-start | bytes 2457608 | tf_op jit(solution)/shard_map/ppermute | solution.py:27
  723.6 64.5 %conditional.25 = (f32[256,1024]{1,0:T(8,128)}, bf16[1024,1024]{0,1:T(8,128)(2,1)}, f32[2,1024]{1,0:T(2,128)S(1)}) conditional(s32[]{:T(128)} %convert_element_type.465, () %tuple.200, (f32[256,1024]{1,0:T(8,128)S(1)}, bf16[1024,1024]{1,0:T(8,128)(2,1)}, s32[4,256]{1,0:T(4,128)S(1)}, s32[4,256]{1,0:T(4,128)S(1)}, bf16[1024,1024]{1,0:T(8,128)(2,1)}, ...), branch_computations={%region_42.45_spmd, %region_43.52_spmd} | conditional | flops 7544243712 | bytes 110719424 | solution.py:338
  742.2 18.1 %branch_1_fun.18 = bf16[1024,1024]{1,0:T(8,128)(2,1)S(1)} custom-call(bf16[1024,1024]{1,0:T(8,128)(2,1)} %get-tuple-element.352.packed_ref, bf16[1024,256]{1,0:T(8,128)(2,1)S(1)} %convolution_convert_fusion.5.grad_ref, f32[2,4,1,512]{3,2,1,0:T(1,128)S(1)} %get-tuple-element.355.log_ref, s32[1,1024]{1,0:T(1,128)S(1)} %bitcast.416, s32[1,1024]{1,0:T(1,128)S(1)} %bitcast.418, ...), custom_call_target="tpu_custom_call" | custom-call | flops 2684354560 | bytes 4194304 | tf_op jit(solution)/shard_map/cond/branch_1_fun/pallas_call | solution.py:246
  799.3 51.9 %conditional.26 = (f32[256,1024]{1,0:T(8,128)S(1)}, bf16[1024,1024]{0,1:T(8,128)(2,1)}, bf16[1024,1024]{1,0:T(8,128)(2,1)}, f32[2,1024]{1,0:T(2,128)S(1)}) conditional(s32[]{:T(128)} %convert_element_type.465, () %tuple.199, (f32[256,1024]{1,0:T(8,128)}, bf16[1024,1024]{0,1:T(8,128)(2,1)}, f32[1024,1024]{1,0:T(8,128)}, ...), branch_computations={%region_50.53_spmd, %region_51.60_spmd} | conditional | flops 8635549696 | bytes 80277784 | solution.py:338
  872.4 65.7 %conditional.27 = (f32[256,1024]{1,0:T(8,128)}, bf16[1024,1024]{0,1:T(8,128)(2,1)S(1)}, f32[2,1024]{1,0:T(2,128)S(1)}) conditional(s32[]{:T(128)} %convert_element_type.465, () %tuple.198, (f32[256,1024]{1,0:T(8,128)S(1)}, bf16[1024,1024]{1,0:T(8,128)(2,1)}, s32[4,256]{1,0:T(4,128)S(1)}, s32[4,256]{1,0:T(4,128)S(1)}, ...), branch_computations={%region_60.63_spmd, %region_61.70_spmd} | conditional | flops 7544243712 | bytes 121205248 | solution.py:338
  892.3 18.1 %branch_1_fun.19 = bf16[1024,1024]{1,0:T(8,128)(2,1)S(1)} custom-call(bf16[1024,1024]{1,0:T(8,128)(2,1)} %get-tuple-element.370.packed_ref, bf16[1024,256]{1,0:T(8,128)(2,1)S(1)} %convolution_convert_fusion.9.grad_ref, f32[2,4,1,512]{3,2,1,0:T(1,128)S(1)} %get-tuple-element.373.log_ref, s32[1,1024]{1,0:T(1,128)S(1)} %bitcast.420, s32[1,1024]{1,0:T(1,128)S(1)} %bitcast.422, ...), custom_call_target="tpu_custom_call" | custom-call | flops 2684354560 | bytes 4194304 | tf_op jit(solution)/shard_map/cond/branch_1_fun/pallas_call | solution.py:246
  948.7 21.3 %collective-permute-done.95 = bf16[512,256]{1,0:T(8,128)(2,1)S(1)} collective-permute-done((bf16[512,256]{1,0:T(8,128)(2,1)S(1)}, bf16[512,256]{1,0:T(8,128)(2,1)S(1)}, u32[]{:S(2)}, u32[]{:S(2)}) %collective-permute-start.95) | collective-permute-done | bytes 262176 | tf_op jit(solution)/shard_map/ppermute | solution.py:27
  1027.5 23.2 %shard_map.529 = (f32[12576,256]{1,0:T(8,128)}, f32[1,256]{1,0:T(1,128)}) custom-call(s32[1]{0:T(128)} %bitcast.54.count_ref, s32[8192]{0:T(1024)} %get-tuple-element.742.list_ref, bf16[4,1600,256]{2,1,0:T(8,128)(2,1)} %pad_maximum_fusion.38.near_ref, bf16[4,1600,256]{2,1,0:T(8,128)(2,1)} %collective-permute-done.99.far_ref, ...), custom_call_target="tpu_custom_call" | custom-call | flops 12877824 | bytes 29949952 | tf_op jit(solution)/shard_map/pallas_call | solution.py:512
  1118.0 31.9 %multiply_subtract_fusion = (f32[12576,256]{1,0:T(8,128)}, f32[12576,256]{1,0:T(8,128)}, f32[12576,256]{1,0:T(8,128)}) fusion(f32[12576,256]{1,0:T(8,128)} %param.83, f32[12576,256]{1,0:T(8,128)} %get-tuple-element.752, f32[]{:T(128)S(6)} %div.278, f32[12576,256]{1,0:T(8,128)} %param.84, f32[12576,256]{1,0:T(8,128)} %param.85), kind=kLoop, calls=%fused_computation.213 | loop fusion | flops 51511296 | bytes 90144768 | tf_op jit(solution)/shard_map/sub | solution.py:558
  (999 shorter events, 805.4 us)
Async XLA Ops:
  7.3 53.8 %all-gather.5.cloned.1.call-start = ((), (), s32[]{:S(2)}) async-start(), calls=%async_computation.6 | async-start | bytes 2621440 | tf_op jit(solution)/shard_map/all_gather | solution.py:639
  10.0 114.8 %all-gather.7.cloned.1.call-start = ((), (), s32[]{:S(2)}) async-start(), calls=%async_computation.7 | async-start | bytes 2621440 | tf_op jit(solution)/shard_map/all_gather | solution.py:639
  19.4 182.2 %all-gather.9.cloned.1.call-start = ((), (), s32[]{:S(2)}) async-start(), calls=%async_computation.8 | async-start | bytes 2621440 | tf_op jit(solution)/shard_map/all_gather | solution.py:639
  61.1 244.8 %all-gather.11.cloned.1.call-start = ((), (), s32[]{:S(2)}) async-start(), calls=%async_computation.9 | async-start | bytes 2621440 | tf_op jit(solution)/shard_map/all_gather | solution.py:639
  68.3 47.2 %collective-permute-start.55 = (bf16[1024,1024]{1,0:T(8,128)(2,1)}, bf16[1024,1024]{1,0:T(8,128)(2,1)}, u32[]{:S(2)}, u32[]{:S(2)}) collective-permute-start(bf16[1024,1024]{1,0:T(8,128)(2,1)} %all-gather.5.cloned.1.call-done), channel_id=1, source_target_pairs={{0,16},{16,0},{1,17},{17,1},{2,18},{18,2},{3,19},{19,3},{4,20},{20... | collective-permute-start | bytes 6291464 | tf_op jit(solution)/shard_map/ppermute | solution.py:27
  93.2 770.6 %reduce-scatter.7.cloned.1.call-start = ((), (), s32[]{:S(2)}) async-start(), calls=%async_computation.10 | async-start | bytes 1310720 | tf_op jit(solution)/shard_map/reduce_scatter | solution.py:531
  124.8 72.3 %collective-permute-start.60 = (bf16[1024,1024]{1,0:T(8,128)(2,1)}, bf16[1024,1024]{1,0:T(8,128)(2,1)}, u32[]{:S(2)}, u32[]{:S(2)}) collective-permute-start(bf16[1024,1024]{1,0:T(8,128)(2,1)} %all-gather.7.cloned.1.call-done), channel_id=1, source_target_pairs={{0,16},{16,0},{1,17},{17,1},{2,18},{18,2},{3,19},{19,3},{4,20},{20... | collective-permute-start | bytes 6291464 | tf_op jit(solution)/shard_map/ppermute | solution.py:27
  192.5 113.3 %collective-permute-start.61 = (bf16[1600,256]{1,0:T(8,128)(2,1)}, bf16[1600,256]{1,0:T(8,128)(2,1)}, u32[]{:S(2)}, u32[]{:S(2)}) collective-permute-start(bf16[1600,256]{1,0:T(8,128)(2,1)} %get-tuple-element.601), channel_id=1, source_target_pairs={{0,4},{4,0},{8,12},{12,8},{1,5},{5,1},{9,13},{13,9},{2,6},{6,2},{1... | collective-permute-start | bytes 2457608 | tf_op jit(solution)/shard_map/ppermute | solution.py:27
  192.5 113.3 %collective-permute-start.62 = (bf16[1600,256]{1,0:T(8,128)(2,1)}, bf16[1600,256]{1,0:T(8,128)(2,1)}, u32[]{:S(2)}, u32[]{:S(2)}) collective-permute-start(bf16[1600,256]{1,0:T(8,128)(2,1)} %get-tuple-element.602), channel_id=1, source_target_pairs={{0,8},{4,12},{8,0},{12,4},{1,9},{5,13},{9,1},{13,5},{2,10},{6,14},... | collective-permute-start | bytes 2457608 | tf_op jit(solution)/shard_map/ppermute | solution.py:27
  195.2 110.7 %collective-permute-start.63 = (bf16[1600,256]{1,0:T(8,128)(2,1)}, bf16[1600,256]{1,0:T(8,128)(2,1)}, u32[]{:S(2)}, u32[]{:S(2)}) collective-permute-start(bf16[1600,256]{1,0:T(8,128)(2,1)} %get-tuple-element.603), channel_id=1, source_target_pairs={{0,12},{4,8},{8,4},{12,0},{1,13},{5,9},{9,5},{13,1},{2,14},{6,10},... | collective-permute-start | bytes 2457608 | tf_op jit(solution)/shard_map/ppermute | solution.py:27
  315.2 72.4 %collective-permute-start.65 = (bf16[1600,1024]{1,0:T(8,128)(2,1)}, bf16[1600,1024]{1,0:T(8,128)(2,1)}, u32[]{:S(2)}, u32[]{:S(2)}) collective-permute-start(bf16[1600,1024]{1,0:T(8,128)(2,1)} %constant_dynamic-update-slice_fusion), channel_id=1, source_target_pairs={{0,16},{16,0},{1,17},{17,1},{2,18},{18,2},{3,19},{19,3},{4,20},{20... | collective-permute-start | bytes 9830408 | tf_op jit(solution)/shard_map/ppermute | solution.py:27
  372.3 52.0 %collective-permute-start.67 = (bf16[256,1024]{1,0:T(8,128)(2,1)S(1)}, bf16[256,1024]{1,0:T(8,128)(2,1)}, u32[]{:S(2)}, u32[]{:S(2)}) collective-permute-start(bf16[256,1024]{1,0:T(8,128)(2,1)S(1)} %get-tuple-element.1175), channel_id=1, source_target_pairs={{0,8},{4,12},{8,0},{12,4},{1,9},{5,13},{9,1},{13,5},{2,10},{6,14},... | collective-permute-start | bytes 1572872 | tf_op jit(solution)/shard_map/ppermute | solution.py:27
  375.3 81.3 %collective-permute-start.68 = (bf16[256,1024]{1,0:T(8,128)(2,1)S(1)}, bf16[256,1024]{1,0:T(8,128)(2,1)S(1)}, u32[]{:S(2)}, u32[]{:S(2)}) collective-permute-start(bf16[256,1024]{1,0:T(8,128)(2,1)S(1)} %get-tuple-element.1175), channel_id=1, source_target_pairs={{0,12},{4,8},{8,4},{12,0},{1,13},{5,9},{9,5},{13,1},{2,14},{6,10},... | collective-permute-start | bytes 1572872 | tf_op jit(solution)/shard_map/ppermute | solution.py:27
  550.8 40.8 %collective-permute-start.82 = (bf16[256,1024]{1,0:T(8,128)(2,1)S(1)}, bf16[256,1024]{1,0:T(8,128)(2,1)}, u32[]{:S(2)}, u32[]{:S(2)}) collective-permute-start(bf16[256,1024]{1,0:T(8,128)(2,1)S(1)} %slice.849), channel_id=1, source_target_pairs={{0,2},{1,3},{2,0},{3,1},{4,6},{5,7},{6,4},{7,5},{8,10},{9,11},{10,... | collective-permute-start | bytes 1572872 | tf_op jit(solution)/shard_map/ppermute | solution.py:27
  554.5 37.1 %collective-permute-start.81 = (bf16[256,1024]{1,0:T(8,128)(2,1)}, bf16[256,1024]{1,0:T(8,128)(2,1)}, u32[]{:S(2)}, u32[]{:S(2)}) collective-permute-start(bf16[256,1024]{1,0:T(8,128)(2,1)} %slice.850), channel_id=1, source_target_pairs={{0,2},{1,3},{2,0},{3,1},{4,6},{5,7},{6,4},{7,5},{8,10},{9,11},{10,... | collective-permute-start | bytes 1572872 | tf_op jit(solution)/shard_map/ppermute | solution.py:27
  600.5 93.8 %collective-permute-start.87 = (bf16[1600,1024]{1,0:T(8,128)(2,1)}, bf16[1600,1024]{1,0:T(8,128)(2,1)}, u32[]{:S(2)}, u32[]{:S(2)}) collective-permute-start(bf16[1600,1024]{1,0:T(8,128)(2,1)} %slice.623), channel_id=1, source_target_pairs={{0,16},{16,0},{1,17},{17,1},{2,18},{18,2},{3,19},{19,3},{4,20},{20... | collective-permute-start | bytes 9830408 | tf_op jit(solution)/shard_map/ppermute | solution.py:27
  601.3 38.5 %collective-permute-start.84 = (bf16[256,1024]{1,0:T(8,128)(2,1)}, bf16[256,1024]{1,0:T(8,128)(2,1)}, u32[]{:S(2)}, u32[]{:S(2)}) collective-permute-start(bf16[256,1024]{1,0:T(8,128)(2,1)} %fusion.74), channel_id=1, source_target_pairs={{0,8},{4,12},{8,0},{12,4},{1,9},{5,13},{9,1},{13,5},{2,10},{6,14},... | collective-permute-start | bytes 1572872 | tf_op jit(solution)/shard_map/ppermute | solution.py:27
  709.2 78.9 %collective-permute-start.90 = (bf16[1024,512]{0,1:T(8,128)(2,1)}, bf16[1024,512]{0,1:T(8,128)(2,1)}, u32[]{:S(2)}, u32[]{:S(2)}) collective-permute-start(bf16[1024,512]{0,1:T(8,128)(2,1)} %constant_dynamic-slice_fusion.5), channel_id=1, source_target_pairs={{0,16},{16,0},{1,17},{17,1},{2,18},{18,2},{3,19},{19,3},{4,20},{20... | collective-permute-start | bytes 3145736 | tf_op jit(solution)/shard_map/ppermute | solution.py:27
  710.4 77.7 %collective-permute-start.91 = (bf16[1024,512]{0,1:T(8,128)(2,1)}, bf16[1024,512]{0,1:T(8,128)(2,1)}, u32[]{:S(2)}, u32[]{:S(2)}) collective-permute-start(bf16[1024,512]{0,1:T(8,128)(2,1)} %constant_dynamic-slice_fusion.4), channel_id=1, source_target_pairs={{0,16},{16,0},{1,17},{17,1},{2,18},{18,2},{3,19},{19,3},{4,20},{20... | collective-permute-start | bytes 3145736 | tf_op jit(solution)/shard_map/ppermute | solution.py:27
  711.2 76.9 %collective-permute-start.88 = (bf16[1600,256]{1,0:T(8,128)(2,1)}, bf16[1600,256]{1,0:T(8,128)(2,1)}, u32[]{:S(2)}, u32[]{:S(2)}) collective-permute-start(bf16[1600,256]{1,0:T(8,128)(2,1)} %get-tuple-element.687), channel_id=1, source_target_pairs={{0,4},{4,0},{8,12},{12,8},{1,5},{5,1},{9,13},{13,9},{2,6},{6,2},{1... | collective-permute-start | bytes 2457608 | tf_op jit(solution)/shard_map/ppermute | solution.py:27
  723.5 64.5 %collective-permute-start.89 = (bf16[1600,256]{1,0:T(8,128)(2,1)}, bf16[1600,256]{1,0:T(8,128)(2,1)}, u32[]{:S(2)}, u32[]{:S(2)}) collective-permute-start(bf16[1600,256]{1,0:T(8,128)(2,1)} %get-tuple-element.688), channel_id=1, source_target_pairs={{0,8},{4,12},{8,0},{12,4},{1,9},{5,13},{9,1},{13,5},{2,10},{6,14},... | collective-permute-start | bytes 2457608 | tf_op jit(solution)/shard_map/ppermute | solution.py:27
  793.8 78.7 %reduce-scatter.9.cloned.1.call-start = ((), (), s32[]{:S(2)}) async-start(), calls=%async_computation.11 | async-start | bytes 1310720 | tf_op jit(solution)/shard_map/reduce_scatter | solution.py:531
  794.4 187.4 %reduce-scatter.13.cloned.1.call-start = ((), (), s32[]{:S(2)}) async-start(), calls=%async_computation.13 | async-start | bytes 2621440 | tf_op jit(solution)/shard_map/reduce_scatter | solution.py:531
  795.7 55.5 %collective-permute-start.93 = (bf16[1024,512]{0,1:T(8,128)(2,1)S(1)}, bf16[1024,512]{0,1:T(8,128)(2,1)}, u32[]{:S(2)}, u32[]{:S(2)}) collective-permute-start(bf16[1024,512]{0,1:T(8,128)(2,1)S(1)} %constant_dynamic-slice_fusion.2), channel_id=1, source_target_pairs={{0,16},{16,0},{1,17},{17,1},{2,18},{18,2},{3,19},{19,3},{4,20},{20... | collective-permute-start | bytes 3145736 | tf_op jit(solution)/shard_map/ppermute | solution.py:27
  797.0 54.2 %collective-permute-start.92 = (bf16[1600,256]{1,0:T(8,128)(2,1)}, bf16[1600,256]{1,0:T(8,128)(2,1)}, u32[]{:S(2)}, u32[]{:S(2)}) collective-permute-start(bf16[1600,256]{1,0:T(8,128)(2,1)} %get-tuple-element.704), channel_id=1, source_target_pairs={{0,12},{4,8},{8,4},{12,0},{1,13},{5,9},{9,5},{13,1},{2,14},{6,10},... | collective-permute-start | bytes 2457608 | tf_op jit(solution)/shard_map/ppermute | solution.py:27
  851.2 136.4 %reduce-scatter.17.cloned.1.call-start = ((), (), s32[]{:S(2)}) async-start(), calls=%async_computation.15 | async-start | bytes 2621440 | tf_op jit(solution)/shard_map/reduce_scatter | solution.py:531
  855.3 195.3 %reduce-scatter.11.cloned.1.call-start = ((), (), s32[]{:S(2)}) async-start(), calls=%async_computation.12 | async-start | bytes 1310720 | tf_op jit(solution)/shard_map/reduce_scatter | solution.py:531
  859.6 122.2 %collective-permute-start.99 = (bf16[4,1600,256]{2,1,0:T(8,128)(2,1)}, bf16[4,1600,256]{2,1,0:T(8,128)(2,1)}, u32[]{:S(2)}, u32[]{:S(2)}) collective-permute-start(bf16[4,1600,256]{2,1,0:T(8,128)(2,1)} %pad_maximum_fusion.38.near_ref), channel_id=1, source_target_pairs={{0,16},{16,0},{1,17},{17,1},{2,18},{18,2},{3,19},{19,3},{4,20},{20... | collective-permute-start | bytes 9830408 | tf_op jit(solution)/shard_map/ppermute | solution.py:27
  863.4 191.0 %reduce-scatter.15.cloned.1.call-start = ((), (), s32[]{:S(2)}) async-start(), calls=%async_computation.14 | async-start | bytes 1310720 | tf_op jit(solution)/shard_map/reduce_scatter | solution.py:531
  938.2 42.6 %collective-permute-start.98 = (bf16[1024,512]{0,1:T(8,128)(2,1)S(1)}, bf16[1024,512]{0,1:T(8,128)(2,1)S(1)}, u32[]{:S(2)}, u32[]{:S(2)}) collective-permute-start(bf16[1024,512]{0,1:T(8,128)(2,1)S(1)} %constant_dynamic-slice_fusion.1), channel_id=1, source_target_pairs={{0,16},{16,0},{1,17},{17,1},{2,18},{18,2},{3,19},{19,3},{4,20},{20... | collective-permute-start | bytes 3145736 | tf_op jit(solution)/shard_map/ppermute | solution.py:27
  1014.7 42.3 %collective-permute-start.109 = (bf16[256,512]{0,1:T(8,128)(2,1)}, bf16[256,512]{0,1:T(8,128)(2,1)S(1)}, u32[]{:S(2)}, u32[]{:S(2)}) collective-permute-start(bf16[256,512]{0,1:T(8,128)(2,1)} %reduce-scatter.9.cloned.1.call-done), channel_id=1, source_target_pairs={{0,16},{16,0},{1,17},{17,1},{2,18},{18,2},{3,19},{19,3},{4,20},{20... | collective-permute-start | bytes 786440 | tf_op jit(solution)/shard_map/ppermute | solution.py:27
  1015.3 45.5 %collective-permute-start.108 = (bf16[256,512]{0,1:T(8,128)(2,1)}, bf16[256,512]{0,1:T(8,128)(2,1)}, u32[]{:S(2)}, u32[]{:S(2)}) collective-permute-start(bf16[256,512]{0,1:T(8,128)(2,1)} %reduce-scatter.7.cloned.1.call-done), channel_id=1, source_target_pairs={{0,16},{16,0},{1,17},{17,1},{2,18},{18,2},{3,19},{19,3},{4,20},{20... | collective-permute-start | bytes 786440 | tf_op jit(solution)/shard_map/ppermute | solution.py:27
  (255 other events, 2831.5 us)
Sparse Core Ops, SparseCore 0:
  10.3 49.6 all-gather.4
  62.1 62.6 all-gather.6
  126.9 45.3 all-gather.8
  174.3 99.7 all-gather.10
  793.9 47.6 reduce-scatter.6
  844.4 27.9 reduce-scatter.8
  875.3 42.5 reduce-scatter.12
  920.3 56.0 reduce-scatter.16
  979.3 27.2 reduce-scatter.10
  1009.4 25.7 reduce-scatter.14

commit v4 on v3

--- a/solution.py
+++ b/solution.py
@@ -78,13 +78,17 @@
 
 
 def from_all(block, axis):
-    size = lax.axis_size(axis)
-    found = jnp.stack([block] + [swap(block, axis, mask) for mask in range(1, size)])
+    names = axis if isinstance(axis, tuple) else (axis,)
+    size = 1
+    for name in names:
+        size *= lax.axis_size(name)
+    routes = [[(i, i ^ mask) for i in range(size)] for mask in range(1, size)]
+    found = jnp.stack([block] + [lax.ppermute(block, axis, route) for route in routes])
     return jnp.take(found, lax.axis_index(axis) ^ jnp.arange(size), axis=0)
 
 
 def sum_everywhere(block):
-    for axis in ("seq", "pipe", "dp"):
+    for axis in ("seq", ("pipe", "dp")):
         block = jnp.sum(from_all(block, axis), 0)
     return block
 
@@ -858,13 +862,11 @@
     gradient, attn_coming = send_halves(gradient, [attn_early])
     late_halves = [swap(part, "pipe", 1) for part in feed_late]
 
-    sent_rows = jnp.concatenate(
-        [(gradient - target_part).astype(BF16), gradient.astype(BF16)], 0
-    )
-    back = exchange_blocks(take_columns(sent_rows, replica, replicas), "dp")
-    position_part = sum(part[shard_rows:].astype(F32) for part in back)
-    position_grad = position_part + swap(position_part, "pipe", 1)
-    back = jnp.concatenate([part[:shard_rows] for part in back], 0)
+    back = exchange_blocks(
+        take_columns((gradient - target_part).astype(BF16), replica, replicas), "dp"
+    )
+    back = jnp.concatenate(back, 0)
+    position_sent = gradient.astype(BF16)
     back, attn_coming, half_far, feed_early[0] = together(
         back, attn_coming, half_far, feed_early[0]
     )
@@ -872,7 +874,14 @@
     attn_early = scatter_over(attn_early, "dp")
     back_other = swap(back, "pipe", 1)
     own_rows = spread(back)
-    back_other, feed_early[1] = together(back_other, feed_early[1])
+    back_other, feed_early[1], position_sent = together(
+        back_other, feed_early[1], position_sent
+    )
+    position_part = sum(
+        part.astype(F32)
+        for part in exchange_blocks(take_columns(position_sent, replica, replicas), "dp")
+    )
+    position_grad = position_part + swap(position_part, "pipe", 1)
     other_rows = spread(back_other)
     table_grad, table_square = scatter_rows(
         back_listing, back_count, half_back, half_far, own_rows, other_rows, slice_rows
@@ -897,9 +906,9 @@
         for k in range(2)
     )
     qkv_grad = attn_part[:, :qkv_columns].reshape(attn_qkv.shape)
-    out_grad = attn_part[:, qkv_columns:].T[None]
-    fc_grad = fc_part[None]
-    proj_grad = proj_part.T[None]
+    out_grad = by_rows(attn_part[:, qkv_columns:].T)[None]
+    fc_grad = by_rows(fc_part)[None]
+    proj_grad = by_rows(proj_part.T)[None]
 
     norm_grad_all = jnp.concatenate([grad_gains[0], grad_gains[1], grad_final], 0)
     squares = (

time: 1170 us -> 1170 us (level)
  starting transfers between devices: 136 us -> 153 us
    ppermute x0 -> x17, starting transfers between devices: none -> 22.9 us  [from_all(): lax.ppermute(block, axis, route)]
    ppermute x116 -> x105, waiting for transfers between devices: 326 us -> 304 us  [swap(): return lax.ppermute(block, axis, route)]
    unnamed x238 -> x211, local copies, waits for them, and re-layouts: 33.6 us -> 22.5 us
    ppermute x116 -> x105, starting transfers between devices: 133 us -> 126 us  [swap(): return lax.ppermute(block, axis, route)]
  transfers between devices with their start and end apart: 128 -> 134, of which waited for: 64 -> 67; matrix products, arithmetic and copies ran while one was open for 26% -> 26% of each run, Pallas kernels for 16% -> 16%
where the time goes in v4:
time: 1170 us; the launch traced here: 1160 us
  waiting for transfers between devices  333 us (28%)
  other arithmetic  209 us (18%)
  Pallas kernels  209 us (18%)
  starting transfers between devices  153 us (13%)
  local copies, waits for them, and re-layouts  133 us (11%)
  matrix products  100 us (9%)
  between operations  24 us (2%)
    ppermute x105, waiting for transfers between devices, swap(): return lax.ppermute(block, axis, route)  304 us
    ppermute x105, starting transfers between devices, swap(): return lax.ppermute(block, axis, route)  126 us
    pallas_call x4, Pallas kernels, head_block(): pl.pallas_call(head_kernel, grid=(length // tile,), in_specs=[pl.BlockSpe...  84.8 us
    sub x8, other arithmetic, adamw_update(): return (master - rate * (ratio + decay * master), first_new, second_new)  44.2 us
    pallas_call x2, Pallas kernels, table_gradient_of(): pl.pallas_call(lambda *refs: table_kernel(count, *refs), grid=(count_tile...  41.4 us
    pallas_call x2, Pallas kernels, attend_backward(): pl.pallas_call(attend_back_kernel, grid=(steps,), in_specs=[pl.BlockSpec(...  36.1 us
    cond x126, local copies, waits for them, and re-layouts  27.1 us
    pallas_call x1, Pallas kernels, scatter_rows(): pl.pallas_call(scatter_kernel, in_specs=[scalars, scalars, whole, whole,...  24.1 us
  transfers between devices with their start and end apart: 134, of which 67 were waited for; matrix products, arithmetic and copies ran while one was open for 26% of the time, Pallas kernels for 16%

profile of v4, /device:TPU:0, one launch (start us, length us, event | category | flops | bytes accessed | tf_op | source)
XLA Modules:
  0.0 1161.0 jit_solution(1991340209416102813)
XLA Ops:
  32.4 20.6 %gather_fusion.1 = bf16[4096,256]{1,0:T(8,128)(2,1)} fusion(f32[12576,256]{1,0:T(8,128)} %param.81, s32[4096]{0:T(1024)S(1)} %broadcast_clamp_fusion), kind=kCustom, calls=%fused_computation.7 | custom fusion | bytes 4210688 | tf_op jit(solution)/shard_map/jit(_take)/gather | solution.py:651
  131.0 56.2 %conditional.14 = (f32[256,1024]{1,0:T(8,128)S(1)}, f32[256,1024]{1,0:T(8,128)S(1)}, bf16[1024,1024]{1,0:T(8,128)(2,1)}, bf16[1024,1024]{1,0:T(8,128)(2,1)}, f32...) conditional(s32[]{:T(128)} %convert_element_type.465, () %tuple.206, (f32[256,1024]{1,0:T(8,128)S(1)}, ...), branch_computations={%region_2.3_spmd, %region_3.6_spmd} | conditional | flops 3771728128 | bytes 59311372 | solution.py:342
  133.3 12.1 %collective-permute-done.7 = bf16[256,1024]{1,0:T(8,128)(2,1)S(1)} collective-permute-done((bf16[256,1024]{1,0:T(8,128)(2,1)S(1)}, bf16[256,1024]{1,0:T(8,128)(2,1)S(1)}, u32[]{:S(2)}, u32[]{:S(2)}) %collective-permute-start.7) | collective-permute-done | bytes 524320 | tf_op jit(solution)/shard_map/cond/branch_1_fun/ppermute | solution.py:27
  174.5 12.4 %collective-permute-done.10 = bf16[256,1024]{1,0:T(8,128)(2,1)S(1)} collective-permute-done((bf16[256,1024]{1,0:T(8,128)(2,1)S(1)}, bf16[256,1024]{1,0:T(8,128)(2,1)S(1)}, u32[]{:S(2)}, u32[]{:S(2)}) %collective-permute-start.10) | collective-permute-done | bytes 524320 | tf_op jit(solution)/shard_map/cond/branch_1_fun/ppermute | solution.py:27
  201.6 46.5 %conditional.15 = (f32[256,1024]{1,0:T(8,128)S(1)}, f32[256,1024]{1,0:T(8,128)S(1)}, bf16[1024,1024]{1,0:T(8,128)(2,1)}, f32[1024,1024]{1,0:T(8,128)}, bf16[1024,1024]{1,0:T(8,128)(2,1)}) conditional(s32[]{:T(128)} %convert_element_type.465, () %tuple.205, (f32[256,1024]{1,0:T(8,128)S(1)}, f32[4,1024]{1,0:T(4,128)S(1)}, ...), branch_computations={%region_6.7_spmd, %region_7.10_spmd} | conditional | flops 4316987392 | bytes 70288648 | solution.py:342
  235.3 12.4 %collective-permute-done.14 = bf16[256,1024]{1,0:T(8,128)(2,1)S(1)} collective-permute-done((bf16[256,1024]{1,0:T(8,128)(2,1)S(1)}, bf16[256,1024]{1,0:T(8,128)(2,1)S(1)}, u32[]{:S(2)}, u32[]{:S(2)}) %collective-permute-start.14) | collective-permute-done | bytes 524320 | tf_op jit(solution)/shard_map/cond/branch_1_fun/ppermute | solution.py:27
  249.0 56.7 %conditional.16 = (f32[256,1024]{1,0:T(8,128)S(1)}, f32[256,1024]{1,0:T(8,128)S(1)}, bf16[1024,1024]{1,0:T(8,128)(2,1)}, bf16[1024,1024]{1,0:T(8,128)(2,1)}, f32...) conditional(s32[]{:T(128)} %convert_element_type.465, () %tuple.204, (f32[256,1024]{1,0:T(8,128)S(1)}, ...), branch_computations={%region_10.11_spmd, %region_11.14_spmd} | conditional | flops 3771728128 | bytes 57214192 | solution.py:342
  293.1 12.4 %collective-permute-done.18 = bf16[256,1024]{1,0:T(8,128)(2,1)S(1)} collective-permute-done((bf16[256,1024]{1,0:T(8,128)(2,1)S(1)}, bf16[256,1024]{1,0:T(8,128)(2,1)S(1)}, u32[]{:S(2)}, u32[]{:S(2)}) %collective-permute-start.18) | collective-permute-done | bytes 524320 | tf_op jit(solution)/shard_map/cond/branch_1_fun/ppermute | solution.py:27
  317.7 49.0 %conditional.17 = (f32[256,1024]{0,1:T(8,128)S(1)}, bf16[1024,1024]{0,1:T(8,128)(2,1)}, f32[1024,1024]{1,0:T(8,128)}, bf16[1024,1024]{1,0:T(8,128)(2,1)}, f32[256,1]{0,1:T(1,128)S(1)}, /*index=5*/f32[256,1024]{1,0:T(8,128)S(1)}) conditional(s32[]{:T(128)} %convert_element_type.465, () %tuple.203, (f32[256,1024]{1,0:T(8,128)S(1)}, ...), branch_computations={%region_14.15_spmd, %region_15.19_spmd} | conditional | flops 4317249536 | bytes 82872648 | solution.py:342
  352.7 12.5 %collective-permute-done.22 = bf16[256,1024]{0,1:T(8,128)(2,1)S(1)} collective-permute-done((bf16[256,1024]{0,1:T(8,128)(2,1)S(1)}, bf16[256,1024]{0,1:T(8,128)(2,1)S(1)}, u32[]{:S(2)}, u32[]{:S(2)}) %collective-permute-start.22) | collective-permute-done | bytes 524320 | tf_op jit(solution)/shard_map/cond/branch_1_fun/ppermute | solution.py:27
  395.3 28.8 %conditional.18 = (bf16[1024,3200]{1,0:T(8,128)(2,1)}, bf16[1024,1024]{1,0:T(8,128)(2,1)}, f32[1,1024]{1,0:T(1,128)}, f32[1,1024]{1,0:T(1,128)}, bf16[512,1024]{...) conditional(s32[]{:T(128)} %convert_element_type.465, ...), branch_computations={%region_20.21_spmd, %region_21.22_spmd} | conditional | flops 13424918528 | bytes 46694652 | solution.py:342
  399.2 20.9 %branch_1_fun.12 = (bf16[1024,3200]{1,0:T(8,128)(2,1)}, bf16[1024,1024]{1,0:T(8,128)(2,1)}, f32[1,1024]{1,0:T(1,128)}, f32[1,1024]{1,0:T(1,128)}) custom-call(bf16[512,1024]{1,0:T(8,128)(2,1)} %copy-done.53, bf16[512,1024]{1,0:T(8,128)(2,1)} %copy-done.88, bf16[3200,1024]{1,0:T(8,128)(2,1)} %get-tuple-element.281.table_ref, ...), custom_call_target="tpu_custom_call" | custom-call | flops 13421772800 | bytes 19398656 | tf_op jit(solution)/shard_map/cond/branch_1_fun/pallas_call | solution.py:400
  426.1 30.3 %conditional.19 = (bf16[1024,3200]{1,0:T(8,128)(2,1)}, bf16[1024,1024]{1,0:T(8,128)(2,1)}, f32[1,1024]{1,0:T(1,128)}, f32[1,1024]{1,0:T(1,128)}, bf16[512,1024]{...) conditional(s32[]{:T(128)} %convert_element_type.465, ...), branch_computations={%region_22.23_spmd, %region_23.24_spmd} | conditional | flops 13424918528 | bytes 42500320 | solution.py:342
  430.0 21.2 %branch_1_fun.13 = (bf16[1024,3200]{1,0:T(8,128)(2,1)}, bf16[1024,1024]{1,0:T(8,128)(2,1)}, f32[1,1024]{1,0:T(1,128)}, f32[1,1024]{1,0:T(1,128)}) custom-call(bf16[512,1024]{1,0:T(8,128)(2,1)} %get-tuple-element.289.first_ref, bf16[512,1024]{1,0:T(8,128)(2,1)} %copy-done.90, bf16[3200,1024]{1,0:T(8,128)(2,1)} %get-tuple-element.290.table_ref, ...), custom_call_target="tpu_custom_call" | custom-call | flops 13421772800 | bytes 19398656 | tf_op jit(solution)/shard_map/cond/branch_1_fun/pallas_call | solution.py:400
  458.5 29.4 %conditional.20 = (bf16[1024,3200]{1,0:T(8,128)(2,1)}, bf16[1024,1024]{1,0:T(8,128)(2,1)}, f32[1,1024]{1,0:T(1,128)}, f32[1,1024]{1,0:T(1,128)}, bf16[512,1024]{...) conditional(s32[]{:T(128)} %convert_element_type.465, ...), branch_computations={%region_24.25_spmd, %region_25.26_spmd} | conditional | flops 13424918528 | bytes 42500320 | solution.py:342
  462.3 21.5 %branch_1_fun.14 = (bf16[1024,3200]{1,0:T(8,128)(2,1)}, bf16[1024,1024]{1,0:T(8,128)(2,1)}, f32[1,1024]{1,0:T(1,128)}, f32[1,1024]{1,0:T(1,128)}) custom-call(bf16[512,1024]{1,0:T(8,128)(2,1)} %get-tuple-element.298.first_ref, bf16[512,1024]{1,0:T(8,128)(2,1)} %copy-done.92, bf16[3200,1024]{1,0:T(8,128)(2,1)} %get-tuple-element.299.table_ref, ...), custom_call_target="tpu_custom_call" | custom-call | flops 13421772800 | bytes 19398656 | tf_op jit(solution)/shard_map/cond/branch_1_fun/pallas_call | solution.py:400
  490.0 30.6 %conditional.21 = (bf16[1024,3200]{1,0:T(8,128)(2,1)}, bf16[1024,1024]{1,0:T(8,128)(2,1)}, f32[1,1024]{1,0:T(1,128)}, f32[1,1024]{1,0:T(1,128)}, f32[512,1024]{1...) conditional(s32[]{:T(128)} %convert_element_type.465, ...), branch_computations={%region_26.27_spmd, %region_27.28_spmd} | conditional | flops 13422821376 | bytes 34111636 | solution.py:342
  493.9 21.2 %branch_1_fun.15 = (bf16[1024,3200]{1,0:T(8,128)(2,1)}, bf16[1024,1024]{1,0:T(8,128)(2,1)}, f32[1,1024]{1,0:T(1,128)}, f32[1,1024]{1,0:T(1,128)}) custom-call(bf16[512,1024]{1,0:T(8,128)(2,1)} %get-tuple-element.307.first_ref, bf16[512,1024]{1,0:T(8,128)(2,1)} %copy-done.94, bf16[3200,1024]{1,0:T(8,128)(2,1)} %get-tuple-element.308.table_ref, ...), custom_call_target="tpu_custom_call" | custom-call | flops 13421772800 | bytes 19398656 | tf_op jit(solution)/shard_map/cond/branch_1_fun/pallas_call | solution.py:400
  563.5 23.7 %conditional.22 = (bf16[1920,1024]{1,0:T(8,128)(2,1)}) conditional(s32[]{:T(128)} %convert_element_type.465, () %tuple.201, (bf16[1024,3200]{1,0:T(8,128)(2,1)}, bf16[1024,3200]{1,0:T(8,128)(2,1)}, bf16[1024,3200]{1,0:T(8,128)(2,1)}, bf16[1024,3200]{1,0:T(8,128)(2,1)}, bf16[512,1024]{1,0:T(8,128)(2,1)}, /*index=5*/bf16[512,1024]{1,0:T(8,128)(2,1)}, ...), branch_computations={%region_28.31_spmd, %region_29.32_spmd} | conditional | flops 16106127360 | bytes 28049416 | solution.py:342
  563.5 23.7 %branch_1_fun.16 = bf16[1920,1024]{1,0:T(8,128)(2,1)} custom-call(bf16[1024,3200]{1,0:T(8,128)(2,1)} %get-tuple-element.314.refs_0_, bf16[1024,3200]{1,0:T(8,128)(2,1)} %get-tuple-element.315.refs_1_, bf16[1024,3200]{1,0:T(8,128)(2,1)} %get-tuple-element.316.refs_2_, bf16[1024,3200]{1,0:T(8,128)(2,1)} %get-tuple-element.317.refs_3_, ...), custom_call_target="tpu_custom_call" | custom-call | flops 16106127360 | bytes 28049408 | tf_op jit(solution)/shard_map/cond/branch_1_fun/pallas_call | solution.py:449
  609.7 17.7 %conditional.23 = (bf16[1280,1024]{1,0:T(8,128)(2,1)}) conditional(s32[]{:T(128)} %convert_element_type.465, () %tuple.240, (bf16[1024,3200]{1,0:T(8,128)(2,1)}, bf16[1024,3200]{1,0:T(8,128)(2,1)}, bf16[1024,3200]{1,0:T(8,128)(2,1)}, bf16[1024,3200]{1,0:T(8,128)(2,1)}, bf16[512,1024]{1,0:T(8,128)(2,1)}, /*index=5*/bf16[512,1024]{1,0:T(8,128)(2,1)}, ...), branch_computations={%region_30.33_spmd, %region_31.34_spmd} | conditional | flops 10737418240 | bytes 21495816 | solution.py:342
  609.7 17.7 %branch_1_fun.17 = bf16[1280,1024]{1,0:T(8,128)(2,1)} custom-call(bf16[1024,3200]{1,0:T(8,128)(2,1)} %get-tuple-element.326.refs_0_, bf16[1024,3200]{1,0:T(8,128)(2,1)} %get-tuple-element.327.refs_1_, bf16[1024,3200]{1,0:T(8,128)(2,1)} %get-tuple-element.328.refs_2_, bf16[1024,3200]{1,0:T(8,128)(2,1)} %get-tuple-element.329.refs_3_, ...), custom_call_target="tpu_custom_call" | custom-call | flops 10737418240 | bytes 21495808 | tf_op jit(solution)/shard_map/cond/branch_1_fun/pallas_call | solution.py:449
  627.4 12.2 %collective-permute-done.84 = bf16[256,1024]{1,0:T(8,128)(2,1)} collective-permute-done((bf16[256,1024]{1,0:T(8,128)(2,1)}, bf16[256,1024]{1,0:T(8,128)(2,1)}, u32[]{:S(2)}, u32[]{:S(2)}) %collective-permute-start.84) | collective-permute-done | bytes 524320 | tf_op jit(solution)/shard_map/ppermute | solution.py:27
  642.0 52.1 %conditional.24 = (f32[256,1024]{1,0:T(8,128)S(1)}, bf16[1024,1024]{0,1:T(8,128)(2,1)S(1)}, bf16[1024,1024]{1,0:T(8,128)(2,1)}, f32[2,1024]{1,0:T(2,128)S(1)}) conditional(s32[]{:T(128)} %convert_element_type.465, () %tuple.200, (f32[256,1024]{1,0:T(8,128)S(1)}, f32[256,1024]{1,0:T(8,128)S(1)}, f32[256]{0:T(256)S(1)}, f32[256,1024]{1,0:T(8,128)S(1)}, ...), branch_computations={%region_32.35_spmd, %region_33.44_spmd} | conditional | flops 8638433280 | bytes 144255392 | solution.py:342
  711.0 12.3 %collective-permute-start.88 = (bf16[1600,256]{1,0:T(8,128)(2,1)}, bf16[1600,256]{1,0:T(8,128)(2,1)}, u32[]{:S(2)}, u32[]{:S(2)}) collective-permute-start(bf16[1600,256]{1,0:T(8,128)(2,1)} %get-tuple-element.687), channel_id=1, source_target_pairs={{0,4},{4,0},{8,12},{12,8},{1,5},{5,1},{9,13},{13,9},{2,6},{6,2},{1... | collective-permute-start | bytes 2457608 | tf_op jit(solution)/shard_map/ppermute | solution.py:27
  723.3 64.5 %conditional.25 = (f32[256,1024]{1,0:T(8,128)}, bf16[1024,1024]{0,1:T(8,128)(2,1)}, f32[2,1024]{1,0:T(2,128)S(1)}) conditional(s32[]{:T(128)} %convert_element_type.465, () %tuple.199, (f32[256,1024]{1,0:T(8,128)S(1)}, bf16[1024,1024]{1,0:T(8,128)(2,1)}, s32[4,256]{1,0:T(4,128)S(1)}, s32[4,256]{1,0:T(4,128)S(1)}, bf16[1024,1024]{1,0:T(8,128)(2,1)}, ...), branch_computations={%region_42.45_spmd, %region_43.52_spmd} | conditional | flops 7544243712 | bytes 110719424 | solution.py:342
  742.0 18.1 %branch_1_fun.18 = bf16[1024,1024]{1,0:T(8,128)(2,1)S(1)} custom-call(bf16[1024,1024]{1,0:T(8,128)(2,1)} %get-tuple-element.351.packed_ref, bf16[1024,256]{1,0:T(8,128)(2,1)S(1)} %convolution_convert_fusion.5.grad_ref, f32[2,4,1,512]{3,2,1,0:T(1,128)S(1)} %get-tuple-element.354.log_ref, s32[1,1024]{1,0:T(1,128)S(1)} %bitcast.437, s32[1,1024]{1,0:T(1,128)S(1)} %bitcast.439, ...), custom_call_target="tpu_custom_call" | custom-call | flops 2684354560 | bytes 4194304 | tf_op jit(solution)/shard_map/cond/branch_1_fun/pallas_call | solution.py:250
  799.1 51.9 %conditional.26 = (f32[256,1024]{1,0:T(8,128)S(1)}, bf16[1024,1024]{0,1:T(8,128)(2,1)}, bf16[1024,1024]{1,0:T(8,128)(2,1)}, f32[2,1024]{1,0:T(2,128)S(1)}) conditional(s32[]{:T(128)} %convert_element_type.465, () %tuple.198, (f32[256,1024]{1,0:T(8,128)}, bf16[1024,1024]{0,1:T(8,128)(2,1)}, f32[1024,1024]{1,0:T(8,128)}, ...), branch_computations={%region_50.53_spmd, %region_51.60_spmd} | conditional | flops 8635549696 | bytes 80277784 | solution.py:342
  872.2 65.7 %conditional.27 = (f32[256,1024]{1,0:T(8,128)}, bf16[1024,1024]{0,1:T(8,128)(2,1)S(1)}, f32[2,1024]{1,0:T(2,128)S(1)}) conditional(s32[]{:T(128)} %convert_element_type.465, () %tuple.197, (f32[256,1024]{1,0:T(8,128)S(1)}, bf16[1024,1024]{1,0:T(8,128)(2,1)}, s32[4,256]{1,0:T(4,128)S(1)}, s32[4,256]{1,0:T(4,128)S(1)}, ...), branch_computations={%region_60.63_spmd, %region_61.70_spmd} | conditional | flops 7544243712 | bytes 121205248 | solution.py:342
  892.1 18.1 %branch_1_fun.19 = bf16[1024,1024]{1,0:T(8,128)(2,1)S(1)} custom-call(bf16[1024,1024]{1,0:T(8,128)(2,1)} %get-tuple-element.369.packed_ref, bf16[1024,256]{1,0:T(8,128)(2,1)S(1)} %convolution_convert_fusion.9.grad_ref, f32[2,4,1,512]{3,2,1,0:T(1,128)S(1)} %get-tuple-element.372.log_ref, s32[1,1024]{1,0:T(1,128)S(1)} %bitcast.441, s32[1,1024]{1,0:T(1,128)S(1)} %bitcast.443, ...), custom_call_target="tpu_custom_call" | custom-call | flops 2684354560 | bytes 4194304 | tf_op jit(solution)/shard_map/cond/branch_1_fun/pallas_call | solution.py:250
  1025.9 24.1 %shard_map.529 = (f32[12576,256]{1,0:T(8,128)}, f32[1,256]{1,0:T(1,128)}) custom-call(s32[1]{0:T(128)} %bitcast.54.count_ref, s32[8192]{0:T(1024)} %get-tuple-element.742.list_ref, bf16[4,1600,256]{2,1,0:T(8,128)(2,1)} %pad_maximum_fusion.38.near_ref, bf16[4,1600,256]{2,1,0:T(8,128)(2,1)} %collective-permute-done.99.far_ref, ...), custom_call_target="tpu_custom_call" | custom-call | flops 12877824 | bytes 29949952 | tf_op jit(solution)/shard_map/pallas_call | solution.py:516
  1114.7 31.7 %multiply_subtract_fusion = (f32[12576,256]{1,0:T(8,128)}, f32[12576,256]{1,0:T(8,128)}, f32[12576,256]{1,0:T(8,128)}) fusion(f32[12576,256]{1,0:T(8,128)} %param.81, f32[12576,256]{1,0:T(8,128)} %get-tuple-element.753, f32[]{:T(128)S(6)} %div.278, f32[12576,256]{1,0:T(8,128)} %param.82, f32[12576,256]{1,0:T(8,128)} %param.83), kind=kLoop, calls=%fused_computation.212 | loop fusion | flops 51511296 | bytes 90144768 | tf_op jit(solution)/shard_map/sub | solution.py:562
  (980 shorter events, 810.6 us)
Async XLA Ops:
  7.3 53.8 %all-gather.5.cloned.1.call-start = ((), (), s32[]{:S(2)}) async-start(), calls=%async_computation.6 | async-start | bytes 2621440 | tf_op jit(solution)/shard_map/all_gather | solution.py:643
  10.0 114.8 %all-gather.7.cloned.1.call-start = ((), (), s32[]{:S(2)}) async-start(), calls=%async_computation.7 | async-start | bytes 2621440 | tf_op jit(solution)/shard_map/all_gather | solution.py:643
  19.4 182.2 %all-gather.9.cloned.1.call-start = ((), (), s32[]{:S(2)}) async-start(), calls=%async_computation.8 | async-start | bytes 2621440 | tf_op jit(solution)/shard_map/all_gather | solution.py:643
  61.1 244.7 %all-gather.11.cloned.1.call-start = ((), (), s32[]{:S(2)}) async-start(), calls=%async_computation.9 | async-start | bytes 2621440 | tf_op jit(solution)/shard_map/all_gather | solution.py:643
  68.2 47.2 %collective-permute-start.55 = (bf16[1024,1024]{1,0:T(8,128)(2,1)}, bf16[1024,1024]{1,0:T(8,128)(2,1)}, u32[]{:S(2)}, u32[]{:S(2)}) collective-permute-start(bf16[1024,1024]{1,0:T(8,128)(2,1)} %all-gather.5.cloned.1.call-done), channel_id=1, source_target_pairs={{0,16},{16,0},{1,17},{17,1},{2,18},{18,2},{3,19},{19,3},{4,20},{20... | collective-permute-start | bytes 6291464 | tf_op jit(solution)/shard_map/ppermute | solution.py:27
  93.2 770.5 %reduce-scatter.7.cloned.1.call-start = ((), (), s32[]{:S(2)}) async-start(), calls=%async_computation.10 | async-start | bytes 1310720 | tf_op jit(solution)/shard_map/reduce_scatter | solution.py:535
  124.7 72.3 %collective-permute-start.60 = (bf16[1024,1024]{1,0:T(8,128)(2,1)}, bf16[1024,1024]{1,0:T(8,128)(2,1)}, u32[]{:S(2)}, u32[]{:S(2)}) collective-permute-start(bf16[1024,1024]{1,0:T(8,128)(2,1)} %all-gather.7.cloned.1.call-done), channel_id=1, source_target_pairs={{0,16},{16,0},{1,17},{17,1},{2,18},{18,2},{3,19},{19,3},{4,20},{20... | collective-permute-start | bytes 6291464 | tf_op jit(solution)/shard_map/ppermute | solution.py:27
  192.5 113.3 %collective-permute-start.61 = (bf16[1600,256]{1,0:T(8,128)(2,1)}, bf16[1600,256]{1,0:T(8,128)(2,1)}, u32[]{:S(2)}, u32[]{:S(2)}) collective-permute-start(bf16[1600,256]{1,0:T(8,128)(2,1)} %get-tuple-element.601), channel_id=1, source_target_pairs={{0,4},{4,0},{8,12},{12,8},{1,5},{5,1},{9,13},{13,9},{2,6},{6,2},{1... | collective-permute-start | bytes 2457608 | tf_op jit(solution)/shard_map/ppermute | solution.py:27
  192.5 113.3 %collective-permute-start.62 = (bf16[1600,256]{1,0:T(8,128)(2,1)}, bf16[1600,256]{1,0:T(8,128)(2,1)}, u32[]{:S(2)}, u32[]{:S(2)}) collective-permute-start(bf16[1600,256]{1,0:T(8,128)(2,1)} %get-tuple-element.602), channel_id=1, source_target_pairs={{0,8},{4,12},{8,0},{12,4},{1,9},{5,13},{9,1},{13,5},{2,10},{6,14},... | collective-permute-start | bytes 2457608 | tf_op jit(solution)/shard_map/ppermute | solution.py:27
  195.2 110.6 %collective-permute-start.63 = (bf16[1600,256]{1,0:T(8,128)(2,1)}, bf16[1600,256]{1,0:T(8,128)(2,1)}, u32[]{:S(2)}, u32[]{:S(2)}) collective-permute-start(bf16[1600,256]{1,0:T(8,128)(2,1)} %get-tuple-element.603), channel_id=1, source_target_pairs={{0,12},{4,8},{8,4},{12,0},{1,13},{5,9},{9,5},{13,1},{2,14},{6,10},... | collective-permute-start | bytes 2457608 | tf_op jit(solution)/shard_map/ppermute | solution.py:27
  315.2 72.4 %collective-permute-start.65 = (bf16[1600,1024]{1,0:T(8,128)(2,1)}, bf16[1600,1024]{1,0:T(8,128)(2,1)}, u32[]{:S(2)}, u32[]{:S(2)}) collective-permute-start(bf16[1600,1024]{1,0:T(8,128)(2,1)} %constant_dynamic-update-slice_fusion.4), channel_id=1, source_target_pairs={{0,16},{16,0},{1,17},{17,1},{2,18},{18,2},{3,19},{19,3},{4,20},{20... | collective-permute-start | bytes 9830408 | tf_op jit(solution)/shard_map/ppermute | solution.py:27
  372.2 52.0 %collective-permute-start.67 = (bf16[256,1024]{1,0:T(8,128)(2,1)S(1)}, bf16[256,1024]{1,0:T(8,128)(2,1)}, u32[]{:S(2)}, u32[]{:S(2)}) collective-permute-start(bf16[256,1024]{1,0:T(8,128)(2,1)S(1)} %get-tuple-element.1041), channel_id=1, source_target_pairs={{0,8},{4,12},{8,0},{12,4},{1,9},{5,13},{9,1},{13,5},{2,10},{6,14},... | collective-permute-start | bytes 1572872 | tf_op jit(solution)/shard_map/ppermute | solution.py:27
  375.2 81.2 %collective-permute-start.68 = (bf16[256,1024]{1,0:T(8,128)(2,1)S(1)}, bf16[256,1024]{1,0:T(8,128)(2,1)S(1)}, u32[]{:S(2)}, u32[]{:S(2)}) collective-permute-start(bf16[256,1024]{1,0:T(8,128)(2,1)S(1)} %get-tuple-element.1041), channel_id=1, source_target_pairs={{0,12},{4,8},{8,4},{12,0},{1,13},{5,9},{9,5},{13,1},{2,14},{6,10},... | collective-permute-start | bytes 1572872 | tf_op jit(solution)/shard_map/ppermute | solution.py:27
  550.5 40.8 %collective-permute-start.82 = (bf16[256,1024]{1,0:T(8,128)(2,1)S(1)}, bf16[256,1024]{1,0:T(8,128)(2,1)}, u32[]{:S(2)}, u32[]{:S(2)}) collective-permute-start(bf16[256,1024]{1,0:T(8,128)(2,1)S(1)} %slice.806), channel_id=1, source_target_pairs={{0,2},{1,3},{2,0},{3,1},{4,6},{5,7},{6,4},{7,5},{8,10},{9,11},{10,... | collective-permute-start | bytes 1572872 | tf_op jit(solution)/shard_map/ppermute | solution.py:27
  554.2 37.1 %collective-permute-start.81 = (bf16[256,1024]{1,0:T(8,128)(2,1)}, bf16[256,1024]{1,0:T(8,128)(2,1)}, u32[]{:S(2)}, u32[]{:S(2)}) collective-permute-start(bf16[256,1024]{1,0:T(8,128)(2,1)} %slice.807), channel_id=1, source_target_pairs={{0,2},{1,3},{2,0},{3,1},{4,6},{5,7},{6,4},{7,5},{8,10},{9,11},{10,... | collective-permute-start | bytes 1572872 | tf_op jit(solution)/shard_map/ppermute | solution.py:27
  600.3 93.9 %collective-permute-start.87 = (bf16[1600,1024]{1,0:T(8,128)(2,1)}, bf16[1600,1024]{1,0:T(8,128)(2,1)}, u32[]{:S(2)}, u32[]{:S(2)}) collective-permute-start(bf16[1600,1024]{1,0:T(8,128)(2,1)} %slice.589), channel_id=1, source_target_pairs={{0,16},{16,0},{1,17},{17,1},{2,18},{18,2},{3,19},{19,3},{4,20},{20... | collective-permute-start | bytes 9830408 | tf_op jit(solution)/shard_map/ppermute | solution.py:27
  601.1 38.5 %collective-permute-start.84 = (bf16[256,1024]{1,0:T(8,128)(2,1)}, bf16[256,1024]{1,0:T(8,128)(2,1)}, u32[]{:S(2)}, u32[]{:S(2)}) collective-permute-start(bf16[256,1024]{1,0:T(8,128)(2,1)} %fusion.74), channel_id=1, source_target_pairs={{0,8},{4,12},{8,0},{12,4},{1,9},{5,13},{9,1},{13,5},{2,10},{6,14},... | collective-permute-start | bytes 1572872 | tf_op jit(solution)/shard_map/ppermute | solution.py:27
  603.2 36.5 %collective-permute-start.85 = (bf16[256,1024]{1,0:T(8,128)(2,1)}, bf16[256,1024]{1,0:T(8,128)(2,1)}, u32[]{:S(2)}, u32[]{:S(2)}) collective-permute-start(bf16[256,1024]{1,0:T(8,128)(2,1)} %fusion.73), channel_id=1, source_target_pairs={{0,12},{4,8},{8,4},{12,0},{1,13},{5,9},{9,5},{13,1},{2,14},{6,10},... | collective-permute-start | bytes 1572872 | tf_op jit(solution)/shard_map/ppermute | solution.py:27
  709.0 78.9 %collective-permute-start.90 = (bf16[1024,512]{0,1:T(8,128)(2,1)}, bf16[1024,512]{0,1:T(8,128)(2,1)}, u32[]{:S(2)}, u32[]{:S(2)}) collective-permute-start(bf16[1024,512]{0,1:T(8,128)(2,1)} %constant_dynamic-slice_fusion.12), channel_id=1, source_target_pairs={{0,16},{16,0},{1,17},{17,1},{2,18},{18,2},{3,19},{19,3},{4,20},{20... | collective-permute-start | bytes 3145736 | tf_op jit(solution)/shard_map/ppermute | solution.py:27
  710.1 77.7 %collective-permute-start.91 = (bf16[1024,512]{0,1:T(8,128)(2,1)}, bf16[1024,512]{0,1:T(8,128)(2,1)}, u32[]{:S(2)}, u32[]{:S(2)}) collective-permute-start(bf16[1024,512]{0,1:T(8,128)(2,1)} %constant_dynamic-slice_fusion.11), channel_id=1, source_target_pairs={{0,16},{16,0},{1,17},{17,1},{2,18},{18,2},{3,19},{19,3},{4,20},{20... | collective-permute-start | bytes 3145736 | tf_op jit(solution)/shard_map/ppermute | solution.py:27
  711.0 76.8 %collective-permute-start.88 = (bf16[1600,256]{1,0:T(8,128)(2,1)}, bf16[1600,256]{1,0:T(8,128)(2,1)}, u32[]{:S(2)}, u32[]{:S(2)}) collective-permute-start(bf16[1600,256]{1,0:T(8,128)(2,1)} %get-tuple-element.687), channel_id=1, source_target_pairs={{0,4},{4,0},{8,12},{12,8},{1,5},{5,1},{9,13},{13,9},{2,6},{6,2},{1... | collective-permute-start | bytes 2457608 | tf_op jit(solution)/shard_map/ppermute | solution.py:27
  723.3 64.5 %collective-permute-start.89 = (bf16[1600,256]{1,0:T(8,128)(2,1)}, bf16[1600,256]{1,0:T(8,128)(2,1)}, u32[]{:S(2)}, u32[]{:S(2)}) collective-permute-start(bf16[1600,256]{1,0:T(8,128)(2,1)} %get-tuple-element.688), channel_id=1, source_target_pairs={{0,8},{4,12},{8,0},{12,4},{1,9},{5,13},{9,1},{13,5},{2,10},{6,14},... | collective-permute-start | bytes 2457608 | tf_op jit(solution)/shard_map/ppermute | solution.py:27
  793.5 78.7 %reduce-scatter.9.cloned.1.call-start = ((), (), s32[]{:S(2)}) async-start(), calls=%async_computation.11 | async-start | bytes 1310720 | tf_op jit(solution)/shard_map/reduce_scatter | solution.py:535
  794.1 172.0 %reduce-scatter.13.cloned.1.call-start = ((), (), s32[]{:S(2)}) async-start(), calls=%async_computation.13 | async-start | bytes 2621440 | tf_op jit(solution)/shard_map/reduce_scatter | solution.py:535
  795.5 55.5 %collective-permute-start.93 = (bf16[1024,512]{0,1:T(8,128)(2,1)S(1)}, bf16[1024,512]{0,1:T(8,128)(2,1)}, u32[]{:S(2)}, u32[]{:S(2)}) collective-permute-start(bf16[1024,512]{0,1:T(8,128)(2,1)S(1)} %constant_dynamic-slice_fusion.9), channel_id=1, source_target_pairs={{0,16},{16,0},{1,17},{17,1},{2,18},{18,2},{3,19},{19,3},{4,20},{20... | collective-permute-start | bytes 3145736 | tf_op jit(solution)/shard_map/ppermute | solution.py:27
  796.8 54.1 %collective-permute-start.92 = (bf16[1600,256]{1,0:T(8,128)(2,1)}, bf16[1600,256]{1,0:T(8,128)(2,1)}, u32[]{:S(2)}, u32[]{:S(2)}) collective-permute-start(bf16[1600,256]{1,0:T(8,128)(2,1)} %get-tuple-element.704), channel_id=1, source_target_pairs={{0,12},{4,8},{8,4},{12,0},{1,13},{5,9},{9,5},{13,1},{2,14},{6,10},... | collective-permute-start | bytes 2457608 | tf_op jit(solution)/shard_map/ppermute | solution.py:27
  851.0 123.0 %reduce-scatter.17.cloned.1.call-start = ((), (), s32[]{:S(2)}) async-start(), calls=%async_computation.15 | async-start | bytes 2621440 | tf_op jit(solution)/shard_map/reduce_scatter | solution.py:535
  855.1 195.0 %reduce-scatter.11.cloned.1.call-start = ((), (), s32[]{:S(2)}) async-start(), calls=%async_computation.12 | async-start | bytes 1310720 | tf_op jit(solution)/shard_map/reduce_scatter | solution.py:535
  859.4 106.7 %collective-permute-start.99 = (bf16[4,1600,256]{2,1,0:T(8,128)(2,1)}, bf16[4,1600,256]{2,1,0:T(8,128)(2,1)}, u32[]{:S(2)}, u32[]{:S(2)}) collective-permute-start(bf16[4,1600,256]{2,1,0:T(8,128)(2,1)} %pad_maximum_fusion.38.near_ref), channel_id=1, source_target_pairs={{0,16},{16,0},{1,17},{17,1},{2,18},{18,2},{3,19},{19,3},{4,20},{20... | collective-permute-start | bytes 9830408 | tf_op jit(solution)/shard_map/ppermute | solution.py:27
  863.2 188.9 %reduce-scatter.15.cloned.1.call-start = ((), (), s32[]{:S(2)}) async-start(), calls=%async_computation.14 | async-start | bytes 1310720 | tf_op jit(solution)/shard_map/reduce_scatter | solution.py:535
  1014.5 45.4 %collective-permute-start.109 = (bf16[256,512]{0,1:T(8,128)(2,1)S(1)}, bf16[256,512]{0,1:T(8,128)(2,1)}, u32[]{:S(2)}, u32[]{:S(2)}) collective-permute-start(bf16[256,512]{0,1:T(8,128)(2,1)S(1)} %copy-done.96), channel_id=1, source_target_pairs={{0,16},{16,0},{1,17},{17,1},{2,18},{18,2},{3,19},{19,3},{4,20},{20... | collective-permute-start | bytes 786440 | tf_op jit(solution)/shard_map/ppermute | solution.py:27
  1015.0 37.9 %collective-permute-start.108 = (bf16[256,512]{0,1:T(8,128)(2,1)}, bf16[256,512]{0,1:T(8,128)(2,1)}, u32[]{:S(2)}, u32[]{:S(2)}) collective-permute-start(bf16[256,512]{0,1:T(8,128)(2,1)} %reduce-scatter.7.cloned.1.call-done), channel_id=1, source_target_pairs={{0,16},{16,0},{1,17},{17,1},{2,18},{18,2},{3,19},{19,3},{4,20},{20... | collective-permute-start | bytes 786440 | tf_op jit(solution)/shard_map/ppermute | solution.py:27
  (247 other events, 2815.3 us)
Sparse Core Ops, SparseCore 0:
  10.3 49.6 all-gather.4
  62.1 62.6 all-gather.6
  126.9 45.4 all-gather.8
  174.3 99.7 all-gather.10
  793.7 47.6 reduce-scatter.6
  844.2 27.9 reduce-scatter.8
  875.1 42.5 reduce-scatter.12
  920.1 51.4 reduce-scatter.16
  974.5 35.5 reduce-scatter.10
  1012.9 26.2 reduce-scatter.14

commit v5 on v4

--- a/solution.py
+++ b/solution.py
@@ -874,18 +874,18 @@
     attn_early = scatter_over(attn_early, "dp")
     back_other = swap(back, "pipe", 1)
     own_rows = spread(back)
-    back_other, feed_early[1], position_sent = together(
-        back_other, feed_early[1], position_sent
-    )
-    position_part = sum(
-        part.astype(F32)
-        for part in exchange_blocks(take_columns(position_sent, replica, replicas), "dp")
-    )
-    position_grad = position_part + swap(position_part, "pipe", 1)
+    back_other, feed_early[1] = together(back_other, feed_early[1])
     other_rows = spread(back_other)
+    position_sent = after(position_sent, other_rows)
+    position_parts = exchange_blocks(take_columns(position_sent, replica, replicas), "dp")
     table_grad, table_square = scatter_rows(
         back_listing, back_count, half_back, half_far, own_rows, other_rows, slice_rows
     )
+
+    position_part = sum(
+        after(part, table_square).astype(F32) for part in position_parts
+    )
+    position_grad = position_part + swap(position_part, "pipe", 1)
 
     feed_coming = [swap(part, "pipe", 1) for part in feed_early]
     attn_late, attn_early, *feed_coming = together(

time: 1170 us -> 1170 us (level)
    unnamed x211 -> x235, local copies, waits for them, and re-layouts: 22.5 us -> 24 us
    concatenate x20 -> x19, other arithmetic: 23 us -> 23.8 us  [spread(): block = jnp.concatenate([block, received], 0)]
  transfers between devices with their start and end apart: 134 -> 134, of which waited for: 67 -> 63; matrix products, arithmetic and copies ran while one was open for 26% -> 27% of each run, Pallas kernels for 16% -> 16%
where the time goes in v5:
time: 1170 us; the launch traced here: 1160 us
  waiting for transfers between devices  324 us (28%)
  other arithmetic  212 us (18%)
  Pallas kernels  212 us (18%)
  starting transfers between devices  149 us (13%)
  local copies, waits for them, and re-layouts  135 us (12%)
  matrix products  100 us (9%)
  between operations  24.1 us (2%)
    ppermute x105, waiting for transfers between devices, swap(): return lax.ppermute(block, axis, route)  296 us
    ppermute x105, starting transfers between devices, swap(): return lax.ppermute(block, axis, route)  123 us
    pallas_call x4, Pallas kernels, head_block(): pl.pallas_call(head_kernel, grid=(length // tile,), in_specs=[pl.BlockSpe...  84.8 us
    sub x8, other arithmetic, adamw_update(): return (master - rate * (ratio + decay * master), first_new, second_new)  44.2 us
    pallas_call x2, Pallas kernels, table_gradient_of(): pl.pallas_call(lambda *refs: table_kernel(count, *refs), grid=(count_tile...  41.4 us
    pallas_call x2, Pallas kernels, attend_backward(): pl.pallas_call(attend_back_kernel, grid=(steps,), in_specs=[pl.BlockSpec(...  36.1 us
    pallas_call x1, Pallas kernels, scatter_rows(): pl.pallas_call(scatter_kernel, in_specs=[scalars, scalars, whole, whole,...  27.2 us
    cond x126, local copies, waits for them, and re-layouts  27.2 us
  transfers between devices with their start and end apart: 134, of which 63 were waited for; matrix products, arithmetic and copies ran while one was open for 27% of the time, Pallas kernels for 16%

profile of v5, /device:TPU:0, one launch (start us, length us, event | category | flops | bytes accessed | tf_op | source)
XLA Modules:
  0.0 1156.9 jit_solution(9232736287669969733)
XLA Ops:
  32.4 20.6 %gather_fusion.1 = bf16[4096,256]{1,0:T(8,128)(2,1)} fusion(f32[12576,256]{1,0:T(8,128)} %param.81, s32[4096]{0:T(1024)S(1)} %broadcast_clamp_fusion), kind=kCustom, calls=%fused_computation.7 | custom fusion | bytes 4210688 | tf_op jit(solution)/shard_map/jit(_take)/gather | solution.py:651
  131.0 56.2 %conditional.14 = (f32[256,1024]{1,0:T(8,128)S(1)}, f32[256,1024]{1,0:T(8,128)S(1)}, bf16[1024,1024]{1,0:T(8,128)(2,1)}, bf16[1024,1024]{1,0:T(8,128)(2,1)}, f32...) conditional(s32[]{:T(128)} %convert_element_type.465, () %tuple.211, (f32[256,1024]{1,0:T(8,128)S(1)}, ...), branch_computations={%region_2.3_spmd, %region_3.6_spmd} | conditional | flops 3771728128 | bytes 59311372 | solution.py:342
  133.3 12.1 %collective-permute-done.7 = bf16[256,1024]{1,0:T(8,128)(2,1)S(1)} collective-permute-done((bf16[256,1024]{1,0:T(8,128)(2,1)S(1)}, bf16[256,1024]{1,0:T(8,128)(2,1)S(1)}, u32[]{:S(2)}, u32[]{:S(2)}) %collective-permute-start.7) | collective-permute-done | bytes 524320 | tf_op jit(solution)/shard_map/cond/branch_1_fun/ppermute | solution.py:27
  174.5 12.4 %collective-permute-done.10 = bf16[256,1024]{1,0:T(8,128)(2,1)S(1)} collective-permute-done((bf16[256,1024]{1,0:T(8,128)(2,1)S(1)}, bf16[256,1024]{1,0:T(8,128)(2,1)S(1)}, u32[]{:S(2)}, u32[]{:S(2)}) %collective-permute-start.10) | collective-permute-done | bytes 524320 | tf_op jit(solution)/shard_map/cond/branch_1_fun/ppermute | solution.py:27
  201.6 46.5 %conditional.15 = (f32[256,1024]{1,0:T(8,128)S(1)}, f32[256,1024]{1,0:T(8,128)S(1)}, bf16[1024,1024]{1,0:T(8,128)(2,1)}, f32[1024,1024]{1,0:T(8,128)}, bf16[1024,1024]{1,0:T(8,128)(2,1)}) conditional(s32[]{:T(128)} %convert_element_type.465, () %tuple.210, (f32[256,1024]{1,0:T(8,128)S(1)}, f32[4,1024]{1,0:T(4,128)S(1)}, ...), branch_computations={%region_6.7_spmd, %region_7.10_spmd} | conditional | flops 4316987392 | bytes 70288648 | solution.py:342
  235.4 12.4 %collective-permute-done.14 = bf16[256,1024]{1,0:T(8,128)(2,1)S(1)} collective-permute-done((bf16[256,1024]{1,0:T(8,128)(2,1)S(1)}, bf16[256,1024]{1,0:T(8,128)(2,1)S(1)}, u32[]{:S(2)}, u32[]{:S(2)}) %collective-permute-start.14) | collective-permute-done | bytes 524320 | tf_op jit(solution)/shard_map/cond/branch_1_fun/ppermute | solution.py:27
  249.1 56.7 %conditional.16 = (f32[256,1024]{1,0:T(8,128)S(1)}, f32[256,1024]{1,0:T(8,128)S(1)}, bf16[1024,1024]{1,0:T(8,128)(2,1)}, bf16[1024,1024]{1,0:T(8,128)(2,1)}, f32...) conditional(s32[]{:T(128)} %convert_element_type.465, () %tuple.209, (f32[256,1024]{1,0:T(8,128)S(1)}, ...), branch_computations={%region_10.11_spmd, %region_11.14_spmd} | conditional | flops 3771728128 | bytes 57214192 | solution.py:342
  293.1 12.4 %collective-permute-done.18 = bf16[256,1024]{1,0:T(8,128)(2,1)S(1)} collective-permute-done((bf16[256,1024]{1,0:T(8,128)(2,1)S(1)}, bf16[256,1024]{1,0:T(8,128)(2,1)S(1)}, u32[]{:S(2)}, u32[]{:S(2)}) %collective-permute-start.18) | collective-permute-done | bytes 524320 | tf_op jit(solution)/shard_map/cond/branch_1_fun/ppermute | solution.py:27
  317.8 49.1 %conditional.17 = (f32[256,1024]{0,1:T(8,128)S(1)}, bf16[1024,1024]{0,1:T(8,128)(2,1)}, f32[1024,1024]{1,0:T(8,128)}, bf16[1024,1024]{1,0:T(8,128)(2,1)}, f32[256,1]{0,1:T(1,128)S(1)}, /*index=5*/f32[256,1024]{1,0:T(8,128)S(1)}) conditional(s32[]{:T(128)} %convert_element_type.465, () %tuple.208, (f32[256,1024]{1,0:T(8,128)S(1)}, ...), branch_computations={%region_14.15_spmd, %region_15.19_spmd} | conditional | flops 4317249536 | bytes 82872648 | solution.py:342
  352.8 12.5 %collective-permute-done.22 = bf16[256,1024]{0,1:T(8,128)(2,1)S(1)} collective-permute-done((bf16[256,1024]{0,1:T(8,128)(2,1)S(1)}, bf16[256,1024]{0,1:T(8,128)(2,1)S(1)}, u32[]{:S(2)}, u32[]{:S(2)}) %collective-permute-start.22) | collective-permute-done | bytes 524320 | tf_op jit(solution)/shard_map/cond/branch_1_fun/ppermute | solution.py:27
  395.4 28.8 %conditional.18 = (bf16[1024,3200]{1,0:T(8,128)(2,1)}, bf16[1024,1024]{1,0:T(8,128)(2,1)}, f32[1,1024]{1,0:T(1,128)}, f32[1,1024]{1,0:T(1,128)}, bf16[512,1024]{...) conditional(s32[]{:T(128)} %convert_element_type.465, ...), branch_computations={%region_20.21_spmd, %region_21.22_spmd} | conditional | flops 13424918528 | bytes 46694652 | solution.py:342
  399.3 20.9 %branch_1_fun.12 = (bf16[1024,3200]{1,0:T(8,128)(2,1)}, bf16[1024,1024]{1,0:T(8,128)(2,1)}, f32[1,1024]{1,0:T(1,128)}, f32[1,1024]{1,0:T(1,128)}) custom-call(bf16[512,1024]{1,0:T(8,128)(2,1)} %copy-done.53, bf16[512,1024]{1,0:T(8,128)(2,1)} %copy-done.92, bf16[3200,1024]{1,0:T(8,128)(2,1)} %get-tuple-element.281.table_ref, ...), custom_call_target="tpu_custom_call" | custom-call | flops 13421772800 | bytes 19398656 | tf_op jit(solution)/shard_map/cond/branch_1_fun/pallas_call | solution.py:400
  426.2 30.3 %conditional.19 = (bf16[1024,3200]{1,0:T(8,128)(2,1)}, bf16[1024,1024]{1,0:T(8,128)(2,1)}, f32[1,1024]{1,0:T(1,128)}, f32[1,1024]{1,0:T(1,128)}, bf16[512,1024]{...) conditional(s32[]{:T(128)} %convert_element_type.465, ...), branch_computations={%region_22.23_spmd, %region_23.24_spmd} | conditional | flops 13424918528 | bytes 42500320 | solution.py:342
  430.1 21.3 %branch_1_fun.13 = (bf16[1024,3200]{1,0:T(8,128)(2,1)}, bf16[1024,1024]{1,0:T(8,128)(2,1)}, f32[1,1024]{1,0:T(1,128)}, f32[1,1024]{1,0:T(1,128)}) custom-call(bf16[512,1024]{1,0:T(8,128)(2,1)} %get-tuple-element.289.first_ref, bf16[512,1024]{1,0:T(8,128)(2,1)} %copy-done.94, bf16[3200,1024]{1,0:T(8,128)(2,1)} %get-tuple-element.290.table_ref, ...), custom_call_target="tpu_custom_call" | custom-call | flops 13421772800 | bytes 19398656 | tf_op jit(solution)/shard_map/cond/branch_1_fun/pallas_call | solution.py:400
  458.6 29.4 %conditional.20 = (bf16[1024,3200]{1,0:T(8,128)(2,1)}, bf16[1024,1024]{1,0:T(8,128)(2,1)}, f32[1,1024]{1,0:T(1,128)}, f32[1,1024]{1,0:T(1,128)}, bf16[512,1024]{...) conditional(s32[]{:T(128)} %convert_element_type.465, ...), branch_computations={%region_24.25_spmd, %region_25.26_spmd} | conditional | flops 13424918528 | bytes 42500320 | solution.py:342
  462.5 21.5 %branch_1_fun.14 = (bf16[1024,3200]{1,0:T(8,128)(2,1)}, bf16[1024,1024]{1,0:T(8,128)(2,1)}, f32[1,1024]{1,0:T(1,128)}, f32[1,1024]{1,0:T(1,128)}) custom-call(bf16[512,1024]{1,0:T(8,128)(2,1)} %get-tuple-element.298.first_ref, bf16[512,1024]{1,0:T(8,128)(2,1)} %copy-done.96, bf16[3200,1024]{1,0:T(8,128)(2,1)} %get-tuple-element.299.table_ref, ...), custom_call_target="tpu_custom_call" | custom-call | flops 13421772800 | bytes 19398656 | tf_op jit(solution)/shard_map/cond/branch_1_fun/pallas_call | solution.py:400
  490.1 30.6 %conditional.21 = (bf16[1024,3200]{1,0:T(8,128)(2,1)}, bf16[1024,1024]{1,0:T(8,128)(2,1)}, f32[1,1024]{1,0:T(1,128)}, f32[1,1024]{1,0:T(1,128)}, f32[512,1024]{1...) conditional(s32[]{:T(128)} %convert_element_type.465, ...), branch_computations={%region_26.27_spmd, %region_27.28_spmd} | conditional | flops 13422821376 | bytes 34111636 | solution.py:342
  494.0 21.2 %branch_1_fun.15 = (bf16[1024,3200]{1,0:T(8,128)(2,1)}, bf16[1024,1024]{1,0:T(8,128)(2,1)}, f32[1,1024]{1,0:T(1,128)}, f32[1,1024]{1,0:T(1,128)}) custom-call(bf16[512,1024]{1,0:T(8,128)(2,1)} %get-tuple-element.307.first_ref, bf16[512,1024]{1,0:T(8,128)(2,1)} %copy-done.98, bf16[3200,1024]{1,0:T(8,128)(2,1)} %get-tuple-element.308.table_ref, ...), custom_call_target="tpu_custom_call" | custom-call | flops 13421772800 | bytes 19398656 | tf_op jit(solution)/shard_map/cond/branch_1_fun/pallas_call | solution.py:400
  563.5 23.7 %conditional.22 = (bf16[1920,1024]{1,0:T(8,128)(2,1)}) conditional(s32[]{:T(128)} %convert_element_type.465, () %tuple.206, (bf16[1024,3200]{1,0:T(8,128)(2,1)}, bf16[1024,3200]{1,0:T(8,128)(2,1)}, bf16[1024,3200]{1,0:T(8,128)(2,1)}, bf16[1024,3200]{1,0:T(8,128)(2,1)}, bf16[512,1024]{1,0:T(8,128)(2,1)}, /*index=5*/bf16[512,1024]{1,0:T(8,128)(2,1)}, ...), branch_computations={%region_28.31_spmd, %region_29.32_spmd} | conditional | flops 16106127360 | bytes 28049416 | solution.py:342
  563.5 23.7 %branch_1_fun.16 = bf16[1920,1024]{1,0:T(8,128)(2,1)} custom-call(bf16[1024,3200]{1,0:T(8,128)(2,1)} %get-tuple-element.314.refs_0_, bf16[1024,3200]{1,0:T(8,128)(2,1)} %get-tuple-element.315.refs_1_, bf16[1024,3200]{1,0:T(8,128)(2,1)} %get-tuple-element.316.refs_2_, bf16[1024,3200]{1,0:T(8,128)(2,1)} %get-tuple-element.317.refs_3_, ...), custom_call_target="tpu_custom_call" | custom-call | flops 16106127360 | bytes 28049408 | tf_op jit(solution)/shard_map/cond/branch_1_fun/pallas_call | solution.py:449
  609.8 17.7 %conditional.23 = (bf16[1280,1024]{1,0:T(8,128)(2,1)}) conditional(s32[]{:T(128)} %convert_element_type.465, () %tuple.245, (bf16[1024,3200]{1,0:T(8,128)(2,1)}, bf16[1024,3200]{1,0:T(8,128)(2,1)}, bf16[1024,3200]{1,0:T(8,128)(2,1)}, bf16[1024,3200]{1,0:T(8,128)(2,1)}, bf16[512,1024]{1,0:T(8,128)(2,1)}, /*index=5*/bf16[512,1024]{1,0:T(8,128)(2,1)}, ...), branch_computations={%region_30.33_spmd, %region_31.34_spmd} | conditional | flops 10737418240 | bytes 21495816 | solution.py:342
  609.8 17.7 %branch_1_fun.17 = bf16[1280,1024]{1,0:T(8,128)(2,1)} custom-call(bf16[1024,3200]{1,0:T(8,128)(2,1)} %get-tuple-element.326.refs_0_, bf16[1024,3200]{1,0:T(8,128)(2,1)} %get-tuple-element.327.refs_1_, bf16[1024,3200]{1,0:T(8,128)(2,1)} %get-tuple-element.328.refs_2_, bf16[1024,3200]{1,0:T(8,128)(2,1)} %get-tuple-element.329.refs_3_, ...), custom_call_target="tpu_custom_call" | custom-call | flops 10737418240 | bytes 21495808 | tf_op jit(solution)/shard_map/cond/branch_1_fun/pallas_call | solution.py:449
  627.5 12.2 %collective-permute-done.84 = bf16[256,1024]{1,0:T(8,128)(2,1)} collective-permute-done((bf16[256,1024]{1,0:T(8,128)(2,1)}, bf16[256,1024]{1,0:T(8,128)(2,1)}, u32[]{:S(2)}, u32[]{:S(2)}) %collective-permute-start.84) | collective-permute-done | bytes 524320 | tf_op jit(solution)/shard_map/ppermute | solution.py:27
  642.7 52.1 %conditional.24 = (f32[256,1024]{1,0:T(8,128)S(1)}, bf16[1024,1024]{0,1:T(8,128)(2,1)S(1)}, bf16[1024,1024]{1,0:T(8,128)(2,1)}, f32[2,1024]{1,0:T(2,128)S(1)}) conditional(s32[]{:T(128)} %convert_element_type.465, () %tuple.205, (f32[256,1024]{1,0:T(8,128)S(1)}, f32[256,1024]{1,0:T(8,128)S(1)}, f32[256]{0:T(256)S(1)}, f32[256,1024]{1,0:T(8,128)S(1)}, ...), branch_computations={%region_32.35_spmd, %region_33.44_spmd} | conditional | flops 8638433280 | bytes 144255392 | solution.py:342
  711.7 12.3 %collective-permute-start.88 = (bf16[1600,256]{1,0:T(8,128)(2,1)}, bf16[1600,256]{1,0:T(8,128)(2,1)}, u32[]{:S(2)}, u32[]{:S(2)}) collective-permute-start(bf16[1600,256]{1,0:T(8,128)(2,1)} %get-tuple-element.691), channel_id=1, source_target_pairs={{0,4},{4,0},{8,12},{12,8},{1,5},{5,1},{9,13},{13,9},{2,6},{6,2},{1... | collective-permute-start | bytes 2457608 | tf_op jit(solution)/shard_map/ppermute | solution.py:27
  724.0 64.5 %conditional.25 = (f32[256,1024]{1,0:T(8,128)}, bf16[1024,1024]{0,1:T(8,128)(2,1)}, f32[2,1024]{1,0:T(2,128)S(1)}) conditional(s32[]{:T(128)} %convert_element_type.465, () %tuple.204, (f32[256,1024]{1,0:T(8,128)S(1)}, bf16[1024,1024]{1,0:T(8,128)(2,1)}, s32[4,256]{1,0:T(4,128)S(1)}, s32[4,256]{1,0:T(4,128)S(1)}, bf16[1024,1024]{1,0:T(8,128)(2,1)}, ...), branch_computations={%region_42.45_spmd, %region_43.52_spmd} | conditional | flops 7544243712 | bytes 110719424 | solution.py:342
  742.7 18.1 %branch_1_fun.18 = bf16[1024,1024]{1,0:T(8,128)(2,1)S(1)} custom-call(bf16[1024,1024]{1,0:T(8,128)(2,1)} %get-tuple-element.351.packed_ref, bf16[1024,256]{1,0:T(8,128)(2,1)S(1)} %convolution_convert_fusion.5.grad_ref, f32[2,4,1,512]{3,2,1,0:T(1,128)S(1)} %get-tuple-element.354.log_ref, s32[1,1024]{1,0:T(1,128)S(1)} %bitcast.437, s32[1,1024]{1,0:T(1,128)S(1)} %bitcast.439, ...), custom_call_target="tpu_custom_call" | custom-call | flops 2684354560 | bytes 4194304 | tf_op jit(solution)/shard_map/cond/branch_1_fun/pallas_call | solution.py:250
  799.7 51.9 %conditional.26 = (f32[256,1024]{1,0:T(8,128)S(1)}, bf16[1024,1024]{0,1:T(8,128)(2,1)}, bf16[1024,1024]{1,0:T(8,128)(2,1)}, f32[2,1024]{1,0:T(2,128)S(1)}) conditional(s32[]{:T(128)} %convert_element_type.465, () %tuple.203, (f32[256,1024]{1,0:T(8,128)}, bf16[1024,1024]{0,1:T(8,128)(2,1)}, f32[1024,1024]{1,0:T(8,128)}, ...), branch_computations={%region_50.53_spmd, %region_51.60_spmd} | conditional | flops 8635549696 | bytes 80277784 | solution.py:342
  872.9 65.7 %conditional.27 = (f32[256,1024]{1,0:T(8,128)}, bf16[1024,1024]{0,1:T(8,128)(2,1)S(1)}, f32[2,1024]{1,0:T(2,128)S(1)}) conditional(s32[]{:T(128)} %convert_element_type.465, () %tuple.202, (f32[256,1024]{1,0:T(8,128)S(1)}, bf16[1024,1024]{1,0:T(8,128)(2,1)}, s32[4,256]{1,0:T(4,128)S(1)}, s32[4,256]{1,0:T(4,128)S(1)}, ...), branch_computations={%region_60.63_spmd, %region_61.70_spmd} | conditional | flops 7544243712 | bytes 121205248 | solution.py:342
  892.8 18.1 %branch_1_fun.19 = bf16[1024,1024]{1,0:T(8,128)(2,1)S(1)} custom-call(bf16[1024,1024]{1,0:T(8,128)(2,1)} %get-tuple-element.369.packed_ref, bf16[1024,256]{1,0:T(8,128)(2,1)S(1)} %convolution_convert_fusion.9.grad_ref, f32[2,4,1,512]{3,2,1,0:T(1,128)S(1)} %get-tuple-element.372.log_ref, s32[1,1024]{1,0:T(1,128)S(1)} %bitcast.441, s32[1,1024]{1,0:T(1,128)S(1)} %bitcast.443, ...), custom_call_target="tpu_custom_call" | custom-call | flops 2684354560 | bytes 4194304 | tf_op jit(solution)/shard_map/cond/branch_1_fun/pallas_call | solution.py:250
  1017.6 27.2 %shard_map.529 = (f32[12576,256]{1,0:T(8,128)}, f32[1,256]{1,0:T(1,128)}) custom-call(s32[1]{0:T(128)} %bitcast.54.count_ref, s32[8192]{0:T(1024)} %get-tuple-element.746.list_ref, bf16[4,1600,256]{2,1,0:T(8,128)(2,1)} %pad_maximum_fusion.38.near_ref, bf16[4,1600,256]{2,1,0:T(8,128)(2,1)} %collective-permute-done.99.far_ref, ...), custom_call_target="tpu_custom_call" | custom-call | flops 12877824 | bytes 29949952 | tf_op jit(solution)/shard_map/pallas_call | solution.py:516
  1110.6 31.7 %multiply_subtract_fusion = (f32[12576,256]{1,0:T(8,128)}, f32[12576,256]{1,0:T(8,128)}, f32[12576,256]{1,0:T(8,128)}) fusion(f32[12576,256]{1,0:T(8,128)} %param.81, f32[12576,256]{1,0:T(8,128)} %get-tuple-element.761, f32[]{:T(128)S(6)} %div.278, f32[12576,256]{1,0:T(8,128)} %param.82, f32[12576,256]{1,0:T(8,128)} %param.83), kind=kLoop, calls=%fused_computation.212 | loop fusion | flops 51511296 | bytes 90144768 | tf_op jit(solution)/shard_map/sub | solution.py:562
  (1004 shorter events, 803.3 us)
Async XLA Ops:
  7.3 53.8 %all-gather.5.cloned.1.call-start = ((), (), s32[]{:S(2)}) async-start(), calls=%async_computation.6 | async-start | bytes 2621440 | tf_op jit(solution)/shard_map/all_gather | solution.py:643
  10.0 114.8 %all-gather.7.cloned.1.call-start = ((), (), s32[]{:S(2)}) async-start(), calls=%async_computation.7 | async-start | bytes 2621440 | tf_op jit(solution)/shard_map/all_gather | solution.py:643
  19.4 182.2 %all-gather.9.cloned.1.call-start = ((), (), s32[]{:S(2)}) async-start(), calls=%async_computation.8 | async-start | bytes 2621440 | tf_op jit(solution)/shard_map/all_gather | solution.py:643
  61.1 244.8 %all-gather.11.cloned.1.call-start = ((), (), s32[]{:S(2)}) async-start(), calls=%async_computation.9 | async-start | bytes 2621440 | tf_op jit(solution)/shard_map/all_gather | solution.py:643
  68.2 47.2 %collective-permute-start.55 = (bf16[1024,1024]{1,0:T(8,128)(2,1)}, bf16[1024,1024]{1,0:T(8,128)(2,1)}, u32[]{:S(2)}, u32[]{:S(2)}) collective-permute-start(bf16[1024,1024]{1,0:T(8,128)(2,1)} %all-gather.5.cloned.1.call-done), channel_id=1, source_target_pairs={{0,16},{16,0},{1,17},{17,1},{2,18},{18,2},{3,19},{19,3},{4,20},{20... | collective-permute-start | bytes 6291464 | tf_op jit(solution)/shard_map/ppermute | solution.py:27
  93.2 771.1 %reduce-scatter.7.cloned.1.call-start = ((), (), s32[]{:S(2)}) async-start(), calls=%async_computation.10 | async-start | bytes 1310720 | tf_op jit(solution)/shard_map/reduce_scatter | solution.py:535
  124.7 72.3 %collective-permute-start.60 = (bf16[1024,1024]{1,0:T(8,128)(2,1)}, bf16[1024,1024]{1,0:T(8,128)(2,1)}, u32[]{:S(2)}, u32[]{:S(2)}) collective-permute-start(bf16[1024,1024]{1,0:T(8,128)(2,1)} %all-gather.7.cloned.1.call-done), channel_id=1, source_target_pairs={{0,16},{16,0},{1,17},{17,1},{2,18},{18,2},{3,19},{19,3},{4,20},{20... | collective-permute-start | bytes 6291464 | tf_op jit(solution)/shard_map/ppermute | solution.py:27
  192.6 113.3 %collective-permute-start.61 = (bf16[1600,256]{1,0:T(8,128)(2,1)}, bf16[1600,256]{1,0:T(8,128)(2,1)}, u32[]{:S(2)}, u32[]{:S(2)}) collective-permute-start(bf16[1600,256]{1,0:T(8,128)(2,1)} %get-tuple-element.605), channel_id=1, source_target_pairs={{0,4},{4,0},{8,12},{12,8},{1,5},{5,1},{9,13},{13,9},{2,6},{6,2},{1... | collective-permute-start | bytes 2457608 | tf_op jit(solution)/shard_map/ppermute | solution.py:27
  192.6 113.3 %collective-permute-start.62 = (bf16[1600,256]{1,0:T(8,128)(2,1)}, bf16[1600,256]{1,0:T(8,128)(2,1)}, u32[]{:S(2)}, u32[]{:S(2)}) collective-permute-start(bf16[1600,256]{1,0:T(8,128)(2,1)} %get-tuple-element.606), channel_id=1, source_target_pairs={{0,8},{4,12},{8,0},{12,4},{1,9},{5,13},{9,1},{13,5},{2,10},{6,14},... | collective-permute-start | bytes 2457608 | tf_op jit(solution)/shard_map/ppermute | solution.py:27
  195.3 110.6 %collective-permute-start.63 = (bf16[1600,256]{1,0:T(8,128)(2,1)}, bf16[1600,256]{1,0:T(8,128)(2,1)}, u32[]{:S(2)}, u32[]{:S(2)}) collective-permute-start(bf16[1600,256]{1,0:T(8,128)(2,1)} %get-tuple-element.607), channel_id=1, source_target_pairs={{0,12},{4,8},{8,4},{12,0},{1,13},{5,9},{9,5},{13,1},{2,14},{6,10},... | collective-permute-start | bytes 2457608 | tf_op jit(solution)/shard_map/ppermute | solution.py:27
  315.2 72.4 %collective-permute-start.65 = (bf16[1600,1024]{1,0:T(8,128)(2,1)}, bf16[1600,1024]{1,0:T(8,128)(2,1)}, u32[]{:S(2)}, u32[]{:S(2)}) collective-permute-start(bf16[1600,1024]{1,0:T(8,128)(2,1)} %constant_dynamic-update-slice_fusion.7), channel_id=1, source_target_pairs={{0,16},{16,0},{1,17},{17,1},{2,18},{18,2},{3,19},{19,3},{4,20},{20... | collective-permute-start | bytes 9830408 | tf_op jit(solution)/shard_map/ppermute | solution.py:27
  372.3 52.0 %collective-permute-start.67 = (bf16[256,1024]{1,0:T(8,128)(2,1)S(1)}, bf16[256,1024]{1,0:T(8,128)(2,1)}, u32[]{:S(2)}, u32[]{:S(2)}) collective-permute-start(bf16[256,1024]{1,0:T(8,128)(2,1)S(1)} %get-tuple-element.1049), channel_id=1, source_target_pairs={{0,8},{4,12},{8,0},{12,4},{1,9},{5,13},{9,1},{13,5},{2,10},{6,14},... | collective-permute-start | bytes 1572872 | tf_op jit(solution)/shard_map/ppermute | solution.py:27
  375.3 81.3 %collective-permute-start.68 = (bf16[256,1024]{1,0:T(8,128)(2,1)S(1)}, bf16[256,1024]{1,0:T(8,128)(2,1)S(1)}, u32[]{:S(2)}, u32[]{:S(2)}) collective-permute-start(bf16[256,1024]{1,0:T(8,128)(2,1)S(1)} %get-tuple-element.1049), channel_id=1, source_target_pairs={{0,12},{4,8},{8,4},{12,0},{1,13},{5,9},{9,5},{13,1},{2,14},{6,10},... | collective-permute-start | bytes 1572872 | tf_op jit(solution)/shard_map/ppermute | solution.py:27
  550.6 40.8 %collective-permute-start.82 = (bf16[256,1024]{1,0:T(8,128)(2,1)S(1)}, bf16[256,1024]{1,0:T(8,128)(2,1)}, u32[]{:S(2)}, u32[]{:S(2)}) collective-permute-start(bf16[256,1024]{1,0:T(8,128)(2,1)S(1)} %slice.806), channel_id=1, source_target_pairs={{0,2},{1,3},{2,0},{3,1},{4,6},{5,7},{6,4},{7,5},{8,10},{9,11},{10,... | collective-permute-start | bytes 1572872 | tf_op jit(solution)/shard_map/ppermute | solution.py:27
  600.3 94.5 %collective-permute-start.87 = (bf16[1600,1024]{1,0:T(8,128)(2,1)}, bf16[1600,1024]{1,0:T(8,128)(2,1)}, u32[]{:S(2)}, u32[]{:S(2)}) collective-permute-start(bf16[1600,1024]{1,0:T(8,128)(2,1)} %slice.589), channel_id=1, source_target_pairs={{0,16},{16,0},{1,17},{17,1},{2,18},{18,2},{3,19},{19,3},{4,20},{20... | collective-permute-start | bytes 9830408 | tf_op jit(solution)/shard_map/ppermute | solution.py:27
  709.6 78.9 %collective-permute-start.90 = (bf16[1024,512]{0,1:T(8,128)(2,1)}, bf16[1024,512]{0,1:T(8,128)(2,1)}, u32[]{:S(2)}, u32[]{:S(2)}) collective-permute-start(bf16[1024,512]{0,1:T(8,128)(2,1)} %constant_dynamic-slice_fusion.13), channel_id=1, source_target_pairs={{0,16},{16,0},{1,17},{17,1},{2,18},{18,2},{3,19},{19,3},{4,20},{20... | collective-permute-start | bytes 3145736 | tf_op jit(solution)/shard_map/ppermute | solution.py:27
  710.8 77.7 %collective-permute-start.91 = (bf16[1024,512]{0,1:T(8,128)(2,1)}, bf16[1024,512]{0,1:T(8,128)(2,1)}, u32[]{:S(2)}, u32[]{:S(2)}) collective-permute-start(bf16[1024,512]{0,1:T(8,128)(2,1)} %constant_dynamic-slice_fusion.12), channel_id=1, source_target_pairs={{0,16},{16,0},{1,17},{17,1},{2,18},{18,2},{3,19},{19,3},{4,20},{20... | collective-permute-start | bytes 3145736 | tf_op jit(solution)/shard_map/ppermute | solution.py:27
  711.7 76.9 %collective-permute-start.88 = (bf16[1600,256]{1,0:T(8,128)(2,1)}, bf16[1600,256]{1,0:T(8,128)(2,1)}, u32[]{:S(2)}, u32[]{:S(2)}) collective-permute-start(bf16[1600,256]{1,0:T(8,128)(2,1)} %get-tuple-element.691), channel_id=1, source_target_pairs={{0,4},{4,0},{8,12},{12,8},{1,5},{5,1},{9,13},{13,9},{2,6},{6,2},{1... | collective-permute-start | bytes 2457608 | tf_op jit(solution)/shard_map/ppermute | solution.py:27
  724.0 64.6 %collective-permute-start.89 = (bf16[1600,256]{1,0:T(8,128)(2,1)}, bf16[1600,256]{1,0:T(8,128)(2,1)}, u32[]{:S(2)}, u32[]{:S(2)}) collective-permute-start(bf16[1600,256]{1,0:T(8,128)(2,1)} %get-tuple-element.692), channel_id=1, source_target_pairs={{0,8},{4,12},{8,0},{12,4},{1,9},{5,13},{9,1},{13,5},{2,10},{6,14},... | collective-permute-start | bytes 2457608 | tf_op jit(solution)/shard_map/ppermute | solution.py:27
  794.3 78.7 %reduce-scatter.9.cloned.1.call-start = ((), (), s32[]{:S(2)}) async-start(), calls=%async_computation.11 | async-start | bytes 1310720 | tf_op jit(solution)/shard_map/reduce_scatter | solution.py:535
  794.8 172.7 %reduce-scatter.13.cloned.1.call-start = ((), (), s32[]{:S(2)}) async-start(), calls=%async_computation.13 | async-start | bytes 2621440 | tf_op jit(solution)/shard_map/reduce_scatter | solution.py:535
  796.2 55.5 %collective-permute-start.93 = (bf16[1024,512]{0,1:T(8,128)(2,1)S(1)}, bf16[1024,512]{0,1:T(8,128)(2,1)}, u32[]{:S(2)}, u32[]{:S(2)}) collective-permute-start(bf16[1024,512]{0,1:T(8,128)(2,1)S(1)} %constant_dynamic-slice_fusion.10), channel_id=1, source_target_pairs={{0,16},{16,0},{1,17},{17,1},{2,18},{18,2},{3,19},{19,3},{4,20},{20... | collective-permute-start | bytes 3145736 | tf_op jit(solution)/shard_map/ppermute | solution.py:27
  797.5 54.1 %collective-permute-start.92 = (bf16[1600,256]{1,0:T(8,128)(2,1)}, bf16[1600,256]{1,0:T(8,128)(2,1)}, u32[]{:S(2)}, u32[]{:S(2)}) collective-permute-start(bf16[1600,256]{1,0:T(8,128)(2,1)} %get-tuple-element.708), channel_id=1, source_target_pairs={{0,12},{4,8},{8,4},{12,0},{1,13},{5,9},{9,5},{13,1},{2,14},{6,10},... | collective-permute-start | bytes 2457608 | tf_op jit(solution)/shard_map/ppermute | solution.py:27
  851.7 123.6 %reduce-scatter.17.cloned.1.call-start = ((), (), s32[]{:S(2)}) async-start(), calls=%async_computation.15 | async-start | bytes 2621440 | tf_op jit(solution)/shard_map/reduce_scatter | solution.py:535
  855.7 191.5 %reduce-scatter.11.cloned.1.call-start = ((), (), s32[]{:S(2)}) async-start(), calls=%async_computation.12 | async-start | bytes 1310720 | tf_op jit(solution)/shard_map/reduce_scatter | solution.py:535
  860.0 107.5 %collective-permute-start.99 = (bf16[4,1600,256]{2,1,0:T(8,128)(2,1)}, bf16[4,1600,256]{2,1,0:T(8,128)(2,1)}, u32[]{:S(2)}, u32[]{:S(2)}) collective-permute-start(bf16[4,1600,256]{2,1,0:T(8,128)(2,1)} %pad_maximum_fusion.38.near_ref), channel_id=1, source_target_pairs={{0,16},{16,0},{1,17},{17,1},{2,18},{18,2},{3,19},{19,3},{4,20},{20... | collective-permute-start | bytes 9830408 | tf_op jit(solution)/shard_map/ppermute | solution.py:27
  863.8 183.4 %reduce-scatter.15.cloned.1.call-start = ((), (), s32[]{:S(2)}) async-start(), calls=%async_computation.14 | async-start | bytes 1310720 | tf_op jit(solution)/shard_map/reduce_scatter | solution.py:535
  1001.1 50.6 %collective-permute-start.109 = (bf16[256,512]{0,1:T(8,128)(2,1)S(1)}, bf16[256,512]{0,1:T(8,128)(2,1)}, u32[]{:S(2)}, u32[]{:S(2)}) collective-permute-start(bf16[256,512]{0,1:T(8,128)(2,1)S(1)} %copy-done.100), channel_id=1, source_target_pairs={{0,16},{16,0},{1,17},{17,1},{2,18},{18,2},{3,19},{19,3},{4,20},{20... | collective-permute-start | bytes 786440 | tf_op jit(solution)/shard_map/ppermute | solution.py:27
  1002.6 44.7 %collective-permute-start.108 = (bf16[256,512]{0,1:T(8,128)(2,1)}, bf16[256,512]{0,1:T(8,128)(2,1)}, u32[]{:S(2)}, u32[]{:S(2)}) collective-permute-start(bf16[256,512]{0,1:T(8,128)(2,1)} %reduce-scatter.7.cloned.1.call-done), channel_id=1, source_target_pairs={{0,16},{16,0},{1,17},{17,1},{2,18},{18,2},{3,19},{19,3},{4,20},{20... | collective-permute-start | bytes 786440 | tf_op jit(solution)/shard_map/ppermute | solution.py:27
  1003.1 41.7 %collective-permute-start.100 = (bf16[256,1024]{0,1:T(8,128)(2,1)}, bf16[256,1024]{0,1:T(8,128)(2,1)}, u32[]{:S(2)}, u32[]{:S(2)}) collective-permute-start(bf16[256,1024]{0,1:T(8,128)(2,1)} %reduce-scatter.13.cloned.1.call-done), channel_id=1, source_target_pairs={{0,16},{16,0},{1,17},{17,1},{2,18},{18,2},{3,19},{19,3},{4,20},{20... | collective-permute-start | bytes 1572872 | tf_op jit(solution)/shard_map/ppermute | solution.py:27
  1005.7 39.1 %collective-permute-start.102 = (bf16[256,1024]{0,1:T(8,128)(2,1)S(1)}, bf16[256,1024]{0,1:T(8,128)(2,1)S(1)}, u32[]{:S(2)}, u32[]{:S(2)}) collective-permute-start(bf16[256,1024]{0,1:T(8,128)(2,1)S(1)} %copy-done.73), channel_id=1, source_target_pairs={{0,16},{16,0},{1,17},{17,1},{2,18},{18,2},{3,19},{19,3},{4,20},{20... | collective-permute-start | bytes 1572872 | tf_op jit(solution)/shard_map/ppermute | solution.py:27
  1011.0 44.0 %collective-permute-start.110 = (bf16[256,256]{1,0:T(8,128)(2,1)}, bf16[256,256]{1,0:T(8,128)(2,1)}, u32[]{:S(2)}, u32[]{:S(2)}) collective-permute-start(bf16[256,256]{1,0:T(8,128)(2,1)} %get-tuple-element.1097), channel_id=1, source_target_pairs={{0,4},{4,0},{8,12},{12,8},{1,5},{5,1},{9,13},{13,9},{2,6},{6,2},{1... | collective-permute-start | bytes 393224 | tf_op jit(solution)/shard_map/ppermute | solution.py:27
  (258 other events, 2897.2 us)
Sparse Core Ops, SparseCore 0:
  10.3 49.6 all-gather.4
  62.1 62.6 all-gather.6
  126.9 45.4 all-gather.8
  174.4 99.7 all-gather.10
  794.4 47.6 reduce-scatter.6
  844.9 27.9 reduce-scatter.8
  875.8 42.5 reduce-scatter.12
  920.7 51.4 reduce-scatter.16
  975.1 27.6 reduce-scatter.10
  1005.6 28.5 reduce-scatter.14
